TPU v7x, 512 devices: a whole 4x4x16 slice. The times are simulated.
512 devices in a mesh: gx: 64 (over z, x), gy: 8 (over y, core).
Axes of the slice: x: 4, y: 4, z: 16, core: 2. Of those that a mesh axis runs over, the one named last changes fastest.
Arguments:
- positions: float32 [3, 131072], P(None, ('gx', 'gy')), may hold values from 0 to 128
- features: float32 [128, 131072], P(None, ('gx', 'gy')), may hold values from -6 to 6
- neighbours: int32 [12, 131072], P(None, ('gx', 'gy')), may hold values from 0 to 25, as said below
- up_weight: float32 [128, 128], replicated, may hold values from -0.5 to 0.5
- radial_in: float32 [64, 8], replicated, may hold values from -2 to 2
- radial_out: float32 [384, 64], replicated, may hold values from -0.75 to 0.75
- coupling: float32 [2, 128], replicated, may hold values from 0.5 to 2
- mix_weight: float32 [128, 128], replicated, may hold values from -0.5 to 0.5
- readout: float32 [128], replicated, may hold values from -0.5 to 0.5
- charge_weight: float32 [128], replicated, may hold values from -0.5 to 0.5
Outputs:
- forces: float32 [3, 131072], P(None, ('gx', 'gy'))
- energy: float32 [], replicated
Inputs may be any that keep to these rules, and one draw needn't show every extreme that they name: `neighbours`: the 12 codes of an atom differ from one another.
All inputs are finite; a program needn't handle non-finite values.
Results may differ from a plain program's by a relative error of at most 0.0003.
Values sent between devices are 32-bit elements; how exact they have to be, the bound alone decides.
No kernel may reach another device: no remote copies, remote signals or barrier semaphores. Data moves between devices by JAX's collectives and lax.ppermute only.
A program may use at most 64 MiB of HBM per device.

v0:
```python
import math

import jax
import jax.numpy as jnp
from jax import lax
from jax.sharding import PartitionSpec as P

NZ = 128


highest = lax.Precision.HIGHEST
ewald_beta = 0.5


def passed_along(array, axis, by):
    devices = lax.axis_size(axis)
    return lax.ppermute(array, axis, [(i, (i + by) % devices) for i in range(devices)])


def lattice_offsets(codes):
    shifted = codes + (codes >= 13).astype(jnp.int32)
    return (shifted // 9 - 1, shifted // 3 % 3 - 1, shifted % 3 - 1)


def harmonics(unit_vec):
    along_x, along_y, along_z = (unit_vec[0], unit_vec[1], unit_vec[2])
    root_three = math.sqrt(3.0)
    root_five = math.sqrt(5.0)
    root_fifteen = math.sqrt(15.0)
    first_order = jnp.stack([root_three * along_x, root_three * along_y, root_three * along_z])
    second_order = jnp.stack(
        [
            root_fifteen * along_x * along_y,
            root_fifteen * along_y * along_z,
            0.5 * root_five * (3.0 * along_z * along_z - 1.0),
            root_fifteen * along_x * along_z,
            0.5 * root_fifteen * (along_x * along_x - along_y * along_y),
        ]
    )
    return (first_order, second_order)


def radial_basis(distance, cutoff, basis_count):
    harmonic_order = jnp.arange(1, basis_count + 1, dtype=jnp.int32).astype(jnp.float32)[:, None]
    scaled = distance[None, :] / cutoff
    envelope = 1.0 - 28.0 * scaled**6 + 48.0 * scaled**7 - 21.0 * scaled**8
    return (
        math.sqrt(2.0 / cutoff)
        * jnp.sin(harmonic_order * math.pi * scaled)
        / distance[None, :]
        * envelope
    )


def interaction(
    ext_pos, ext_up, features, codes, radial_in, radial_out, coupling, mix_weight, z_cells
):
    z_sites = ext_pos.shape[3]
    channels, atom_count = features.shape
    neighbour_count = codes.shape[0]
    atom_index = jnp.arange(atom_count, dtype=jnp.int32)
    plane_index = atom_index // (8 * z_sites)
    row_index = atom_index // z_sites % 8
    site_index = atom_index % z_sites
    step_x, step_y, step_z = lattice_offsets(codes)
    target_z = site_index[None, :] + step_z
    wrapped = (target_z >= z_sites).astype(jnp.int32) - (target_z < 0).astype(jnp.int32)
    target = (
        ((plane_index[None, :] + step_x + 1) * 10 + row_index[None, :] + step_y + 1) * z_sites
        + target_z
        - wrapped * z_sites
    )
    flat_target = target.reshape(-1)
    own_pos = ext_pos[:, 1:3, 1:9, :].reshape(3, atom_count)
    other_pos = jnp.take(ext_pos.reshape(3, -1), flat_target, axis=1).reshape(
        3, neighbour_count, atom_count
    )
    relative = other_pos - own_pos[:, None, :]
    relative = jnp.stack(
        [relative[0], relative[1], relative[2] + wrapped.astype(jnp.float32) * z_cells]
    )
    distance = jnp.sqrt(jnp.sum(relative * relative, axis=0))
    unit_vec = relative / distance[None]
    cutoff = 2.0 * z_cells / z_sites + 4.0
    basis = radial_basis(distance.reshape(-1), cutoff, radial_in.shape[1])
    hidden = jax.nn.silu(jnp.dot(radial_in, basis, precision=highest))
    radial = jnp.dot(radial_out, hidden, precision=highest).reshape(
        3, channels, neighbour_count, atom_count
    )
    neighbour_up = jnp.take(ext_up, flat_target, axis=1).reshape(
        channels, neighbour_count, atom_count
    )
    weighted = radial * neighbour_up[None]
    first_order, second_order = harmonics(unit_vec)
    scalar_part = jnp.sum(weighted[0], axis=1) / neighbour_count
    vector_part = (
        jnp.einsum("ckn,mkn->mcn", weighted[1], first_order, precision=highest) / neighbour_count
    )
    tensor_part = (
        jnp.einsum("ckn,mkn->mcn", weighted[2], second_order, precision=highest) / neighbour_count
    )
    product = (
        scalar_part
        + coupling[0][:, None] * jnp.sum(vector_part * vector_part, axis=0)
        + coupling[1][:, None] * jnp.sum(tensor_part * tensor_part, axis=0)
    )
    return features + jnp.dot(mix_weight, product, precision=highest)


def spline_weights(fraction):
    remainder = 1.0 - fraction
    fraction_square = fraction * fraction
    fraction_cube = fraction_square * fraction
    return [
        remainder * remainder * remainder / 6.0,
        (3.0 * fraction_cube - 6.0 * fraction_square + 4.0) / 6.0,
        (-3.0 * fraction_cube + 3.0 * fraction_square + 3.0 * fraction + 1.0) / 6.0,
        fraction_cube / 6.0,
    ]


def spline_table(coordinate, cell_count, first_cell, periodic):
    floored = jnp.floor(coordinate)
    base_index = floored.astype(jnp.int32)
    cell_index = jnp.arange(cell_count, dtype=jnp.int32)[:, None]
    table_sum = jnp.zeros((cell_count, coordinate.shape[0]), jnp.float32)
    for spline_step, weight in enumerate(spline_weights(coordinate - floored)):
        target = base_index + spline_step - 1 + first_cell
        if periodic:
            target = target % cell_count
        table_sum = table_sum + jnp.where(cell_index == target[None, :], weight[None, :], 0.0)
    return table_sum


def spread_local(own_pos, charges, z_cells):
    weights_x = spline_table(own_pos[0], 5, 1, False)
    weights_y = spline_table(own_pos[1], 19, 1, False)
    weights_z = spline_table(own_pos[2], z_cells, 0, True)
    planes = ((charges[None, :] * weights_x)[:, None, :] * weights_y[None, :, :]).reshape(95, -1)
    return jnp.einsum("pa,za->pz", planes, weights_z, precision=highest).reshape(5, 19, z_cells)


def ewald_kernel(index_x, index_y, index_z, length_x, length_y, length_z):
    squared = 0.0
    moduli = 1.0
    for wave_index, length in ((index_x, length_x), (index_y, length_y), (index_z, length_z)):
        folded = wave_index - length * (2 * wave_index >= length).astype(jnp.int32)
        wave_number = 2.0 * math.pi / length * folded.astype(jnp.float32)
        squared = squared + wave_number * wave_number
        moduli = (
            moduli
            * (6.0 / (4.0 + 2.0 * jnp.cos(2.0 * math.pi / length * wave_index.astype(jnp.float32))))
            ** 2
        )
    anchor = (index_x == 0) & (index_y == 0) & (index_z == 0)
    safe_square = jnp.where(anchor, 1.0, squared)
    return jnp.where(
        anchor,
        0.0,
        4.0 * math.pi * jnp.exp(-safe_square / (4.0 * ewald_beta**2)) / safe_square * moduli,
    )


def fourier_tables(length):
    wave_index = jnp.arange(length, dtype=jnp.int32)
    angle = (
        2.0
        * math.pi
        / length
        * (wave_index[:, None] * wave_index[None, :] % length).astype(jnp.float32)
    )
    return (jnp.cos(angle), jnp.sin(angle))


def apply_table(data, table, axis_pos):
    last_axis = jnp.moveaxis(data, axis_pos, -1)
    return jnp.moveaxis(
        jnp.einsum("...j,kj->...k", last_axis, table, precision=highest), -1, axis_pos
    )


def rotate(real, imag, cosine, sine, axis_pos, sign):
    return (
        apply_table(real, cosine, axis_pos) + sign * apply_table(imag, sine, axis_pos),
        apply_table(imag, cosine, axis_pos) - sign * apply_table(real, sine, axis_pos),
    )


def shards(
    positions,
    features,
    neighbours,
    up_weight,
    radial_in,
    radial_out,
    coupling,
    mix_weight,
    readout,
    charge_weight,
):
    channels, atom_count = features.shape
    z_sites = atom_count // 16
    z_cells = NZ
    grid_planes = 2 * lax.axis_size("gx")
    grid_rows = 16 * lax.axis_size("gy")
    z_part = z_cells // lax.axis_size("gy")
    y_part = grid_rows // lax.axis_size("gx")
    volume = grid_planes * grid_rows * z_cells
    own_up = jnp.dot(up_weight, features, precision=highest)
    packed = jnp.concatenate([positions, own_up], axis=0).reshape(channels + 3, 2, 8, z_sites)
    layer_ghosts = {}
    for toward, plane_pick, offset in ((1, 1, -2.0), (-1, 0, 2.0)):
        received = passed_along(packed[:, plane_pick], "gx", toward)
        layer_ghosts[toward] = received.at[0].add(offset)
    widened = jnp.stack([layer_ghosts[1], packed[:, 0], packed[:, 1], layer_ghosts[-1]], axis=1)
    row_ghosts = {}
    for toward, row_pick, offset in ((1, 7, -16.0), (-1, 0, 16.0)):
        received = passed_along(widened[:, :, row_pick], "gy", toward)
        row_ghosts[toward] = received.at[1].add(offset)
    ghost_table = jnp.concatenate(
        [row_ghosts[1][:, :, None], widened, row_ghosts[-1][:, :, None]], axis=2
    )
    ext_pos = ghost_table[:3]
    ext_up = ghost_table[3:].reshape(channels, -1)

    def layer_output(table_pos):
        return interaction(
            table_pos,
            ext_up,
            features,
            neighbours,
            radial_in,
            radial_out,
            coupling,
            mix_weight,
            float(z_cells),
        )

    updated, layer_pull = jax.vjp(layer_output, ext_pos)
    site_energy = jnp.dot(readout, updated, precision=highest)
    charges = jnp.dot(charge_weight, updated, precision=highest)

    def spread(own_pos, atom_charges):
        return spread_local(own_pos, atom_charges, z_cells)

    spread_grid, spread_pull = jax.vjp(spread, positions, charges)
    folded = spread_grid[1:3]
    for toward, first_plane, last_plane, target_plane in ((1, 3, 5, 0), (-1, 0, 1, 1)):
        received = passed_along(spread_grid[first_plane:last_plane], "gx", toward)
        folded = folded.at[target_plane : target_plane + last_plane - first_plane].add(received)
    charge_grid = folded[:, 1:17]
    for toward, first_row, last_row, target_row in ((1, 17, 19, 0), (-1, 0, 1, 15)):
        received = passed_along(folded[:, first_row:last_row], "gy", toward)
        charge_grid = charge_grid.at[:, target_row : target_row + last_row - first_row].add(
            received
        )
    cosine_x, sine_x = fourier_tables(grid_planes)
    cosine_y, sine_y = fourier_tables(grid_rows)
    cosine_z, sine_z = fourier_tables(z_cells)
    start_z = lax.axis_index("gy") * z_part
    real = apply_table(charge_grid, cosine_z, 2)
    imag = -apply_table(charge_grid, sine_z, 2)
    spectrum = lax.all_to_all(
        jnp.stack([real, imag]), "gy", split_axis=3, concat_axis=2, tiled=True
    )
    real, imag = rotate(spectrum[0], spectrum[1], cosine_y, sine_y, 1, 1.0)
    spectrum = jnp.stack([real, imag])
    spectrum = lax.all_to_all(spectrum, "gx", split_axis=2, concat_axis=1, tiled=True)
    real, imag = rotate(spectrum[0], spectrum[1], cosine_x, sine_x, 0, 1.0)
    index_x = jnp.arange(grid_planes, dtype=jnp.int32)[:, None, None]
    index_y = lax.axis_index("gx") * y_part + jnp.arange(y_part, dtype=jnp.int32)[None, :, None]
    index_z = start_z + jnp.arange(z_part, dtype=jnp.int32)[None, None, :]
    kernel = ewald_kernel(index_x, index_y, index_z, grid_planes, grid_rows, z_cells)
    long_part = jnp.sum(kernel * (real * real + imag * imag)) / (2.0 * volume)
    totals = lax.psum((jnp.sum(site_energy), long_part), ("gx", "gy"))
    energy = (totals[0] + totals[1]) / (atom_count * lax.axis_size("gx") * lax.axis_size("gy"))
    real, imag = rotate(kernel * real, kernel * imag, cosine_x, sine_x, 0, -1.0)
    spectrum = lax.all_to_all(
        jnp.stack([real, imag]), "gx", split_axis=1, concat_axis=2, tiled=True
    )
    real, imag = rotate(spectrum[0], spectrum[1], cosine_y, sine_y, 1, -1.0)
    spectrum = lax.all_to_all(
        jnp.stack([real, imag]), "gy", split_axis=2, concat_axis=3, tiled=True
    )
    potential = (
        apply_table(spectrum[0], cosine_z, 2) - apply_table(spectrum[1], sine_z, 2)
    ) / volume
    plane_parts = {}
    for toward, first_plane, last_plane in ((1, 1, 2), (-1, 0, 2)):
        plane_parts[toward] = passed_along(potential[first_plane:last_plane], "gx", toward)
    planes_ext = jnp.concatenate([plane_parts[1], potential, plane_parts[-1]], axis=0)
    row_parts = {}
    for toward, first_row, last_row in ((1, 15, 16), (-1, 0, 2)):
        row_parts[toward] = passed_along(planes_ext[:, first_row:last_row], "gy", toward)
    potential_ext = jnp.concatenate([row_parts[1], planes_ext, row_parts[-1]], axis=1)
    spread_pos_grad, charge_grad = spread_pull(potential_ext)
    cotangent = readout[:, None] + charge_weight[:, None] * charge_grad[None, :]
    (table_grad,) = layer_pull(cotangent)
    row_grad = table_grad[:, :, 1:9]
    for toward, source_row, target_row in ((-1, 0, 7), (1, 9, 0)):
        received = passed_along(table_grad[:, :, source_row], "gy", toward)
        row_grad = row_grad.at[:, :, target_row].add(received)
    own_grad = row_grad[:, 1:3]
    for toward, source_plane, target_plane in ((-1, 0, 1), (1, 3, 0)):
        received = passed_along(row_grad[:, source_plane], "gx", toward)
        own_grad = own_grad.at[:, target_plane].add(received)
    forces = -(own_grad.reshape(3, atom_count) + spread_pos_grad)
    return (forces, energy)


def solution(mesh):
    placed = (
        P(None, ("gx", "gy")),
        P(None, ("gx", "gy")),
        P(None, ("gx", "gy")),
        P(),
        P(),
        P(),
        P(),
        P(),
        P(),
        P(),
    )
    return jax.shard_map(
        shards, mesh=mesh, in_specs=placed, out_specs=(P(None, ("gx", "gy")), P()), check_vma=False
    )
```

profile of v0, /device:TPU:1, one launch (start us, length us, event | category | flops | bytes accessed | tf_op | source)
XLA Modules:
  0.0 447.5 jit_solution(6050851230744225928)
XLA Ops:
  0.7 1.3 fusion.352
  2.8 14.1 %collective-permute-start.1 = (f32[131,8,16]{0,2,1:T(8,128)S(1)}, f32[131,8,16]{0,2,1:T(8,128)S(1)}, u32[]{:S(2)}, u32[]{:S(2)}) collective-permute-start(f32[131,8,16]{0,2,1:T(8,128)S(1)} %get-tuple-element.197), channel_id=1, source_target_pairs={{0,504},{8,0},{16,8},{24,16},{32,24},{40,32},{48,40},{56,48},{64,5... | collective-permute-start | bytes 201224 | tf_op jit(solution)/shard_map/ppermute | solution.py:17
  16.9 1.9 collective-permute-start
  18.9 1.4 fusion.233
  20.3 1.4 broadcast_add_fusion.6
  25.2 1.4 slice_bitcast_fusion.17
  34.6 8.1 %gather_fusion = f32[3072,3]{1,0:T(8,128)S(1)} fusion(f32[3,640]{0,1:T(8,128)S(1)} %bitcast.364, s32[3072]{0:T(1024)S(1)} %broadcast_clamp_fusion), kind=kCustom, calls=%fused_computation | custom fusion | bytes 86016 | tf_op jit(solution)/shard_map/jvp(jit(_take))/gather | solution.py:75
  46.9 5.6 %convolution_bitcast_fusion = f32[384,3072]{0,1:T(8,128)} fusion(f32[384,64]{0,1:T(8,128)S(1)} %copy-done, f32[64,3072]{1,0:T(8,128)S(1)} %convolution_bitcast_fusion.2), kind=kOutput, calls=%fused_computation.5 | convolution fusion | flops 906756096 | bytes 5603328 | tf_op jit(solution)/shard_map/jvp()/dot_general | solution.py:87
  52.5 8.0 %reshape.1449 = f32[3,128,12,256]{1,0,3,2:T(4,128)} reshape(f32[384,3072]{0,1:T(8,128)} %convolution_bitcast_fusion) | data formatting | bytes 9437184 | tf_op jit(solution)/shard_map/jvp()/reshape | solution.py:87
  60.5 10.9 %gather_fusion.1 = f32[3072,128]{1,0:T(8,128)} fusion(f32[128,640]{0,1:T(8,128)S(1)} %bitcast.356, s32[3072]{0:T(1024)S(1)} %broadcast_clamp_fusion), kind=kCustom, calls=%fused_computation.1 | custom fusion | bytes 3158016 | tf_op jit(solution)/shard_map/jvp(jit(_take))/gather | solution.py:90
  72.4 4.7 %copy_select_fusion = f32[128,12,256]{0,1,2:T(8,128)S(1)} fusion(f32[128,12,256]{0,2,1:T(8,128)} %bitcast.359, pred[12,256]{0,1:T(8,128)(4,1)S(1)} %copy.412), kind=kLoop, calls=%fused_computation.12 | loop fusion | flops 393216 | bytes 3148800 | tf_op jit(solution)/shard_map/jvp(jit(_take))/select_n | solution.py:90
  77.1 5.6 %copy_multiply_fusion = f32[3,128,12,256]{1,2,3,0:T(8,128)S(1)} fusion(f32[3,128,12,256]{1,0,3,2:T(4,128)} %reshape.1449, f32[128,12,256]{0,1,2:T(8,128)S(1)} %copy_select_fusion), kind=kLoop, calls=%fused_computation.3 | loop fusion | flops 1179648 | bytes 11010048 | tf_op jit(solution)/shard_map/jvp()/mul | solution.py:93
  83.1 2.3 copy-done.1
  85.4 3.5 multiply_reduce_fusion.1
  89.6 4.7 %multiply_reduce_fusion = (f32[256,128]{1,0:T(8,128)S(1)}, f32[256,5,128]{2,1,0:T(8,128)}) fusion(f32[5,12,256]{1,0,2:T(8,128)S(1)} %copy.415, f32[3,128,12,256]{1,2,3,0:T(8,128)} %copy-done.1), kind=kOutput, calls=%fused_computation.47 | convolution fusion | flops 24051712 | bytes 2945024 | tf_op jit(solution)/shard_map/jvp(ckn,mkn->mcn)/dot_general | solution.py:100
  97.9 1.9 collective-permute-start.4
  99.9 6.7 %collective-permute-start.5 = (f32[1,19,128]{2,1,0:T(8,128)S(1)}, f32[1,19,128]{2,1,0:T(8,128)S(1)}, u32[]{:S(2)}, u32[]{:S(2)}) collective-permute-start(f32[1,19,128]{2,1,0:T(8,128)S(1)} %slice_bitcast_fusion.15), channel_id=1, source_target_pairs={{0,504},{8,0},{16,8},{24,16},{32,24},{40,32},{48,40},{56,48},{64,5... | collective-permute-start | bytes 29192 | tf_op jit(solution)/shard_map/ppermute | solution.py:17
  107.4 3.1 collective-permute-start.6
  110.5 1.3 broadcast_and_fusion
  111.8 2.2 collective-permute-start.7
  116.6 1.9 reshape.1452
  118.5 7.8 %all-to-all-start = ((f32[8,1,1024]{2,1,0:T(1,128)}), f32[8,1,1024]{2,1,0:T(1,128)S(1)}, u32[]{:S(2)}, u32[]{:S(2)}) async-start(f32[8,1,1024]{2,1,0:T(1,128)} %reshape.1452), calls=%async_computation | async-start | bytes 65536 | tf_op jit(solution)/shard_map/all_to_all | solution.py:263
  126.3 1.3 broadcast_and_fusion.1
  127.7 3.4 all-to-all-done
  135.2 1.6 squeeze.74
  136.8 1.8 fusion.86
  143.7 1.9 reshape.1454
  145.6 10.6 %all-to-all-start.1 = ((f32[64,1,128]{2,1,0:T(1,128)}), f32[64,1,128]{2,1,0:T(1,128)S(1)}, u32[]{:S(2)}, u32[]{:S(2)}) async-start(f32[64,1,128]{2,1,0:T(1,128)} %reshape.1454), calls=%async_computation.1 | async-start | bytes 65536 | tf_op jit(solution)/shard_map/all_to_all | solution.py:268
  157.5 12.3 %all-to-all-done.1 = f32[64,1,128]{2,1,0:T(1,128)S(1)} async-done(((f32[64,1,128]{2,1,0:T(1,128)}), f32[64,1,128]{2,1,0:T(1,128)S(1)}, u32[]{:S(2)}, u32[]{:S(2)}) %all-to-all-start.1) | async-done | bytes 32800 | tf_op jit(solution)/shard_map/all_to_all | solution.py:268
  174.1 1.8 fusion.84
  178.7 1.2 convolution_add_fusion
  181.1 1.8 fusion.151
  186.7 1.3 reshape.1456
  188.0 17.4 %all_to_all.60 = f32[64,1,128]{2,1,0:T(1,128)S(1)} all-to-all(f32[64,1,128]{2,1,0:T(1,128)S(1)} %reshape.1456), channel_id=1, replica_groups=mesh['gx'=64,'gy'=8] {'gx'}, dimensions={0} | all-to-all | bytes 65536 | tf_op jit(solution)/shard_map/all_to_all | solution.py:278
  209.7 1.8 fusion.74
  214.3 1.2 fusion.7
  217.6 1.3 reshape.1458
  218.9 10.4 %all_to_all.61 = f32[8,1,1024]{2,1,0:T(1,128)S(1)} all-to-all(f32[8,1,1024]{2,1,0:T(1,128)S(1)} %reshape.1458), channel_id=1, replica_groups=mesh['gx'=64,'gy'=8] {'gy'}, dimensions={0} | all-to-all | bytes 65536 | tf_op jit(solution)/shard_map/all_to_all | solution.py:282
  232.9 1.6 squeeze.79
  234.5 1.8 fusion.72
  238.2 2.7 collective-permute-start.9
  241.0 2.5 collective-permute-start.8
  243.5 5.2 %collective-permute-done.8 = f32[1,16,128]{2,1,0:T(8,128)S(1)} collective-permute-done((f32[1,16,128]{2,1,0:T(8,128)S(1)}, f32[1,16,128]{2,1,0:T(8,128)S(1)}, u32[]{:S(2)}, u32[]{:S(2)}) %collective-permute-start.8) | collective-permute-done | bytes 8224 | tf_op jit(solution)/shard_map/ppermute | solution.py:17
  248.7 2.2 collective-permute-start.11
  253.8 99.6 %psum.16 = f32[]{:T(128)} all-reduce(f32[]{:T(128)S(6)} %add.796), channel_id=1, replica_groups=mesh['gx'=64,'gy'=8] {'gx','gy'}, use_global_device_ids=true, to_apply=%region_26.27 | all-reduce | flops 1 | bytes 8 | tf_op jit(solution)/shard_map/psum | solution.py:275
  354.1 1.7 multiply_reduce_fusion.2
  355.9 1.3 select_reduce_fusion.8
  357.2 2.0 multiply_bitcast_fusion
  359.2 6.0 %fusion.2 = f32[256,3,12]{2,1,0:T(4,128)} fusion(f32[3,128,12,256]{1,2,3,0:T(8,128)} %copy-done.1, f32[256,3,128]{2,1,0:T(4,128)} %get-tuple-element.264, f32[256,128]{1,0:T(8,128)S(1)} %get-tuple-element.201), kind=kOutput, calls=%fused_computation.15 | convolution fusion | flops 14450688 | bytes 2789376 | tf_op jit(solution)/shard_map/transpose(jvp(ckn,mkn->mcn))/dot_general | solution.py:97
  365.2 1.8 copy.435
  367.0 6.3 %fusion = f32[256,5,12]{2,1,0:T(8,128)} fusion(f32[3,128,12,256]{1,2,3,0:T(8,128)} %copy-done.1, f32[256,5,128]{2,1,0:T(8,128)} %get-tuple-element.262, f32[256,128]{1,0:T(8,128)S(1)} %get-tuple-element.202), kind=kOutput, calls=%fused_computation.13 | convolution fusion | flops 24084480 | bytes 3338240 | tf_op jit(solution)/shard_map/transpose(jvp(ckn,mkn->mcn))/dot_general | solution.py:100
  373.4 2.2 copy.434
  375.6 2.0 fusion.206
  377.6 1.7 fusion.205
  379.3 4.7 %convolution_bitcast_fusion.4 = f32[1,128,12,256]{1,2,3,0:T(8,128)S(1)} fusion(f32[3,12,256]{1,0,2:T(4,128)} %copy-done.3, f32[256,3,128]{2,1,0:T(4,128)} %get-tuple-element.264, f32[256,128]{1,0:T(8,128)S(1)} %get-tuple-element.201), kind=kOutput, calls=%fused_computation.17 | convolution fusion | flops 14450688 | bytes 2134016 | tf_op jit(solution)/shard_map/transpose(jvp(ckn,mkn->mcn))/dot_general | solution.py:97
  384.0 3.7 convolution_bitcast_fusion.5
  387.9 2.9 add_multiply_fusion
  390.8 6.7 %copy.438 = f32[3,128,12,256]{3,2,1,0:T(8,128)} copy(f32[3,128,12,256]{1,2,3,0:T(8,128)} %add_multiply_fusion) | data formatting | bytes 9437184 | tf_op jit(solution)/shard_map/transpose(jvp())/mul | solution.py:93
  397.5 7.2 %copy.469 = f32[48,8,12,256]{3,1,2,0:T(8,128)S(1)} copy(f32[48,8,12,256]{3,2,1,0:T(8,128)} %bitcast.357) | data formatting | bytes 9437184
  404.9 3.1 convolution_bitcast_fusion.1
  410.5 17.1 %scatter_custom_fusion = f32[3,640]{0,1:T(8,128)S(1)} fusion(s32[3072]{0:T(1024)} %bitcast.396, f32[3072,3]{1,0:T(8,128)S(1)} %copy.444, f32[]{:T(128)} %constant.631.clone.1), kind=kCustom, calls=%fused_computation.70 | custom fusion | flops 9216 | bytes 8192 | tf_op jit(solution)/shard_map/transpose(jvp(jit(_take)))/scatter-add | solution.py:75
  431.4 5.7 %collective-permute-start.14 = (f32[3,8,16]{0,2,1:T(8,128)S(1)}, f32[3,8,16]{0,2,1:T(8,128)S(1)}, u32[]{:S(2)}, u32[]{:S(2)}) collective-permute-start(f32[3,8,16]{0,2,1:T(8,128)S(1)} %get-tuple-element.187), channel_id=1, source_target_pairs={{0,504},{8,0},{16,8},{24,16},{32,24},{40,32},{48,40},{56,48},{64,5... | collective-permute-start | bytes 4616 | tf_op jit(solution)/shard_map/ppermute | solution.py:17
  437.1 1.9 collective-permute-start.15
  439.1 6.4 %collective-permute-done.15 = f32[3,8,16]{0,2,1:T(8,128)S(1)} collective-permute-done((f32[3,8,16]{0,2,1:T(8,128)S(1)}, f32[3,8,16]{0,2,1:T(8,128)S(1)}, u32[]{:S(2)}, u32[]{:S(2)}) %collective-permute-start.15) | collective-permute-done | bytes 1568 | tf_op jit(solution)/shard_map/ppermute | solution.py:17
  (364 shorter events, 70.5 us)
Async XLA Ops:
  0.6 46.3 %copy-start = (f32[384,64]{0,1:T(8,128)S(1)}, f32[384,64]{0,1:T(8,128)}, u32[]{:S(2)}) copy-start(f32[384,64]{0,1:T(8,128)} %param.41) | copy-start | bytes 294916
  0.6 29.6 %copy-start.7 = (f32[128,256]{1,0:T(8,128)S(1)}, f32[128,256]{1,0:T(8,128)}, u32[]{:S(2)}) copy-start(f32[128,256]{1,0:T(8,128)} %param.37) | copy-start | bytes 393220
  2.8 25.6 %collective-permute-start.1 = (f32[131,8,16]{0,2,1:T(8,128)S(1)}, f32[131,8,16]{0,2,1:T(8,128)S(1)}, u32[]{:S(2)}, u32[]{:S(2)}) collective-permute-start(f32[131,8,16]{0,2,1:T(8,128)S(1)} %get-tuple-element.197), channel_id=1, source_target_pairs={{0,504},{8,0},{16,8},{24,16},{32,24},{40,32},{48,40},{56,48},{64,5... | collective-permute-start | bytes 201224 | tf_op jit(solution)/shard_map/ppermute | solution.py:17
  16.9 11.6 %collective-permute-start = (f32[131,8,16]{0,2,1:T(8,128)S(1)}, f32[131,8,16]{0,2,1:T(8,128)S(1)}, u32[]{:S(2)}, u32[]{:S(2)}) collective-permute-start(f32[131,8,16]{0,2,1:T(8,128)S(1)} %get-tuple-element.196), channel_id=1, source_target_pairs={{0,8},{8,16},{16,24},{24,32},{32,40},{40,48},{48,56},{56,64},{64,7... | collective-permute-start | bytes 201224 | tf_op jit(solution)/shard_map/ppermute | solution.py:17
  20.3 8.3 %copy-start.58 = (f32[1,256]{1,0:T(1,128)}, f32[1,256]{1,0:T(1,128)S(1)}, u32[]{:S(2)}) copy-start(f32[1,256]{1,0:T(1,128)S(1)} %get-tuple-element.175) | copy-start | bytes 3076
  20.3 8.3 %copy-start.60 = (f32[1,256]{1,0:T(1,128)}, f32[1,256]{1,0:T(1,128)S(1)}, u32[]{:S(2)}) copy-start(f32[1,256]{1,0:T(1,128)S(1)} %get-tuple-element.240) | copy-start | bytes 3076
  20.3 8.3 %copy-start.62 = (f32[1,256]{1,0:T(1,128)}, f32[1,256]{1,0:T(1,128)S(1)}, u32[]{:S(2)}) copy-start(f32[1,256]{1,0:T(1,128)S(1)} %get-tuple-element.237) | copy-start | bytes 3076
  20.3 13.8 %copy-start.45 = (s32[1,256]{1,0:T(1,128)}, s32[1,256]{1,0:T(1,128)S(1)}, u32[]{:S(2)}) copy-start(s32[1,256]{1,0:T(1,128)S(1)} %get-tuple-element.238) | copy-start | bytes 3076
  21.7 12.4 %copy-start.47 = (s32[1,256]{1,0:T(1,128)}, s32[1,256]{1,0:T(1,128)S(1)}, u32[]{:S(2)}) copy-start(s32[1,256]{1,0:T(1,128)S(1)} %get-tuple-element.227) | copy-start | bytes 3076
  25.2 9.0 %copy-start.30 = (s32[3072,1]{0,1:T(1,128)}, s32[3072,1]{0,1:T(1,128)S(1)}, u32[]{:S(2)}) copy-start(s32[3072,1]{0,1:T(1,128)S(1)} %compare_select_fusion) | copy-start | bytes 36868
  28.4 16.5 %copy-start.80 = (f32[8]{0:T(128)}, f32[8]{0:T(128)S(1)}, u32[]{:S(2)}) copy-start(f32[8]{0:T(128)S(1)} %convert_multiply_fusion) | copy-start | bytes 100
  28.8 4.1 collective-permute-start.3
  31.1 2.9 collective-permute-start.2
  33.3 10.1 %copy-start.29 = (f32[3,256]{1,0:T(4,128)S(1)}, f32[3,256]{1,0:T(4,128)}, u32[]{:S(2)}) copy-start(f32[3,256]{1,0:T(4,128)} %param.36) | copy-start | bytes 9220
  34.2 9.3 %copy-start.25 = (s32[12,256]{1,0:T(8,128)S(1)}, s32[12,256]{1,0:T(8,128)}, u32[]{:S(2)}) copy-start(s32[12,256]{1,0:T(8,128)} %param.38) | copy-start | bytes 36868
  34.6 10.3 %copy-start.66 = (f32[64,8]{0,1:T(8,128)S(1)}, f32[64,8]{0,1:T(8,128)}, u32[]{:S(2)}) copy-start(f32[64,8]{0,1:T(8,128)} %param.40) | copy-start | bytes 6148
  43.6 8.8 %copy-start.17 = (f32[12,256]{1,0:T(8,128)}, f32[12,256]{1,0:T(8,128)S(1)}, u32[]{:S(2)}) copy-start(f32[12,256]{1,0:T(8,128)S(1)} %get-tuple-element.215) | copy-start | bytes 36868
  44.3 27.1 %copy-start.11 = (f32[12,256]{1,0:T(8,128)}, f32[12,256]{1,0:T(8,128)S(1)}, u32[]{:S(2)}) copy-start(f32[12,256]{1,0:T(8,128)S(1)} %get-tuple-element.218) | copy-start | bytes 36868
  44.3 8.2 %copy-start.19 = (f32[3072]{0:T(1024)}, f32[3072]{0:T(1024)S(1)}, u32[]{:S(2)}) copy-start(f32[3072]{0:T(1024)S(1)} %sqrt.34) | copy-start | bytes 36868
  72.3 10.7 %copy-start.3 = (f32[3,12,256]{1,0,2:T(4,128)}, f32[3,12,256]{1,0,2:T(4,128)S(1)}, u32[]{:S(2)}) copy-start(f32[3,12,256]{1,0,2:T(4,128)S(1)} %copy.416) | copy-start | bytes 110596
  97.9 8.6 %collective-permute-start.4 = (f32[2,19,128]{2,1,0:T(8,128)S(1)}, f32[2,19,128]{2,1,0:T(8,128)S(1)}, u32[]{:S(2)}, u32[]{:S(2)}) collective-permute-start(f32[2,19,128]{2,1,0:T(8,128)S(1)} %slice.470), channel_id=1, source_target_pairs={{0,8},{8,16},{16,24},{24,32},{32,40},{40,48},{48,56},{56,64},{64,7... | collective-permute-start | bytes 58376 | tf_op jit(solution)/shard_map/ppermute | solution.py:17
  99.9 7.5 %collective-permute-start.5 = (f32[1,19,128]{2,1,0:T(8,128)S(1)}, f32[1,19,128]{2,1,0:T(8,128)S(1)}, u32[]{:S(2)}, u32[]{:S(2)}) collective-permute-start(f32[1,19,128]{2,1,0:T(8,128)S(1)} %slice_bitcast_fusion.15), channel_id=1, source_target_pairs={{0,504},{8,0},{16,8},{24,16},{32,24},{40,32},{48,40},{56,48},{64,5... | collective-permute-start | bytes 29192 | tf_op jit(solution)/shard_map/ppermute | solution.py:17
  107.4 6.6 %collective-permute-start.6 = (f32[2,2,128]{2,1,0:T(2,128)S(1)}, f32[2,2,128]{2,1,0:T(2,128)S(1)}, u32[]{:S(2)}, u32[]{:S(2)}) collective-permute-start(f32[2,2,128]{2,1,0:T(2,128)S(1)} %slice.526), channel_id=1, source_target_pairs={{0,1},{1,2},{2,3},{3,4},{4,5},{5,6},{6,7},{7,0},{8,9},{9,10},{10,1... | collective-permute-start | bytes 6152 | tf_op jit(solution)/shard_map/ppermute | solution.py:17
  111.8 3.0 collective-permute-start.7
  118.5 12.5 %all-to-all-start = ((f32[8,1,1024]{2,1,0:T(1,128)}), f32[8,1,1024]{2,1,0:T(1,128)S(1)}, u32[]{:S(2)}, u32[]{:S(2)}) async-start(f32[8,1,1024]{2,1,0:T(1,128)} %reshape.1452), calls=%async_computation | async-start | bytes 65536 | tf_op jit(solution)/shard_map/all_to_all | solution.py:263
  145.6 24.1 %all-to-all-start.1 = ((f32[64,1,128]{2,1,0:T(1,128)}), f32[64,1,128]{2,1,0:T(1,128)S(1)}, u32[]{:S(2)}, u32[]{:S(2)}) async-start(f32[64,1,128]{2,1,0:T(1,128)} %reshape.1454), calls=%async_computation.1 | async-start | bytes 65536 | tf_op jit(solution)/shard_map/all_to_all | solution.py:268
  177.5 7.8 %copy-start.87 = (f32[16]{0:T(128)S(1)}, f32[16]{0:T(128)}, u32[]{:S(2)}) copy-start(f32[16]{0:T(128)} %get-tuple-element.272) | copy-start | bytes 196
  177.5 7.8 %copy-start.88 = (f32[16]{0:T(128)S(1)}, f32[16]{0:T(128)}, u32[]{:S(2)}) copy-start(f32[16]{0:T(128)} %get-tuple-element.273) | copy-start | bytes 196
  177.6 7.8 %copy-start.89 = (pred[16]{0:T(512)(128)(4,1)S(1)}, pred[16]{0:T(512)(128)(4,1)}, u32[]{:S(2)}) copy-start(pred[16]{0:T(512)(128)(4,1)} %fusion.254) | copy-start | bytes 52
  238.2 119.0 %copy-start.21 = (f32[2,16,128]{2,1,0:T(8,128)}, f32[2,16,128]{2,1,0:T(8,128)S(1)}, u32[]{:S(2)}) copy-start(f32[2,16,128]{2,1,0:T(8,128)S(1)} %fusion.5) | copy-start | bytes 49156
  238.2 10.5 %collective-permute-start.9 = (f32[2,16,128]{2,1,0:T(8,128)S(1)}, f32[2,16,128]{2,1,0:T(8,128)S(1)}, u32[]{:S(2)}, u32[]{:S(2)}) collective-permute-start(f32[2,16,128]{2,1,0:T(8,128)S(1)} %fusion.5), channel_id=1, source_target_pairs={{0,504},{8,0},{16,8},{24,16},{32,24},{40,32},{48,40},{56,48},{64,5... | collective-permute-start | bytes 49160 | tf_op jit(solution)/shard_map/ppermute | solution.py:17
  241.0 7.7 %collective-permute-start.8 = (f32[1,16,128]{2,1,0:T(8,128)S(1)}, f32[1,16,128]{2,1,0:T(8,128)S(1)}, u32[]{:S(2)}, u32[]{:S(2)}) collective-permute-start(f32[1,16,128]{2,1,0:T(8,128)S(1)} %slice.537), channel_id=1, source_target_pairs={{0,8},{8,16},{16,24},{24,32},{32,40},{40,48},{48,56},{56,64},{64,7... | collective-permute-start | bytes 24584 | tf_op jit(solution)/shard_map/ppermute | solution.py:17
  248.7 108.5 %copy-start.37 = (f32[1,16,128]{2,1,0:T(8,128)}, f32[1,16,128]{2,1,0:T(8,128)S(1)}, u32[]{:S(2)}) copy-start(f32[1,16,128]{2,1,0:T(8,128)S(1)} %collective-permute-done.8) | copy-start | bytes 24580
  248.7 108.5 %copy-start.26 = (f32[2,16,128]{2,1,0:T(8,128)}, f32[2,16,128]{2,1,0:T(8,128)S(1)}, u32[]{:S(2)}) copy-start(f32[2,16,128]{2,1,0:T(8,128)S(1)} %collective-permute-done.9) | copy-start | bytes 49156
  248.7 105.4 %collective-permute-start.11 = (f32[5,2,128]{2,1,0:T(2,128)S(1)}, f32[5,2,128]{2,1,0:T(2,128)S(1)}, u32[]{:S(2)}, u32[]{:S(2)}) collective-permute-start(f32[5,2,128]{2,1,0:T(2,128)S(1)} %pad_maximum_fusion.13), channel_id=1, source_target_pairs={{0,7},{1,0},{2,1},{3,2},{4,3},{5,4},{6,5},{7,6},{8,15},{9,8},{10,9... | collective-permute-start | bytes 15368 | tf_op jit(solution)/shard_map/ppermute | solution.py:17
  250.9 103.2 %collective-permute-start.10 = (f32[5,1,128]{2,1,0:T(1,128)S(1)}, f32[5,1,128]{2,1,0:T(1,128)S(1)}, u32[]{:S(2)}, u32[]{:S(2)}) collective-permute-start(f32[5,1,128]{2,1,0:T(1,128)S(1)} %pad_maximum_fusion.15), channel_id=1, source_target_pairs={{0,1},{1,2},{2,3},{3,4},{4,5},{5,6},{6,7},{7,0},{8,9},{9,10},{10,1... | collective-permute-start | bytes 7688 | tf_op jit(solution)/shard_map/ppermute | solution.py:17
  375.6 8.4 %copy-start.2 = (f32[256,5,128]{2,1,0:T(8,128)S(1)}, f32[256,5,128]{2,1,0:T(8,128)}, u32[]{:S(2)}) copy-start(f32[256,5,128]{2,1,0:T(8,128)} %get-tuple-element.262) | copy-start | bytes 1966084
  409.2 20.4 %copy-start.68 = (f32[256]{0:T(256)S(1)}, f32[256]{0:T(256)}, u32[]{:S(2)}) copy-start(f32[256]{0:T(256)} %get-tuple-element.167) | copy-start | bytes 3076
  409.3 20.4 %copy-start.39 = (f32[19,256]{1,0:T(8,128)S(1)}, f32[19,256]{1,0:T(8,128)}, u32[]{:S(2)}) copy-start(f32[19,256]{1,0:T(8,128)} %get-tuple-element.161) | copy-start | bytes 58372
  409.3 20.4 %copy-start.46 = (s32[1,256]{1,0:T(1,128)S(1)}, s32[1,256]{1,0:T(1,128)}, u32[]{:S(2)}) copy-start(s32[1,256]{1,0:T(1,128)} %copy-done.45) | copy-start | bytes 3076
  409.3 20.4 %copy-start.48 = (s32[1,256]{1,0:T(1,128)S(1)}, s32[1,256]{1,0:T(1,128)}, u32[]{:S(2)}) copy-start(s32[1,256]{1,0:T(1,128)} %copy-done.47) | copy-start | bytes 3076
  409.3 20.4 %copy-start.50 = (s32[1,256]{1,0:T(1,128)S(1)}, s32[1,256]{1,0:T(1,128)}, u32[]{:S(2)}) copy-start(s32[1,256]{1,0:T(1,128)} %copy-done.49) | copy-start | bytes 3076
  409.3 20.4 %copy-start.52 = (s32[1,256]{1,0:T(1,128)S(1)}, s32[1,256]{1,0:T(1,128)}, u32[]{:S(2)}) copy-start(s32[1,256]{1,0:T(1,128)} %copy-done.51) | copy-start | bytes 3076
  409.3 20.4 %copy-start.69 = (f32[256]{0:T(256)S(1)}, f32[256]{0:T(256)}, u32[]{:S(2)}) copy-start(f32[256]{0:T(256)} %get-tuple-element.168) | copy-start | bytes 3076
  409.3 20.4 %copy-start.70 = (f32[256]{0:T(256)S(1)}, f32[256]{0:T(256)}, u32[]{:S(2)}) copy-start(f32[256]{0:T(256)} %get-tuple-element.170) | copy-start | bytes 3076
  409.3 20.4 %copy-start.71 = (f32[256]{0:T(256)S(1)}, f32[256]{0:T(256)}, u32[]{:S(2)}) copy-start(f32[256]{0:T(256)} %get-tuple-element.171) | copy-start | bytes 3076
  409.3 20.4 %copy-start.22 = (f32[2,16,128]{2,1,0:T(8,128)S(1)}, f32[2,16,128]{2,1,0:T(8,128)}, u32[]{:S(2)}) copy-start(f32[2,16,128]{2,1,0:T(8,128)} %copy-done.21) | copy-start | bytes 49156
  409.3 20.4 %copy-start.24 = (f32[19,256]{1,0:T(8,128)S(1)}, f32[19,256]{1,0:T(8,128)}, u32[]{:S(2)}) copy-start(f32[19,256]{1,0:T(8,128)} %select_add_fusion.4) | copy-start | bytes 58372
  409.4 20.4 %copy-start.27 = (f32[2,16,128]{2,1,0:T(8,128)S(1)}, f32[2,16,128]{2,1,0:T(8,128)}, u32[]{:S(2)}) copy-start(f32[2,16,128]{2,1,0:T(8,128)} %copy-done.26) | copy-start | bytes 49156
  409.4 20.4 %copy-start.36 = (f32[5,256]{1,0:T(8,128)S(1)}, f32[5,256]{1,0:T(8,128)}, u32[]{:S(2)}) copy-start(f32[5,256]{1,0:T(8,128)} %copy-done.35) | copy-start | bytes 15364
  409.4 20.4 %copy-start.38 = (f32[1,16,128]{2,1,0:T(8,128)S(1)}, f32[1,16,128]{2,1,0:T(8,128)}, u32[]{:S(2)}) copy-start(f32[1,16,128]{2,1,0:T(8,128)} %copy-done.37) | copy-start | bytes 24580
  409.4 20.4 %copy-start.75 = (s32[1,256]{1,0:T(1,128)S(1)}, s32[1,256]{1,0:T(1,128)}, u32[]{:S(2)}) copy-start(s32[1,256]{1,0:T(1,128)} %get-tuple-element.232) | copy-start | bytes 3076
  409.4 20.4 %copy-start.76 = (s32[1,256]{1,0:T(1,128)S(1)}, s32[1,256]{1,0:T(1,128)}, u32[]{:S(2)}) copy-start(s32[1,256]{1,0:T(1,128)} %get-tuple-element.233) | copy-start | bytes 3076
  409.4 20.4 %copy-start.77 = (s32[1,256]{1,0:T(1,128)S(1)}, s32[1,256]{1,0:T(1,128)}, u32[]{:S(2)}) copy-start(s32[1,256]{1,0:T(1,128)} %get-tuple-element.234) | copy-start | bytes 3076
  409.4 20.4 %copy-start.78 = (s32[1,256]{1,0:T(1,128)S(1)}, s32[1,256]{1,0:T(1,128)}, u32[]{:S(2)}) copy-start(s32[1,256]{1,0:T(1,128)} %get-tuple-element.235) | copy-start | bytes 3076
  409.4 20.4 %copy-start.83 = (f32[5,2,128]{2,1,0:T(2,128)S(1)}, f32[5,2,128]{2,1,0:T(2,128)}, u32[]{:S(2)}) copy-start(f32[5,2,128]{2,1,0:T(2,128)} %copy-done.82) | copy-start | bytes 15364
  409.4 20.4 %copy-start.85 = (f32[5,1,128]{2,1,0:T(1,128)S(1)}, f32[5,1,128]{2,1,0:T(1,128)}, u32[]{:S(2)}) copy-start(f32[5,1,128]{2,1,0:T(1,128)} %copy-done.84) | copy-start | bytes 7684
  409.7 20.6 %copy-start.59 = (f32[1,256]{1,0:T(1,128)S(1)}, f32[1,256]{1,0:T(1,128)}, u32[]{:S(2)}) copy-start(f32[1,256]{1,0:T(1,128)} %copy-done.58) | copy-start | bytes 3076
  409.7 20.6 %copy-start.63 = (f32[1,256]{1,0:T(1,128)S(1)}, f32[1,256]{1,0:T(1,128)}, u32[]{:S(2)}) copy-start(f32[1,256]{1,0:T(1,128)} %copy-done.62) | copy-start | bytes 3076
  410.5 26.6 %copy-start.61 = (f32[1,256]{1,0:T(1,128)S(1)}, f32[1,256]{1,0:T(1,128)}, u32[]{:S(2)}) copy-start(f32[1,256]{1,0:T(1,128)} %copy-done.60) | copy-start | bytes 3076
  427.8 3.4 collective-permute-start.12
  428.5 2.9 collective-permute-start.13
  431.4 7.7 %collective-permute-start.14 = (f32[3,8,16]{0,2,1:T(8,128)S(1)}, f32[3,8,16]{0,2,1:T(8,128)S(1)}, u32[]{:S(2)}, u32[]{:S(2)}) collective-permute-start(f32[3,8,16]{0,2,1:T(8,128)S(1)} %get-tuple-element.187), channel_id=1, source_target_pairs={{0,504},{8,0},{16,8},{24,16},{32,24},{40,32},{48,40},{56,48},{64,5... | collective-permute-start | bytes 4616 | tf_op jit(solution)/shard_map/ppermute | solution.py:17
  437.1 8.3 %collective-permute-start.15 = (f32[3,8,16]{0,2,1:T(8,128)S(1)}, f32[3,8,16]{0,2,1:T(8,128)S(1)}, u32[]{:S(2)}, u32[]{:S(2)}) collective-permute-start(f32[3,8,16]{0,2,1:T(8,128)S(1)} %get-tuple-element.186), channel_id=1, source_target_pairs={{0,8},{8,16},{16,24},{24,32},{32,40},{40,48},{48,56},{56,64},{64,7... | collective-permute-start | bytes 4616 | tf_op jit(solution)/shard_map/ppermute | solution.py:17
  (44 other events, 182.9 us)
where the time goes:
time: 457 us; the launch traced here: 447 us
  blocking collectives  127 us (28%)
  local copies, waits for them, and re-layouts  88.3 us (19%)
  matrix products  72 us (16%)
  starting transfers between devices  67.7 us (15%)
  other arithmetic  55.2 us (12%)
  waiting for transfers between devices  31 us (7%)
  between operations  5.89 us (1%)
    psum x1, blocking collectives, shards(): totals = lax.psum((jnp.sum(site_energy), long_part), ('gx', 'gy'))  99.6 us
    ppermute x16, starting transfers between devices, passed_along(): lax.ppermute(array, axis, [(i, (i + by) % devices) for i in range(devices)])  49.2 us
    dot_general x20, matrix products, apply_table(): jnp.einsum('...j,kj->...k', last_axis, table, precision=highest)  24.4 us
    unnamed x193, local copies, waits for them, and re-layouts  24.3 us
    all_to_all x1, blocking collectives, shards(): lax.all_to_all(jnp.stack([real, imag]), 'gx', split_axis=1, concat_axis=2...  17.4 us
    scatter-add x1, other arithmetic, interaction(): jnp.take(ext_pos.reshape(3, -1), flat_target, axis=1)  17.1 us
    ppermute x16, waiting for transfers between devices, passed_along(): lax.ppermute(array, axis, [(i, (i + by) % devices) for i in range(devices)])  15.4 us
    dot_general x3, matrix products, interaction(): jnp.einsum('ckn,mkn->mcn', weighted[2], second_order, precision=highest)  14.7 us
  transfers between devices with their start and end apart: 18, of which 10 were waited for; matrix products, arithmetic and copies ran while one was open for 4% of the time, Pallas kernels for 0%

commit v1 on v0

v1 whole, which is shorter than its diff:
```python
import math

import jax
import jax.numpy as jnp
import numpy as np
from jax import lax
from jax.experimental import pallas as pl
from jax.experimental.pallas import tpu as pltpu
from jax.sharding import PartitionSpec as P

NZ = 128
N_GX = 64
N_GY = 8
K = 12
C = 128
RH = 64
NB = 8
ATOMS_ALL = 131072
ATOM = 256
EXT = 640
CUTOFF = 20.0
BETA = 0.5

PLANE0 = -1
PLANES = 5
ROW0 = -1
ROWS = 19
ROW_PAD = 24
SUM_ROW = 23
SUM_LANE = 16 * PLANES

highest = lax.Precision.HIGHEST
f32 = jnp.float32
bf16 = jnp.bfloat16


def real_basis(n):
    cell = np.arange(n)
    rows = [np.full(n, 1.0 / math.sqrt(n))]
    freq = [0]
    for m in range(1, n // 2):
        angle = 2.0 * math.pi / n * (m * cell % n)
        rows += [math.sqrt(2.0 / n) * np.cos(angle), math.sqrt(2.0 / n) * np.sin(angle)]
        freq += [m, m]
    rows.append(np.where(cell % 2 == 0, 1.0, -1.0) / math.sqrt(n))
    freq.append(n // 2)
    return np.stack(rows), np.array(freq)


def tables():
    basis, freq = real_basis(NZ)
    wave = 2.0 * math.pi / NZ * freq
    square = wave * wave
    gain = np.exp(-square / (4.0 * BETA**2)) * (6.0 / (4.0 + 2.0 * np.cos(wave))) ** 2

    plane = (2 * np.arange(N_GX)[None, :] + PLANE0 + np.arange(PLANES)[:, None]) % NZ
    x_in = np.concatenate([basis[:, plane[p]] for p in range(PLANES)], axis=0)
    x_out = np.concatenate([basis[:, plane[p]].T for p in range(PLANES)], axis=0)

    y_in = np.zeros((NZ, N_GY * ROW_PAD))
    for j in range(N_GY):
        for r in range(ROWS):
            y_in[:, j * ROW_PAD + r] = basis[:, (16 * j + ROW0 + r) % NZ]
        y_in[:, j * ROW_PAD + SUM_ROW] = 1.0

    x_side = np.zeros((NZ, NZ, 2))
    x_side[:, :, 0] = 4.0 * math.pi * gain[:, None]
    x_side[:, :, 1] = square[:, None]

    yz = np.zeros((N_GX * N_GY, 4, 128))
    for i in range(N_GX):
        for j in range(N_GY):
            z = slice(16 * j, 16 * j + 16)
            for half in range(2):
                y = i + 64 * half
                yz[i * N_GY + j, 2 * half, :16] = gain[y] * gain[z]
                yz[i * N_GY + j, 2 * half + 1, :16] = square[y] + square[z]
    as32 = lambda a: np.ascontiguousarray(a, dtype=np.float32)
    return {
        "z": as32(basis),
        "y_in": as32(y_in),
        "y_out": as32(y_in.T),
        "x_in": as32(x_in),
        "x_out": as32(x_out),
        "x_gain": as32(x_side[:, :, 0]),
        "x_square": as32(x_side[:, :, 1]),
        "yz": as32(yz),
    }


TABLES = tables()


def dot(a, b, precision=None):
    return jnp.dot(a, b, precision=precision, preferred_element_type=f32)


def dot_nt(a, b, precision=None):
    return lax.dot_general(
        a, b, (((1,), (1,)), ((), ())), precision=precision, preferred_element_type=f32
    )


def halves(x):
    high = x.astype(bf16).astype(f32)
    return high, x - high


def spline(f):
    g = 1.0 - f
    f2 = f * f
    f3 = f2 * f
    weights = [
        g * g * g / 6.0,
        (3.0 * f3 - 6.0 * f2 + 4.0) / 6.0,
        (-3.0 * f3 + 3.0 * f2 + 3.0 * f + 1.0) / 6.0,
        f3 / 6.0,
    ]
    slopes = [-0.5 * g * g, 1.5 * f2 - 2.0 * f, -1.5 * f2 + f + 0.5, 0.5 * f2]
    return weights, slopes


def spline_rows(u, first, rows, periodic):
    floor = jnp.floor(u)
    base = floor.astype(jnp.int32)
    weights, slopes = spline(u - floor)
    cell = lax.broadcasted_iota(jnp.int32, (rows, u.shape[1]), 0) + first
    table = jnp.zeros((rows, u.shape[1]), f32)
    slope_table = jnp.zeros((rows, u.shape[1]), f32)
    for step in range(4):
        target = base + (step - 1)
        if periodic:
            target = target & (rows - 1)
        hit = cell == target
        table = jnp.where(hit, weights[step], table)
        slope_table = jnp.where(hit, slopes[step], slope_table)
    return table, slope_table


def edge_targets(codes):
    shape = codes.shape
    e = codes + (codes >= 13).astype(jnp.int32)
    nine = (e >= 9).astype(jnp.int32) + (e >= 18).astype(jnp.int32)
    rest = e - 9 * nine
    three = (rest >= 3).astype(jnp.int32) + (rest >= 6).astype(jnp.int32)
    step_z = rest - 3 * three - 1
    n = lax.broadcasted_iota(jnp.int32, shape, 1)
    plane = (n >> 7) + nine
    row = ((n >> 4) & 7) + three - 1
    z = (n & 15) + step_z
    wrap = (z >= 16).astype(jnp.int32) - (z < 0).astype(jnp.int32)
    z = z - 16 * wrap
    target = jnp.where(
        row < 0,
        512 + plane * 16 + z,
        jnp.where(row > 7, 576 + plane * 16 + z, plane * 128 + row * 16 + z),
    )
    return target, wrap


def one_hot(target_ref, k):
    row = jnp.broadcast_to(target_ref[pl.ds(k, 1), :], (EXT, ATOM))
    column = lax.broadcasted_iota(jnp.int32, (EXT, ATOM), 0)
    return jnp.where(column == row, 1.0, 0.0).astype(bf16)


EDGE_SCRATCH = [
    pltpu.VMEM((136, EXT), f32),
    pltpu.VMEM((288, EXT), bf16),
    pltpu.VMEM((K, ATOM), jnp.int32),
    pltpu.VMEM((3, K, ATOM), f32),
    pltpu.VMEM((K, C, ATOM), f32),
    pltpu.VMEM((K, NB, ATOM), f32),
    pltpu.VMEM((K, NB, ATOM), f32),
    pltpu.VMEM((K, 8, 8, ATOM), f32),
    pltpu.VMEM((3 * C, 3 * RH), f32),
    pltpu.VMEM((K, 3 * C, ATOM), f32),
    pltpu.VMEM((9, C, ATOM), f32),
    pltpu.VMEM((8, C), f32),
]


def edges(left, own, right, low, high, codes, up_weight, radial_in, radial_out, scratch, slopes):
    (table, split, target_ref, near, up, basis, basis_slope, harm, weights, radial, sums, _) = (
        scratch
    )
    table[:, 0:128] = left[...]
    table[:, 128:384] = own[...]
    table[:, 384:512] = right[...]
    table[:, 512:576] = low[...]
    table[:, 576:640] = high[...]

    w_high, w_low = halves(up_weight[...])
    t_high, t_low = halves(table[0:C, :])
    t_high = t_high.astype(bf16)
    mapped = dot(w_high.astype(bf16), t_high)
    mapped = mapped + dot(w_high.astype(bf16), t_low.astype(bf16))
    mapped = mapped + dot(w_low.astype(bf16), t_high)
    m_high, m_low = halves(mapped)
    split[0:C, :] = m_high.astype(bf16)
    split[C : 2 * C, :] = m_low.astype(bf16)

    lane = lax.broadcasted_iota(jnp.int32, (8, EXT), 1)
    part = lax.broadcasted_iota(jnp.int32, (8, EXT), 0)
    plane = jnp.where(lane < 512, lane >> 7, (lane >> 4) & 3)
    shift_x = jnp.where(plane == 0, -2.0, jnp.where(plane == 3, 2.0, 0.0))
    shift_y = jnp.where(lane >= 576, 16.0, jnp.where(lane >= 512, -16.0, 0.0))
    places = table[C : C + 8, :] + jnp.where(
        part == 0, shift_x, jnp.where(part == 1, shift_y, 0.0)
    )
    p_high, p_rest = halves(places)
    p_mid, p_low = halves(p_rest)
    split[2 * C : 2 * C + 32, :] = jnp.concatenate(
        [p_high, p_mid, p_low, jnp.zeros_like(p_low)], axis=0
    ).astype(bf16)

    target, wrap = edge_targets(codes[...])
    target_ref[...] = target

    def gather(k, carry):
        found = dot(split[...], one_hot(target_ref, k))
        up[k] = found[0:C] + found[C : 2 * C]
        place = found[256:264] + found[264:272] + found[272:280]
        for c in range(3):
            near[c, pl.ds(k, 1), :] = place[c : c + 1]
        return carry

    lax.fori_loop(0, K, gather, 0)

    rel_x = near[0] - own[C : C + 1, :]
    rel_y = near[1] - own[C + 1 : C + 2, :]
    rel_z = near[2] - own[C + 2 : C + 3, :] + wrap.astype(f32) * float(NZ)
    square = rel_x * rel_x + rel_y * rel_y + rel_z * rel_z
    dist = jnp.sqrt(square)
    inv = 1.0 / dist
    ux, uy, uz = rel_x * inv, rel_y * inv, rel_z * inv
    r3, r5, r15 = math.sqrt(3.0), math.sqrt(5.0), math.sqrt(15.0)
    harmonic = [
        r3 * ux,
        r3 * uy,
        r3 * uz,
        r15 * ux * uy,
        r15 * uy * uz,
        0.5 * r5 * (3.0 * uz * uz - 1.0),
        r15 * ux * uz,
        0.5 * r15 * (ux * ux - uy * uy),
    ]
    for m in range(8):
        for k in range(K):
            harm[k, m] = jnp.broadcast_to(harmonic[m][k : k + 1, :], (8, ATOM))

    t = dist * (1.0 / CUTOFF)
    t2 = t * t
    t4 = t2 * t2
    t5 = t4 * t
    t6 = t4 * t2
    envelope = 1.0 - t6 * (28.0 - t * (48.0 - 21.0 * t))
    theta = math.pi * t
    sines, cosines = {1: jnp.sin(theta)}, {1: jnp.cos(theta)}
    for b in range(2, NB + 1):
        i, j = (b + 1) // 2, b // 2
        sines[b] = sines[i] * cosines[j] + cosines[i] * sines[j]
        cosines[b] = cosines[i] * cosines[j] - sines[i] * sines[j]
    scale = math.sqrt(2.0 / CUTOFF)
    shape = scale * envelope * inv
    if slopes:
        envelope_slope = (-168.0 / CUTOFF) * t5 * (1.0 - t) * (1.0 - t)
        shape_slope = scale * inv * (envelope_slope - envelope * inv)
    for b in range(1, NB + 1):
        value = sines[b] * shape
        for k in range(K):
            basis[k, b - 1 : b, :] = value[k : k + 1, :]
        if slopes:
            value = (b * math.pi / CUTOFF) * cosines[b] * shape + sines[b] * shape_slope
            for k in range(K):
                basis_slope[k, b - 1 : b, :] = value[k : k + 1, :]

    o_high, o_low = halves(radial_out[...])
    weights[:, 0:RH] = o_high
    weights[:, RH : 2 * RH] = o_high
    weights[:, 2 * RH : 3 * RH] = o_low
    wide = weights[...].astype(bf16)

    def layered(hidden):
        s_high, s_low = halves(hidden)
        return dot(wide, jnp.concatenate([s_high, s_low, s_high], axis=0).astype(bf16))

    for k in range(K):
        before = dot(radial_in[...], basis[k], highest)
        gate = jax.nn.sigmoid(before)
        radial[k] = layered(before * gate)
        if slopes:
            before_slope = dot(radial_in[...], basis_slope[k], highest)
            gate_slope = gate * (1.0 + before * (1.0 - gate))
            slopes[0][k] = layered(gate_slope * before_slope)

    def accumulate(step, carry):
        c0 = pl.multiple_of((step % 16) * 8, 8)
        n0 = pl.multiple_of((step // 16) * 128, 128)
        total = [jnp.zeros((8, 128), f32) for _ in range(9)]
        for k in range(K):
            u = up[k, pl.ds(c0, 8), pl.ds(n0, 128)]
            total[0] += radial[k, pl.ds(c0, 8), pl.ds(n0, 128)] * u
            first = radial[k, pl.ds(c0 + C, 8), pl.ds(n0, 128)] * u
            second = radial[k, pl.ds(c0 + 2 * C, 8), pl.ds(n0, 128)] * u
            for m in range(8):
                total[1 + m] += (first if m < 3 else second) * harm[k, m, :, pl.ds(n0, 128)]
        for m in range(9):
            sums[m, pl.ds(c0, 8), pl.ds(n0, 128)] = total[m]
        return carry

    lax.fori_loop(0, 32, accumulate, 0)
    return dist, inv, ux, uy, uz


def readout_rows(readout, charge_weight, mix_weight, rows):
    rows[...] = jnp.zeros_like(rows)
    rows[0:1, :] = readout[...]
    rows[1:2, :] = charge_weight[...]
    return rows[...], dot(rows[...], mix_weight[...], highest)


def charges_kernel(
    left, own, right, low, high, codes, up_weight, radial_in, radial_out, coupling, mix_weight,
    readout, charge_weight, z_table, spread, charge_out, *scratch,
):
    own_pos = own[C : C + 8, :]
    weights_x, _ = spline_rows(own_pos[0:1], PLANE0, 8, False)
    weights_y, _ = spline_rows(own_pos[1:2], ROW0, ROW_PAD, False)
    weights_z, _ = spline_rows(own_pos[2:3], 0, NZ, True)
    waves_z = dot(z_table[...], weights_z, highest)

    edges(
        left, own, right, low, high, codes, up_weight, radial_in, radial_out, scratch, None
    )
    sums = scratch[10]
    direct, mixed = readout_rows(readout, charge_weight, mix_weight, scratch[11])
    inv_k = 1.0 / K
    first = sum(sums[m] * sums[m] for m in range(1, 4))
    second = sum(sums[m] * sums[m] for m in range(4, 9))
    outs = dot(direct, own[0:C, :], highest)
    outs = outs + dot(mixed * inv_k, sums[0], highest)
    outs = outs + dot(mixed * coupling[0:1, :] * inv_k**2, first, highest)
    outs = outs + dot(mixed * coupling[1:2, :] * inv_k**2, second, highest)
    site = jnp.sum(outs[0:1, :])
    charge = outs[1:2, :]
    charge_out[...] = charge

    charged = weights_y * charge
    planes = [dot_nt(charged * weights_x[p : p + 1], waves_z, highest) for p in range(PLANES)]
    lane = lax.broadcasted_iota(jnp.int32, (ROW_PAD, 128), 1)
    row = lax.broadcasted_iota(jnp.int32, (ROW_PAD, 128), 0)
    extra = jnp.where((lane == SUM_LANE) & (row == SUM_ROW), site, 0.0)
    for g in range(N_GY):
        part = extra
        for p in range(PLANES):
            moved = pltpu.roll(planes[p], (16 * (p - g)) % 128, 1)
            part = jnp.where((lane >> 4) == p, moved, part)
        spread[g] = part


def y_in_kernel(rows, table, out):
    waves = dot(table[...], rows[...].reshape(N_GY * ROW_PAD, 128), highest)
    out[:, 0, :] = waves[0:64]
    out[:, 1, :] = waves[64:128]


def x_kernel(planes, x_in, x_out, x_gain, x_square, yz, out):
    sides = jnp.concatenate([planes[:, 0, :], planes[:, 1, :]], axis=1)
    site = jnp.sum(planes[:, 0, SUM_LANE : SUM_LANE + 1])
    waves = dot(x_in[...], sides, highest)
    filtered = []
    energy = site * (1.0 / (N_GX * N_GY))
    for half in range(2):
        total = waves[0:128, 128 * half : 128 * half + 128]
        for p in range(1, PLANES):
            block = waves[128 * p : 128 * p + 128, 128 * half : 128 * half + 128]
            total = total + pltpu.roll(block, (128 - 16 * p) % 128, 1)
        square = x_square[...] + yz[0, 2 * half + 1 : 2 * half + 2, :]
        anchor = square == 0.0
        kernel = jnp.where(
            anchor,
            0.0,
            x_gain[...] * yz[0, 2 * half : 2 * half + 1, :] / jnp.where(anchor, 1.0, square),
        )
        shaped = kernel * total
        energy = energy + 0.5 * jnp.sum(shaped * total)
        filtered.append(shaped)
    back = dot(x_out[...], jnp.concatenate(filtered, axis=1), highest)
    lane = lax.broadcasted_iota(jnp.int32, (64, 128), 1)
    for half in range(2):
        total = jnp.where(lane == SUM_LANE, energy, 0.0) if half == 0 else jnp.zeros((64, 128), f32)
        for p in range(PLANES):
            block = back[64 * p : 64 * p + 64, 128 * half : 128 * half + 128]
            moved = pltpu.roll(block, 16 * p, 1) if p else block
            total = total + moved
        out[:, half, :] = total


def y_out_kernel(waves, table, out):
    both = jnp.concatenate([waves[:, 0, :], waves[:, 1, :]], axis=0)
    out[...] = dot(table[...], both, highest).reshape(N_GY, ROW_PAD, 128)


def slopes_kernel(
    left, own, right, low, high, codes, up_weight, radial_in, radial_out, coupling, mix_weight,
    readout, charge_weight, pulls, *scratch,
):
    edge_scratch, (radial_slope, columns, gathered) = scratch[:12], scratch[12:]
    dist, inv, ux, uy, uz = edges(
        left, own, right, low, high, codes, up_weight, radial_in, radial_out, edge_scratch,
        (radial_slope,),
    )
    up, harm, radial, sums = (edge_scratch[i] for i in (4, 7, 9, 10))
    _, mixed = readout_rows(readout, charge_weight, mix_weight, edge_scratch[11])
    part = lax.broadcasted_iota(jnp.int32, (8, C), 0)
    inv_k = 1.0 / K
    rows = mixed * inv_k
    rows = jnp.where(part == 2, coupling[0:1, :] * (2.0 * inv_k), rows)
    rows = jnp.where(part == 3, coupling[1:2, :] * (2.0 * inv_k), rows)
    standing = rows.T
    for i in range(4):
        columns[i] = jnp.broadcast_to(standing[:, i : i + 1], (C, 128))
    for m in range(1, 9):
        for half in range(2):
            lanes = slice(128 * half, 128 * half + 128)
            sums[m, :, lanes] = sums[m, :, lanes] * columns[2 if m < 4 else 3]

    def pull(step, carry):
        k = step // 2
        n0 = pl.multiple_of((step % 2) * 128, 128)
        spots = pl.ds(n0, 128)
        total = [jnp.zeros((8, 128), f32) for _ in range(18)]
        shapes = [harm[k, m, :, spots] for m in range(8)]
        for block in range(16):
            c0 = 8 * block
            u = up[k, c0 : c0 + 8, spots]
            along = [sums[1 + m, c0 : c0 + 8, spots] for m in range(8)]
            turn_1 = sum(along[m] * shapes[m] for m in range(3))
            turn_2 = sum(along[m] * shapes[m] for m in range(3, 8))
            stretch = u * (
                radial_slope[k, c0 : c0 + 8, spots]
                + radial_slope[k, C + c0 : C + c0 + 8, spots] * turn_1
                + radial_slope[k, 2 * C + c0 : 2 * C + c0 + 8, spots] * turn_2
            )
            first = radial[k, C + c0 : C + c0 + 8, spots] * u
            second = radial[k, 2 * C + c0 : 2 * C + c0 + 8, spots] * u
            for w in range(2):
                weight = columns[w, c0 : c0 + 8, :]
                total[9 * w] += weight * stretch
                first_w = weight * first
                second_w = weight * second
                for m in range(8):
                    total[9 * w + 1 + m] += (first_w if m < 3 else second_w) * along[m]
        sums_18 = [jnp.sum(total[i], axis=0, keepdims=True) for i in range(18)]
        gathered[k, :, spots] = jnp.concatenate(sums_18 + [jnp.zeros((6, 128), f32)], axis=0)
        return carry

    lax.fori_loop(0, 2 * K, pull, 0)

    r3, r5, r15 = math.sqrt(3.0), math.sqrt(5.0), math.sqrt(15.0)
    for w in range(2):
        g = [
            jnp.concatenate([gathered[k, 9 * w + i : 9 * w + i + 1, :] for k in range(K)], axis=0)
            for i in range(9)
        ]
        vx = r3 * g[1] + r15 * (uy * g[4] + uz * g[7] + ux * g[8])
        vy = r3 * g[2] + r15 * (ux * g[4] + uz * g[5] - uy * g[8])
        vz = r3 * g[3] + r15 * (uy * g[5] + ux * g[7]) + (3.0 * r5) * uz * g[6]
        radial_part = g[0] - (vx * ux + vy * uy + vz * uz) * inv
        pulls[3 * w] = radial_part * ux + vx * inv
        pulls[3 * w + 1] = radial_part * uy + vy * inv
        pulls[3 * w + 2] = radial_part * uz + vz * inv


def final_kernel(potential, positions, codes, charge, z_table, pulls, out, energy_out, target_ref):
    target, _ = edge_targets(codes[...])
    target_ref[...] = target
    weights_x, slopes_x = spline_rows(positions[0:1, :], PLANE0, 8, False)
    weights_y, slopes_y = spline_rows(positions[1:2, :], ROW0, ROW_PAD, False)
    weights_z, slopes_z = spline_rows(positions[2:3, :], 0, NZ, True)
    waves = dot(z_table[...], jnp.concatenate([weights_z, slopes_z], axis=1), highest)

    lane = lax.broadcasted_iota(jnp.int32, (ROW_PAD, 128), 1)
    phi = jnp.zeros((1, ATOM), f32)
    slope = [phi, phi, phi]
    energy = jnp.zeros((1, 1), f32)
    for g in range(N_GY):
        energy = energy + potential[g, SUM_ROW : SUM_ROW + 1, SUM_LANE : SUM_LANE + 1]
    energy_out[...] = energy * (1.0 / ATOMS_ALL)
    for p in range(PLANES):
        plane = jnp.zeros((ROW_PAD, 128), f32)
        for g in range(N_GY):
            amount = (16 * (g - p)) % 128
            moved = pltpu.roll(potential[g], amount, 1) if amount else potential[g]
            plane = jnp.where((lane >> 4) == g, moved, plane)
        felt = dot(plane, waves, highest)
        here = felt[:, 0:ATOM]
        by_y = jnp.sum(here * weights_y, axis=0, keepdims=True)
        phi = phi + by_y * weights_x[p : p + 1]
        slope[0] = slope[0] + by_y * slopes_x[p : p + 1]
        by_y = jnp.sum(here * slopes_y, axis=0, keepdims=True)
        slope[1] = slope[1] + by_y * weights_x[p : p + 1]
        by_y = jnp.sum(felt[:, ATOM:] * weights_y, axis=0, keepdims=True)
        slope[2] = slope[2] + by_y * weights_x[p : p + 1]

    total = [pulls[c] + phi * pulls[3 + c] for c in range(3)]
    out[...] = jnp.zeros_like(out)
    table = jnp.zeros((16, EXT), f32)
    for k in range(K):
        rows = jnp.concatenate(
            [total[c][k : k + 1, :] for c in range(3)] + [jnp.zeros((5, ATOM), f32)], axis=0
        )
        high, low = halves(rows)
        both = jnp.concatenate([high, low], axis=0).astype(bf16)
        table = table + dot_nt(both, one_hot(target_ref, k))
    out[...] = table[0:8] + table[8:16]
    for c in range(3):
        own = charge[...] * slope[c] - jnp.sum(total[c], axis=0, keepdims=True)
        out[c : c + 1, 128:384] = out[c : c + 1, 128:384] + own


def call(kernel, outs, scratch, flops, *args):
    return pl.pallas_call(
        kernel,
        out_shape=outs,
        scratch_shapes=scratch,
        compiler_params=pltpu.CompilerParams(vmem_limit_bytes=48 * 1024 * 1024),
        cost_estimate=pl.CostEstimate(flops=flops, bytes_accessed=2000000, transcendentals=0),
    )(*args)


def passed_along(array, axis, by):
    devices = lax.axis_size(axis)
    return lax.ppermute(array, axis, [(i, (i + by) % devices) for i in range(devices)])


def struct(*shape):
    return jax.ShapeDtypeStruct(shape, f32)


def shards(
    positions, features, neighbours, up_weight, radial_in, radial_out, coupling, mix_weight,
    readout, charge_weight,
):
    table = {name: jnp.asarray(value) for name, value in TABLES.items()}
    own = jnp.concatenate([features, positions, jnp.zeros((5, ATOM), f32)], axis=0)
    left = passed_along(own[:, 128:256], "gx", 1)
    right = passed_along(own[:, 0:128], "gx", -1)
    low = passed_along(
        jnp.concatenate([left[:, 112:], own[:, 112:128], own[:, 240:], right[:, 112:]], axis=1),
        "gy",
        1,
    )
    high = passed_along(
        jnp.concatenate([left[:, :16], own[:, 0:16], own[:, 128:144], right[:, :16]], axis=1),
        "gy",
        -1,
    )
    edge_args = (left, own, right, low, high, neighbours, up_weight, radial_in, radial_out)
    weight_args = (coupling, mix_weight, readout.reshape(1, C), charge_weight.reshape(1, C))

    spread, charge = call(
        charges_kernel,
        (struct(N_GY, ROW_PAD, 128), struct(1, ATOM)),
        EDGE_SCRATCH,
        10**9,
        *edge_args,
        *weight_args,
        table["z"],
    )
    rows = lax.all_to_all(spread, "gy", split_axis=0, concat_axis=0, tiled=True)
    waves = call(y_in_kernel, struct(N_GX, 2, 128), [], 10**7, rows, table["y_in"])
    planes = lax.all_to_all(waves, "gx", split_axis=0, concat_axis=0, tiled=True)
    device = lax.axis_index("gx") * N_GY + lax.axis_index("gy")
    yz = lax.dynamic_slice(table["yz"], (device, 0, 0), (1, 4, 128))
    waves = call(
        x_kernel,
        struct(N_GX, 2, 128),
        [],
        10**7,
        planes,
        table["x_in"],
        table["x_out"],
        table["x_gain"],
        table["x_square"],
        yz,
    )
    waves = lax.all_to_all(waves, "gx", split_axis=0, concat_axis=0, tiled=True)
    rows = call(y_out_kernel, struct(N_GY, ROW_PAD, 128), [], 10**7, waves, table["y_out"])
    potential = lax.all_to_all(rows, "gy", split_axis=0, concat_axis=0, tiled=True)

    pulls = call(
        slopes_kernel,
        struct(6, K, ATOM),
        EDGE_SCRATCH
        + [
            pltpu.VMEM((K, 3 * C, ATOM), f32),
            pltpu.VMEM((4, C, 128), f32),
            pltpu.VMEM((K, 24, ATOM), f32),
        ],
        4 * 10**9,
        *edge_args,
        *weight_args,
    )
    gradient, energy = call(
        final_kernel,
        (struct(8, EXT), struct(1, 1)),
        [pltpu.VMEM((K, ATOM), jnp.int32)],
        10**9,
        potential,
        positions,
        neighbours,
        charge,
        table["z"],
        pulls,
    )
    gradient = gradient[:3]
    from_high = passed_along(gradient[:, 512:576], "gy", -1)
    from_low = passed_along(gradient[:, 576:640], "gy", 1)
    main = gradient[:, :512].reshape(3, 4, 8, 16)
    main = main.at[:, :, 7].add(from_high.reshape(3, 4, 16))
    main = main.at[:, :, 0].add(from_low.reshape(3, 4, 16))
    main = main.reshape(3, 4, 128)
    from_right = passed_along(main[:, 0], "gx", -1)
    from_left = passed_along(main[:, 3], "gx", 1)
    forces = -jnp.concatenate([main[:, 1] + from_left, main[:, 2] + from_right], axis=1)
    return (forces, energy.reshape(()))


def solution(mesh):
    placed = (P(None, ("gx", "gy")),) * 3 + (P(),) * 7
    return jax.shard_map(
        shards, mesh=mesh, in_specs=placed, out_specs=(P(None, ("gx", "gy")), P()), check_vma=False
    )
```

time: 457 us -> 134 us (0.29)
  the two profiles are of different devices: /device:TPU:1 before, /device:TPU:6 now
where the time goes in v1:
time: 134 us
  starting transfers between devices  38.1 us (28%)
  waiting for transfers between devices  32 us (24%)
  Pallas kernels  29.9 us (22%)
  blocking collectives  27.5 us (21%)
  local copies, waits for them, and re-layouts  3.15 us (2%)
  other arithmetic  1.88 us (1%)
    pallas_call x6, Pallas kernels, call(): pl.pallas_call(kernel, out_shape=outs, scratch_shapes=scratch, compiler_p...  29.9 us
    ppermute x8, waiting for transfers between devices, passed_along(): lax.ppermute(array, axis, [(i, (i + by) % devices) for i in range(devices)])  19.7 us
    all_to_all x1, blocking collectives, shards(): waves = lax.all_to_all(waves, 'gx', split_axis=0, concat_axis=0, tiled=True)  19.2 us
    all_to_all x1, starting transfers between devices, shards(): lax.all_to_all(waves, 'gx', split_axis=0, concat_axis=0, tiled=True)  18.3 us
    ppermute x8, starting transfers between devices, passed_along(): lax.ppermute(array, axis, [(i, (i + by) % devices) for i in range(devices)])  16.3 us
    all_to_all x1, waiting for transfers between devices, shards(): lax.all_to_all(waves, 'gx', split_axis=0, concat_axis=0, tiled=True)  12.3 us
    all_to_all x1, blocking collectives, shards(): rows = lax.all_to_all(spread, 'gy', split_axis=0, concat_axis=0, tiled=True)  8.31 us
    all_to_all x1, starting transfers between devices, shards(): lax.all_to_all(rows, 'gy', split_axis=0, concat_axis=0, tiled=True)  3.54 us
  transfers between devices with their start and end apart: 10, of which 8 were waited for; matrix products, arithmetic and copies ran while one was open for 1% of the time, Pallas kernels for 11%

profile of v1, /device:TPU:6, one launch (start us, length us, event | category | flops | bytes accessed | tf_op | source)
XLA Modules:
  0.0 133.6 jit_solution(4691897891988705249)
XLA Ops:
  0.6 0.1 pad.16.clone
  0.7 1.0 maximum_maximum_fusion.own
  1.7 3.7 %collective-permute-start = (f32[136,128]{1,0:T(8,128)S(1)}, f32[136,128]{1,0:T(8,128)S(1)}, u32[]{:S(2)}, u32[]{:S(2)}) collective-permute-start(f32[136,128]{1,0:T(8,128)S(1)} %get-tuple-element.39), channel_id=1, source_target_pairs={{0,8},{8,16},{16,24},{24,32},{32,40},{40,48},{48,56},{56,64},{64,7... | collective-permute-start | bytes 208904 | tf_op jit(solution)/shard_map/ppermute | solution.py:535
  5.5 2.1 %collective-permute-start.1 = (f32[136,128]{1,0:T(8,128)S(1)}, f32[136,128]{1,0:T(8,128)S(1)}, u32[]{:S(2)}, u32[]{:S(2)}) collective-permute-start(f32[136,128]{1,0:T(8,128)S(1)} %get-tuple-element.38), channel_id=1, source_target_pairs={{0,504},{8,0},{16,8},{24,16},{32,24},{40,32},{48,40},{56,48},{64,5... | collective-permute-start | bytes 208904 | tf_op jit(solution)/shard_map/ppermute | solution.py:535
  7.6 0.1 fusion.2
  7.7 0.2 collective-permute-done.left
  7.9 0.1 fusion.4
  8.0 5.8 %collective-permute-done.1.right = f32[136,128]{1,0:T(8,128)S(1)} collective-permute-done((f32[136,128]{1,0:T(8,128)S(1)}, f32[136,128]{1,0:T(8,128)S(1)}, u32[]{:S(2)}, u32[]{:S(2)}) %collective-permute-start.1) | collective-permute-done | bytes 69664 | tf_op jit(solution)/shard_map/ppermute | solution.py:535
  13.8 0.1 fusion.5
  13.9 0.1 pad_maximum_fusion.1
  14.0 1.0 collective-permute-start.3
  15.1 0.1 pad_maximum_fusion
  15.2 0.0 copy-start.15
  15.2 0.0 copy-start.7
  15.2 0.0 copy-start.8
  15.2 0.0 copy-start.13
  15.2 0.0 collective-permute-start.2
  15.3 0.7 copy-done.14
  16.0 0.1 copy.28.radial_out
  16.1 0.0 copy-done.15
  16.1 0.0 copy-start.9
  16.1 0.0 copy-start.12
  16.1 0.1 copy.27.radial_in
  16.2 0.8 collective-permute-done.3.high
  17.0 3.2 %collective-permute-done.2.low = f32[136,64]{1,0:T(8,128)S(1)} collective-permute-done((f32[136,64]{1,0:T(8,128)S(1)}, f32[136,64]{1,0:T(8,128)S(1)}, u32[]{:S(2)}, u32[]{:S(2)}) %collective-permute-start.2) | collective-permute-done | bytes 34848 | tf_op jit(solution)/shard_map/ppermute | solution.py:535
  20.2 0.0 copy-done.7
  20.2 0.0 copy-done.8
  20.2 0.0 copy-done.13
  20.2 0.0 copy-done.9
  20.2 0.0 copy-done.12
  20.2 0.6 copy-done.10
  20.9 0.0 copy-done.11
  20.9 9.7 %shard_map.185 = (f32[8,24,128]{2,1,0:T(8,128)S(1)}, f32[1,256]{1,0:T(1,128)S(1)}) custom-call(f32[136,128]{1,0:T(8,128)S(1)} %collective-permute-done.left, f32[136,256]{1,0:T(8,128)S(1)} %maximum_maximum_fusion.own, f32[136,128]{1,0:T(8,128)S(1)} %collective-permute-done.1.right, f32[136,64]{1,0:T(8,128)S(1)} %collective-permute-done.2.low, ...), custom_call_target="tpu_custom_call" | custom-call | flops 1000000000 | bytes 2000000 | tf_op jit(solution)/shard_map/pallas_call | solution.py:524
  30.6 0.0 copy-start
  30.6 8.3 %all_to_all.20.rows = f32[8,24,128]{2,1,0:T(8,128)S(1)} all-to-all(f32[8,24,128]{2,1,0:T(8,128)S(1)} %get-tuple-element.30), channel_id=1, replica_groups=mesh['gx'=64,'gy'=8] {'gy'}, dimensions={0} | all-to-all | bytes 196608 | tf_op jit(solution)/shard_map/all_to_all | solution.py:572
  38.9 0.0 copy-done.2
  38.9 0.9 shard_map.186
  39.8 18.3 %all-to-all-start.1 = ((f32[64,2,128]{2,1,0:T(2,128)}), f32[64,2,128]{2,1,0:T(2,128)S(1)}, u32[]{:S(2)}, u32[]{:S(2)}) async-start(f32[64,2,128]{2,1,0:T(2,128)} %shard_map.186), calls=%async_computation.1 | async-start | bytes 131072 | tf_op jit(solution)/shard_map/all_to_all | solution.py:574
  58.2 0.7 constant_dynamic-slice_fusion.yz
  58.9 12.3 %all-to-all-done.1.planes = f32[64,2,128]{2,1,0:T(2,128)S(1)} async-done(((f32[64,2,128]{2,1,0:T(2,128)}), f32[64,2,128]{2,1,0:T(2,128)S(1)}, u32[]{:S(2)}, u32[]{:S(2)}) %all-to-all-start.1) | async-done | bytes 65568 | tf_op jit(solution)/shard_map/all_to_all | solution.py:574
  71.1 0.0 copy-done.1
  71.2 1.7 %shard_map.187 = f32[64,2,128]{2,1,0:T(2,128)S(1)} custom-call(f32[64,2,128]{2,1,0:T(2,128)S(1)} %all-to-all-done.1.planes, f32[640,64]{1,0:T(8,128)S(1)} %copy-done, f32[320,128]{1,0:T(8,128)S(1)} %copy-done.1, f32[128,128]{1,0:T(8,128)S(1)} %copy-done.4, f32[128,128]{1,0:T(8,128)S(1)} %copy-done.5, f32[1,4,128]{2,1,0:T(4,128)S(1)} %constant_dynamic-slice_fusion.yz), custom_call_target="tpu_custom_call" | custom-call | flops 10000000 | bytes 2000000 | tf_op jit(solution)/shard_map/pallas_call | solution.py:524
  72.9 0.0 copy-start.3
  72.9 19.2 %all_to_all.21.waves = f32[64,2,128]{2,1,0:T(2,128)S(1)} all-to-all(f32[64,2,128]{2,1,0:T(2,128)S(1)} %shard_map.187), channel_id=1, replica_groups=mesh['gx'=64,'gy'=8] {'gx'}, dimensions={0} | all-to-all | bytes 131072 | tf_op jit(solution)/shard_map/all_to_all | solution.py:589
  92.1 0.9 shard_map.188
  93.0 3.5 %all-to-all-start.3 = ((f32[8,24,128]{2,1,0:T(8,128)}), f32[8,24,128]{2,1,0:T(8,128)S(1)}, u32[]{:S(2)}, u32[]{:S(2)}) async-start(f32[8,24,128]{2,1,0:T(8,128)} %shard_map.188), calls=%async_computation.3 | async-start | bytes 196608 | tf_op jit(solution)/shard_map/all_to_all | solution.py:591
  96.6 0.0 copy-start.6
  96.6 14.1 %shard_map.189.pulls = f32[6,12,256]{2,1,0:T(8,128)S(1)} custom-call(f32[136,128]{1,0:T(8,128)S(1)} %collective-permute-done.left, f32[136,256]{1,0:T(8,128)S(1)} %maximum_maximum_fusion.own, f32[136,128]{1,0:T(8,128)S(1)} %collective-permute-done.1.right, f32[136,64]{1,0:T(8,128)S(1)} %collective-permute-done.2.low, ...), custom_call_target="tpu_custom_call" | custom-call | flops 4000000000 | bytes 2000000 | tf_op jit(solution)/shard_map/pallas_call | solution.py:524
  110.7 0.0 all-to-all-done.3.potential
  110.7 2.6 %shard_map.190 = (f32[8,640]{1,0:T(8,128)S(1)}, f32[1,1]{1,0:T(1,128)}) custom-call(f32[8,24,128]{2,1,0:T(8,128)S(1)} %all-to-all-done.3.potential, f32[3,256]{1,0:T(4,128)S(1)} %copy-done.6, s32[12,256]{1,0:T(8,128)S(1)} %copy-done.9, f32[1,256]{1,0:T(1,128)S(1)} %get-tuple-element.31.charge, f32[128,128]{1,0:T(8,128)S(1)} %copy-done.13, ...), custom_call_target="tpu_custom_call" | custom-call | flops 1000000000 | bytes 2000000 | tf_op jit(solution)/shard_map/pallas_call | solution.py:524
  113.3 0.1 fusion.6
  113.4 2.7 %collective-permute-start.4 = (f32[3,64]{1,0:T(4,128)S(1)}, f32[3,64]{1,0:T(4,128)S(1)}, u32[]{:S(2)}, u32[]{:S(2)}) collective-permute-start(f32[3,64]{1,0:T(4,128)S(1)} %get-tuple-element.45), channel_id=1, source_target_pairs={{0,7},{1,0},{2,1},{3,2},{4,3},{5,4},{6,5},{7,6},{8,15},{9,8},{10,9... | collective-permute-start | bytes 2312 | tf_op jit(solution)/shard_map/ppermute | solution.py:535
  116.1 0.1 reshape.95
  116.2 0.0 collective-permute-start.5
  116.2 1.2 collective-permute-done.4
  117.4 0.1 reshape.96
  117.6 2.9 %collective-permute-done.5 = f32[3,64]{1,0:T(4,128)S(1)} collective-permute-done((f32[3,64]{1,0:T(4,128)S(1)}, f32[3,64]{1,0:T(4,128)S(1)}, u32[]{:S(2)}, u32[]{:S(2)}) %collective-permute-start.5) | collective-permute-done | bytes 800 | tf_op jit(solution)/shard_map/ppermute | solution.py:535
  120.4 0.1 reshape.97
  120.6 0.1 reshape.98
  120.7 4.7 %collective-permute-start.6 = (f32[3,128]{1,0:T(4,128)S(1)}, f32[3,128]{1,0:T(4,128)S(1)}, u32[]{:S(2)}, u32[]{:S(2)}) collective-permute-start(f32[3,128]{1,0:T(4,128)S(1)} %bitcast.28), channel_id=1, source_target_pairs={{0,8},{8,16},{16,24},{24,32},{32,40},{40,48},{48,56},{56,64},{64,7... | collective-permute-start | bytes 4616 | tf_op jit(solution)/shard_map/ppermute | solution.py:535
  125.4 1.9 %collective-permute-start.7 = (f32[3,128]{1,0:T(4,128)S(1)}, f32[3,128]{1,0:T(4,128)S(1)}, u32[]{:S(2)}, u32[]{:S(2)}) collective-permute-start(f32[3,128]{1,0:T(4,128)S(1)} %bitcast.27), channel_id=1, source_target_pairs={{0,504},{8,0},{16,8},{24,16},{32,24},{40,32},{48,40},{56,48},{64,5... | collective-permute-start | bytes 4616 | tf_op jit(solution)/shard_map/ppermute | solution.py:535
  127.3 0.0 collective-permute-done.6
  127.4 5.6 %collective-permute-done.7 = f32[3,128]{1,0:T(4,128)S(1)} collective-permute-done((f32[3,128]{1,0:T(4,128)S(1)}, f32[3,128]{1,0:T(4,128)S(1)}, u32[]{:S(2)}, u32[]{:S(2)}) %collective-permute-start.7) | collective-permute-done | bytes 1568 | tf_op jit(solution)/shard_map/ppermute | solution.py:535
  133.0 0.6 maximum_negate_fusion
  (24 shorter events, 0.2 us)
Async XLA Ops:
  1.7 6.2 %collective-permute-start = (f32[136,128]{1,0:T(8,128)S(1)}, f32[136,128]{1,0:T(8,128)S(1)}, u32[]{:S(2)}, u32[]{:S(2)}) collective-permute-start(f32[136,128]{1,0:T(8,128)S(1)} %get-tuple-element.39), channel_id=1, source_target_pairs={{0,8},{8,16},{16,24},{24,32},{32,40},{40,48},{48,56},{56,64},{64,7... | collective-permute-start | bytes 208904 | tf_op jit(solution)/shard_map/ppermute | solution.py:535
  5.5 8.3 %collective-permute-start.1 = (f32[136,128]{1,0:T(8,128)S(1)}, f32[136,128]{1,0:T(8,128)S(1)}, u32[]{:S(2)}, u32[]{:S(2)}) collective-permute-start(f32[136,128]{1,0:T(8,128)S(1)} %get-tuple-element.38), channel_id=1, source_target_pairs={{0,504},{8,0},{16,8},{24,16},{32,24},{40,32},{48,40},{56,48},{64,5... | collective-permute-start | bytes 208904 | tf_op jit(solution)/shard_map/ppermute | solution.py:535
  14.0 3.0 %collective-permute-start.3 = (f32[136,64]{1,0:T(8,128)S(1)}, f32[136,64]{1,0:T(8,128)S(1)}, u32[]{:S(2)}, u32[]{:S(2)}) collective-permute-start(f32[136,64]{1,0:T(8,128)S(1)} %pad_maximum_fusion.1), channel_id=1, source_target_pairs={{0,7},{1,0},{2,1},{3,2},{4,3},{5,4},{6,5},{7,6},{8,15},{9,8},{10,9... | collective-permute-start | bytes 104456 | tf_op jit(solution)/shard_map/ppermute | solution.py:535
  15.1 0.9 copy-start.14
  15.2 0.9 copy-start.15
  15.2 5.0 %copy-start.7 = (f32[128,128]{1,0:T(8,128)S(1)}, f32[128,128]{1,0:T(8,128)}, u32[]{:S(2)}) copy-start(f32[128,128]{1,0:T(8,128)} %up_weight.3) | copy-start | bytes 196612
  15.2 5.0 %copy-start.8 = (f32[128,128]{1,0:T(8,128)S(1)}, f32[128,128]{1,0:T(8,128)}, u32[]{:S(2)}) copy-start(f32[128,128]{1,0:T(8,128)} %mix_weight.3) | copy-start | bytes 196612
  15.2 5.0 %copy-start.13 = (f32[128,128]{1,0:T(8,128)S(1)}, f32[128,128]{1,0:T(8,128)}, u32[]{:S(2)}) copy-start(f32[128,128]{1,0:T(8,128)} %constant.87.clone.z_table) | copy-start | bytes 196612
  15.2 5.0 %collective-permute-start.2 = (f32[136,64]{1,0:T(8,128)S(1)}, f32[136,64]{1,0:T(8,128)S(1)}, u32[]{:S(2)}, u32[]{:S(2)}) collective-permute-start(f32[136,64]{1,0:T(8,128)S(1)} %pad_maximum_fusion), channel_id=1, source_target_pairs={{0,1},{1,2},{2,3},{3,4},{4,5},{5,6},{6,7},{7,0},{8,9},{9,10},{10,1... | collective-permute-start | bytes 104456 | tf_op jit(solution)/shard_map/ppermute | solution.py:535
  16.1 4.1 %copy-start.9 = (s32[12,256]{1,0:T(8,128)S(1)}, s32[12,256]{1,0:T(8,128)}, u32[]{:S(2)}) copy-start(s32[12,256]{1,0:T(8,128)} %codes.5) | copy-start | bytes 36868
  16.1 4.1 %copy-start.12 = (f32[128]{0:T(128)S(1)}, f32[128]{0:T(128)}, u32[]{:S(2)}) copy-start(f32[128]{0:T(128)} %param.31) | copy-start | bytes 1540
  20.2 0.7 copy-start.10
  20.2 0.7 copy-start.11
  20.9 18.1 %copy-start.2 = (f32[128,192]{1,0:T(8,128)S(1)}, f32[128,192]{1,0:T(8,128)}, u32[]{:S(2)}) copy-start(f32[128,192]{1,0:T(8,128)} %constant.88.clone.table) | copy-start | bytes 294916
  30.6 40.5 %copy-start = (f32[640,64]{1,0:T(8,128)S(1)}, f32[640,64]{1,0:T(8,128)}, u32[]{:S(2)}) copy-start(f32[640,64]{1,0:T(8,128)} %constant.90.clone.x_in) | copy-start | bytes 491524
  38.9 32.2 %copy-start.1 = (f32[320,128]{1,0:T(8,128)S(1)}, f32[320,128]{1,0:T(8,128)}, u32[]{:S(2)}) copy-start(f32[320,128]{1,0:T(8,128)} %constant.91.clone.x_out) | copy-start | bytes 491524
  39.8 31.3 %copy-start.4 = (f32[128,128]{1,0:T(8,128)S(1)}, f32[128,128]{1,0:T(8,128)}, u32[]{:S(2)}) copy-start(f32[128,128]{1,0:T(8,128)} %constant.92.clone.x_gain) | copy-start | bytes 196612
  39.8 31.3 %copy-start.5 = (f32[128,128]{1,0:T(8,128)S(1)}, f32[128,128]{1,0:T(8,128)}, u32[]{:S(2)}) copy-start(f32[128,128]{1,0:T(8,128)} %constant.93.clone.x_square) | copy-start | bytes 196612
  39.8 31.3 %all-to-all-start.1 = ((f32[64,2,128]{2,1,0:T(2,128)}), f32[64,2,128]{2,1,0:T(2,128)S(1)}, u32[]{:S(2)}, u32[]{:S(2)}) async-start(f32[64,2,128]{2,1,0:T(2,128)} %shard_map.186), calls=%async_computation.1 | async-start | bytes 131072 | tf_op jit(solution)/shard_map/all_to_all | solution.py:574
  72.9 19.2 %copy-start.3 = (f32[192,128]{1,0:T(8,128)S(1)}, f32[192,128]{1,0:T(8,128)}, u32[]{:S(2)}) copy-start(f32[192,128]{1,0:T(8,128)} %constant.89.clone.table) | copy-start | bytes 294916
  93.0 17.7 %all-to-all-start.3 = ((f32[8,24,128]{2,1,0:T(8,128)}), f32[8,24,128]{2,1,0:T(8,128)S(1)}, u32[]{:S(2)}, u32[]{:S(2)}) async-start(f32[8,24,128]{2,1,0:T(8,128)} %shard_map.188), calls=%async_computation.3 | async-start | bytes 196608 | tf_op jit(solution)/shard_map/all_to_all | solution.py:591
  96.6 14.1 %copy-start.6 = (f32[3,256]{1,0:T(4,128)S(1)}, f32[3,256]{1,0:T(4,128)}, u32[]{:S(2)}) copy-start(f32[3,256]{1,0:T(4,128)} %positions.1) | copy-start | bytes 9220
  113.4 4.0 %collective-permute-start.4 = (f32[3,64]{1,0:T(4,128)S(1)}, f32[3,64]{1,0:T(4,128)S(1)}, u32[]{:S(2)}, u32[]{:S(2)}) collective-permute-start(f32[3,64]{1,0:T(4,128)S(1)} %get-tuple-element.45), channel_id=1, source_target_pairs={{0,7},{1,0},{2,1},{3,2},{4,3},{5,4},{6,5},{7,6},{8,15},{9,8},{10,9... | collective-permute-start | bytes 2312 | tf_op jit(solution)/shard_map/ppermute | solution.py:535
  116.2 4.2 %collective-permute-start.5 = (f32[3,64]{1,0:T(4,128)S(1)}, f32[3,64]{1,0:T(4,128)S(1)}, u32[]{:S(2)}, u32[]{:S(2)}) collective-permute-start(f32[3,64]{1,0:T(4,128)S(1)} %get-tuple-element.44), channel_id=1, source_target_pairs={{0,1},{1,2},{2,3},{3,4},{4,5},{5,6},{6,7},{7,0},{8,9},{9,10},{10,1... | collective-permute-start | bytes 2312 | tf_op jit(solution)/shard_map/ppermute | solution.py:535
  120.7 6.7 %collective-permute-start.6 = (f32[3,128]{1,0:T(4,128)S(1)}, f32[3,128]{1,0:T(4,128)S(1)}, u32[]{:S(2)}, u32[]{:S(2)}) collective-permute-start(f32[3,128]{1,0:T(4,128)S(1)} %bitcast.28), channel_id=1, source_target_pairs={{0,8},{8,16},{16,24},{24,32},{32,40},{40,48},{48,56},{56,64},{64,7... | collective-permute-start | bytes 4616 | tf_op jit(solution)/shard_map/ppermute | solution.py:535
  125.4 7.6 %collective-permute-start.7 = (f32[3,128]{1,0:T(4,128)S(1)}, f32[3,128]{1,0:T(4,128)S(1)}, u32[]{:S(2)}, u32[]{:S(2)}) collective-permute-start(f32[3,128]{1,0:T(4,128)S(1)} %bitcast.27), channel_id=1, source_target_pairs={{0,504},{8,0},{16,8},{24,16},{32,24},{40,32},{48,40},{56,48},{64,5... | collective-permute-start | bytes 4616 | tf_op jit(solution)/shard_map/ppermute | solution.py:535

commit v2 on v1

v2 whole, which is shorter than its diff:
```python
import functools
import math

import jax
import jax.numpy as jnp
import ml_dtypes
import numpy as np
from jax import lax
from jax.experimental import pallas as pl
from jax.experimental.pallas import tpu as pltpu
from jax.sharding import PartitionSpec as P

NZ = 128
N_GX = 64
N_GY = 8
K = 12
HALF = K // 2
C = 128
RH = 64
NB = 8
ATOMS_ALL = 131072
ATOM = 256
EXT = 640
CUTOFF = 20.0
BETA = 0.5

PLANE0 = -2
PLANES = 7
OWN_PLANES = range(1, 6)
ROW0 = -3
ROWS = 23
ROW_PAD = 24
SUM_ROW = 23
SUM_LANE = 16 * PLANES

highest = lax.Precision.HIGHEST
f32 = jnp.float32
bf16 = jnp.bfloat16


def real_basis(n):
    cell = np.arange(n)
    rows = [np.full(n, 1.0 / math.sqrt(n))]
    freq = [0]
    for m in range(1, n // 2):
        angle = 2.0 * math.pi / n * (m * cell % n)
        rows += [math.sqrt(2.0 / n) * np.cos(angle), math.sqrt(2.0 / n) * np.sin(angle)]
        freq += [m, m]
    rows.append(np.where(cell % 2 == 0, 1.0, -1.0) / math.sqrt(n))
    freq.append(n // 2)
    return np.stack(rows), np.array(freq)


def tables():
    basis, freq = real_basis(NZ)
    wave = 2.0 * math.pi / NZ * freq
    square = wave * wave
    gain = np.exp(-square / (4.0 * BETA**2)) * (6.0 / (4.0 + 2.0 * np.cos(wave))) ** 2

    plane = (2 * np.arange(N_GX)[None, :] + PLANE0 + np.arange(PLANES)[:, None]) % NZ
    x_in = np.concatenate([basis[:, plane[p]] for p in OWN_PLANES], axis=0)
    x_out = np.concatenate([basis[:, plane[p]].T for p in range(PLANES)], axis=0)

    y_in = np.zeros((NZ, N_GY * ROW_PAD))
    for j in range(N_GY):
        for r in range(ROWS):
            y_in[:, j * ROW_PAD + r] = basis[:, (16 * j + ROW0 + r) % NZ]
        y_in[:, j * ROW_PAD + SUM_ROW] = 1.0

    x_side = np.zeros((NZ, NZ, 2))
    x_side[:, :, 0] = 4.0 * math.pi * gain[:, None]
    x_side[:, :, 1] = square[:, None]

    yz = np.zeros((N_GX * N_GY, 4, 128))
    for i in range(N_GX):
        for j in range(N_GY):
            z = slice(16 * j, 16 * j + 16)
            for half in range(2):
                y = i + 64 * half
                yz[i * N_GY + j, 2 * half, :16] = gain[y] * gain[z]
                yz[i * N_GY + j, 2 * half + 1, :16] = square[y] + square[z]
    as32 = lambda a: np.ascontiguousarray(a, dtype=np.float32)

    def split(a):
        high = as32(a).astype(ml_dtypes.bfloat16)
        low = (as32(a) - high.astype(np.float32)).astype(ml_dtypes.bfloat16)
        return np.concatenate([high, high, low], axis=1)

    return {
        "z": as32(basis),
        "y_in": split(y_in),
        "y_out": split(y_in.T),
        "x_in": split(x_in),
        "x_out": split(x_out),
        "x_gain": as32(x_side[:, :, 0]),
        "x_square": as32(x_side[:, :, 1]),
        "yz": as32(yz),
    }


TABLES = tables()


def dot(a, b, precision=None):
    return jnp.dot(a, b, precision=precision, preferred_element_type=f32)


def dot_nt(a, b, precision=None):
    return lax.dot_general(
        a, b, (((1,), (1,)), ((), ())), precision=precision, preferred_element_type=f32
    )


def halves(x):
    high = x.astype(bf16).astype(f32)
    return high, x - high


def layered(wide, x):
    high, low = halves(x)
    return dot(wide[...], jnp.concatenate([high, low, high], axis=0).astype(bf16))


def spread_out(value, lane):
    high, rest = halves(jnp.full(lane.shape, value, f32))
    mid, low = halves(rest)
    return jnp.where(
        lane == SUM_LANE,
        high,
        jnp.where(lane == SUM_LANE + 1, mid, jnp.where(lane == SUM_LANE + 2, low, 0.0)),
    )


def spline(f):
    g = 1.0 - f
    f2 = f * f
    f3 = f2 * f
    weights = [
        g * g * g / 6.0,
        (3.0 * f3 - 6.0 * f2 + 4.0) / 6.0,
        (-3.0 * f3 + 3.0 * f2 + 3.0 * f + 1.0) / 6.0,
        f3 / 6.0,
    ]
    slopes = [-0.5 * g * g, 1.5 * f2 - 2.0 * f, -1.5 * f2 + f + 0.5, 0.5 * f2]
    return weights, slopes


def spline_rows(u, first, rows, periodic):
    floor = jnp.floor(u)
    base = floor.astype(jnp.int32)
    weights, slopes = spline(u - floor)
    cell = lax.broadcasted_iota(jnp.int32, (rows, u.shape[1]), 0) + first
    table = jnp.zeros((rows, u.shape[1]), f32)
    slope_table = jnp.zeros((rows, u.shape[1]), f32)
    for step in range(4):
        target = base + (step - 1)
        if periodic:
            target = target & (rows - 1)
        hit = cell == target
        table = jnp.where(hit, weights[step], table)
        slope_table = jnp.where(hit, slopes[step], slope_table)
    return table, slope_table


def offsets(codes):
    e = codes + (codes >= 13).astype(jnp.int32)
    nine = (e >= 9).astype(jnp.int32) + (e >= 18).astype(jnp.int32)
    rest = e - 9 * nine
    three = (rest >= 3).astype(jnp.int32) + (rest >= 6).astype(jnp.int32)
    return nine, three, rest - 3 * three - 1


def own_targets(codes):
    nine, three, step_z = offsets(codes)
    n = lax.broadcasted_iota(jnp.int32, codes.shape, 1)
    inner = n < 512
    plane = jnp.where(inner, n >> 7, (n >> 4) & 3) + nine - 2
    row = jnp.where(inner, (n >> 4) & 7, jnp.where(n < 576, -1, 8)) + three - 1
    z = ((n & 15) + step_z) & 15
    here = (plane >= 0) & (plane <= 1) & (row >= 0) & (row <= 7)
    return jnp.where(here, plane * 128 + row * 16 + z, -1)


def edge_targets(codes):
    nine, three, step_z = offsets(codes)
    n = lax.broadcasted_iota(jnp.int32, codes.shape, 1)
    plane = (n >> 7) + nine
    row = ((n >> 4) & 7) + three - 1
    z = (n & 15) + step_z
    wrap = (z >= 16).astype(jnp.int32) - (z < 0).astype(jnp.int32)
    z = z - 16 * wrap
    target = jnp.where(
        row < 0,
        512 + plane * 16 + z,
        jnp.where(row > 7, 576 + plane * 16 + z, plane * 128 + row * 16 + z),
    )
    return target, wrap


def one_hot(target_ref, k, columns):
    lanes = target_ref.shape[1]
    row = jnp.broadcast_to(target_ref[k : k + 1, :], (columns, lanes))
    column = lax.broadcasted_iota(jnp.int32, (columns, lanes), 0)
    return jnp.where(column == row, 1.0, 0.0).astype(bf16)


def beside(x):
    high, low = halves(x)
    return jnp.concatenate([high, high, low], axis=1).astype(bf16)


def prepare_kernel(
    own, coupling, mix_weight, readout, charge_weight, up_weight, radial_in, radial_out, z_table,
    waves_out, columns_out, up_wide, in_wide, out_wide, rows,
):
    weights_z, _ = spline_rows(own[C + 2 : C + 3, :], 0, NZ, True)
    waves_out[...] = beside(dot(z_table[...], weights_z, highest))

    rows[...] = jnp.zeros_like(rows)
    rows[0:1, :] = readout[...]
    rows[1:2, :] = charge_weight[...]
    mixed = dot(rows[...], mix_weight[...], highest) * (1.0 / K)
    for w, direct in enumerate((readout, charge_weight)):
        row = mixed[w : w + 1]
        rows[4 * w : 4 * w + 1, :] = row
        rows[4 * w + 1 : 4 * w + 2, :] = row * coupling[0:1, :] * (1.0 / K)
        rows[4 * w + 2 : 4 * w + 3, :] = row * coupling[1:2, :] * (1.0 / K)
        rows[4 * w + 3 : 4 * w + 4, :] = direct[...]
    standing = rows[...].T
    for i in range(8):
        columns_out[i] = jnp.broadcast_to(standing[:, i : i + 1], (C, 128))
    rows[0:2, :] = coupling[...] * (2.0 / K)
    standing = rows[...].T
    for i in range(2):
        columns_out[8 + i] = jnp.broadcast_to(standing[:, i : i + 1], (C, 128))

    up_wide[...] = beside(up_weight[...])
    out_wide[...] = beside(radial_out[...].T)
    inner = radial_in[...].T
    column = lax.broadcasted_iota(jnp.int32, (NB, 8 * NB), 1)
    wave = lax.broadcasted_iota(jnp.int32, (NB, 8 * NB), 0)
    picks = [jnp.where(column == 8 * wave + k, 1.0, 0.0) for k in range(HALF)]
    in_wide[...] = beside(jnp.concatenate([dot(inner, p, highest) for p in picks], axis=0))


def slot(k):
    return 8 * (k // HALF) + k % HALF


def geometry(rel_x, rel_y, rel_z, harm, basis, basis_slope):
    square = rel_x * rel_x + rel_y * rel_y + rel_z * rel_z
    dist = jnp.sqrt(square)
    inv = 1.0 / dist
    ux, uy, uz = rel_x * inv, rel_y * inv, rel_z * inv
    r3, r5, r15 = math.sqrt(3.0), math.sqrt(5.0), math.sqrt(15.0)
    harmonic = [
        r3 * ux,
        r3 * uy,
        r3 * uz,
        r15 * ux * uy,
        r15 * uy * uz,
        0.5 * r5 * (3.0 * uz * uz - 1.0),
        r15 * ux * uz,
        0.5 * r15 * (ux * ux - uy * uy),
    ]
    for m in range(8):
        harm[m] = harmonic[m]

    t = dist * (1.0 / CUTOFF)
    t2 = t * t
    t4 = t2 * t2
    t5 = t4 * t
    t6 = t4 * t2
    envelope = 1.0 - t6 * (28.0 - t * (48.0 - 21.0 * t))
    theta = math.pi * t
    sines, cosines = {1: jnp.sin(theta)}, {1: jnp.cos(theta)}
    for b in range(2, NB + 1):
        i, j = (b + 1) // 2, b // 2
        sines[b] = sines[i] * cosines[j] + cosines[i] * sines[j]
        cosines[b] = cosines[i] * cosines[j] - sines[i] * sines[j]
    scale = math.sqrt(2.0 / CUTOFF)
    shape = scale * envelope * inv
    if basis_slope is not None:
        envelope_slope = (-168.0 / CUTOFF) * t5 * (1.0 - t) * (1.0 - t)
        shape_slope = scale * inv * (envelope_slope - envelope * inv)
    for b in range(1, NB + 1):
        value = sines[b] * shape
        for half in range(value.shape[0] // 8):
            basis[half, 8 * b - 8 : 8 * b, :] = value[8 * half : 8 * half + 8]
        if basis_slope is not None:
            basis_slope[8 * b - 8 : 8 * b, :] = (
                (b * math.pi / CUTOFF) * cosines[b] * shape + sines[b] * shape_slope
            )
    return inv, ux, uy, uz


CHARGE_SCRATCH = [
    pltpu.VMEM((136, EXT), f32),
    pltpu.VMEM((288, EXT), bf16),
    pltpu.VMEM((16, ATOM), jnp.int32),
    pltpu.VMEM((2, 8 * NB, ATOM), f32),
    pltpu.VMEM((8, 16, ATOM), f32),
    pltpu.VMEM((K, 3 * C, ATOM), f32),
    pltpu.VMEM((K, C, ATOM), f32),
    pltpu.SemaphoreType.DMA((1,)),
]


def charges_kernel(
    left, own, right, low, high, codes, up_wide, in_wide, out_wide, columns, waves_z,
    spread, charge_out, rel, places_out, along, kept,
    table, split, target_ref, basis, harm, radial, up, sems,
):
    own_pos = own[C : C + 8, :]
    weights_x, _ = spline_rows(own_pos[0:1], PLANE0, 8, False)
    weights_y, _ = spline_rows(own_pos[1:2], ROW0, ROW_PAD, False)

    table[:, 0:128] = left[...]
    table[:, 128:384] = own[...]
    table[:, 384:512] = right[...]
    table[:, 512:576] = low[...]
    table[:, 576:640] = high[...]

    mapped = layered(up_wide, table[0:C, :])
    m_high, m_low = halves(mapped)
    split[0:C, :] = m_high.astype(bf16)
    split[C : 2 * C, :] = m_low.astype(bf16)

    lane = lax.broadcasted_iota(jnp.int32, (8, EXT), 1)
    part = lax.broadcasted_iota(jnp.int32, (8, EXT), 0)
    plane = jnp.where(lane < 512, lane >> 7, (lane >> 4) & 3)
    shift_x = jnp.where(plane == 0, -2.0, jnp.where(plane == 3, 2.0, 0.0))
    shift_y = jnp.where(lane >= 576, 16.0, jnp.where(lane >= 512, -16.0, 0.0))
    places = table[C : C + 8, :] + jnp.where(
        part == 0, shift_x, jnp.where(part == 1, shift_y, 0.0)
    )
    places_out[...] = places
    p_high, p_rest = halves(places)
    p_mid, p_low = halves(p_rest)
    split[2 * C : 2 * C + 32, :] = jnp.concatenate(
        [p_high, p_mid, p_low, jnp.zeros_like(p_low)], axis=0
    ).astype(bf16)

    padded = jnp.concatenate(
        [codes[0:HALF, :], codes[0:2, :], codes[HALF:K, :], codes[0:2, :]], axis=0
    )
    target, wrap = edge_targets(padded)
    target_ref[...] = target
    for k in range(K):
        found = dot(split[...], one_hot(target_ref, slot(k), EXT))
        up[k] = found[0:C] + found[C : 2 * C]
        place = found[256:264] + found[264:272] + found[272:280]
        for c in range(3):
            rel[c, slot(k) : slot(k) + 1, :] = place[c : c + 1]

    keep_up = pltpu.make_async_copy(up, kept, sems.at[0])
    keep_up.start()

    rel_x = rel[0] - own_pos[0:1]
    rel_y = rel[1] - own_pos[1:2]
    rel_z = rel[2] - own_pos[2:3] + wrap.astype(f32) * float(NZ)
    spare = (lax.broadcasted_iota(jnp.int32, (16, ATOM), 0) & 7) >= HALF
    rel_x, rel_y, rel_z = (jnp.where(spare, 1.0, x) for x in (rel_x, rel_y, rel_z))
    rel[0], rel[1], rel[2] = rel_x, rel_y, rel_z
    geometry(rel_x, rel_y, rel_z, harm, basis, None)

    for half in range(2):
        before = layered(in_wide, basis[half])
        hidden = before * jax.nn.sigmoid(before)
        for k in range(HALF):
            radial[HALF * half + k] = layered(out_wide, hidden[RH * k : RH * k + RH])

    charge = []
    site = jnp.zeros((8, 128), f32)
    for half in range(2):
        lanes = slice(128 * half, 128 * half + 128)

        def accumulate(step, carry):
            c0 = pl.multiple_of(step * 8, 8)
            block = pl.ds(c0, 8)
            total = [jnp.zeros((8, 128), f32) for _ in range(9)]
            for k in range(K):
                u = up[k, block, lanes]
                total[0] += radial[k, block, lanes] * u
                first = radial[k, pl.ds(c0 + C, 8), lanes] * u
                second = radial[k, pl.ds(c0 + 2 * C, 8), lanes] * u
                for m in range(8):
                    total[1 + m] += (
                        first if m < 3 else second
                    ) * harm[m, slot(k) : slot(k) + 1, lanes]
            for m in range(8):
                along[m, block, lanes] = total[1 + m] * columns[8 if m < 3 else 9, block, :]
            first = sum(total[m] * total[m] for m in range(1, 4))
            second = sum(total[m] * total[m] for m in range(4, 9))
            feature = own[block, lanes]
            return tuple(
                carry[w]
                + columns[4 * w, block, :] * total[0]
                + columns[4 * w + 1, block, :] * first
                + columns[4 * w + 2, block, :] * second
                + columns[4 * w + 3, block, :] * feature
                for w in range(2)
            )

        zero = jnp.zeros((8, 128), f32)
        sites, charges = lax.fori_loop(0, 16, accumulate, (zero, zero))
        site = site + sites
        charge.append(jnp.sum(charges, axis=0, keepdims=True))
    charge = jnp.concatenate(charge, axis=1)
    charge_out[...] = charge

    charged = weights_y * charge
    planes = jnp.concatenate([charged * weights_x[p : p + 1] for p in OWN_PLANES], axis=0)
    top, rest = halves(planes)
    planes = dot_nt(jnp.concatenate([top, rest, top], axis=1).astype(bf16), waves_z[...])
    lane = lax.broadcasted_iota(jnp.int32, (ROW_PAD, 128), 1)
    row = lax.broadcasted_iota(jnp.int32, (ROW_PAD, 128), 0)
    extra = jnp.where(row == SUM_ROW, spread_out(jnp.sum(site), lane), 0.0)
    for g in range(N_GY):
        part = extra
        for i, p in enumerate(OWN_PLANES):
            amount = (16 * (p - g)) % 128
            moved = planes[ROW_PAD * i : ROW_PAD * i + ROW_PAD]
            moved = pltpu.roll(moved, amount, 1) if amount else moved
            part = jnp.where((lane >> 4) == p, moved, part)
        spread[g] = part
    keep_up.wait()


def y_in_kernel(rows, table, out):
    waves = layered(table, rows[...].reshape(N_GY * ROW_PAD, 128))
    out[:, 0, :] = waves[0:64]
    out[:, 1, :] = waves[64:128]


def x_kernel(planes, x_in, x_out, x_gain, x_square, yz, out):
    sides = jnp.concatenate([planes[:, 0, :], planes[:, 1, :]], axis=1)
    site = jnp.sum(planes[:, 0, SUM_LANE : SUM_LANE + 3])
    waves = layered(x_in, sides)
    filtered = []
    energy = site * (1.0 / (N_GX * N_GY))
    for half in range(2):
        total = jnp.zeros((128, 128), f32)
        for i, p in enumerate(OWN_PLANES):
            block = waves[128 * i : 128 * i + 128, 128 * half : 128 * half + 128]
            total = total + pltpu.roll(block, (128 - 16 * p) % 128, 1)
        square = x_square[...] + yz[0, 2 * half + 1 : 2 * half + 2, :]
        anchor = square == 0.0
        kernel = jnp.where(
            anchor,
            0.0,
            x_gain[...] * yz[0, 2 * half : 2 * half + 1, :] / jnp.where(anchor, 1.0, square),
        )
        shaped = kernel * total
        energy = energy + 0.5 * jnp.sum(shaped * total)
        filtered.append(shaped)
    back = layered(x_out, jnp.concatenate(filtered, axis=1))
    lane = lax.broadcasted_iota(jnp.int32, (64, 128), 1)
    for half in range(2):
        total = spread_out(energy, lane) if half == 0 else jnp.zeros((64, 128), f32)
        for p in range(PLANES):
            block = back[64 * p : 64 * p + 64, 128 * half : 128 * half + 128]
            moved = pltpu.roll(block, 16 * p, 1) if p else block
            total = total + moved
        out[:, half, :] = total


def y_out_kernel(waves, table, out):
    both = jnp.concatenate([waves[:, 0, :], waves[:, 1, :]], axis=0)
    out[...] = layered(table, both).reshape(N_GY, ROW_PAD, 128)


SLOPE_SCRATCH = [
    pltpu.VMEM((1, 8 * NB, ATOM), f32),
    pltpu.VMEM((8 * NB, ATOM), f32),
    pltpu.VMEM((8, 8, ATOM), f32),
    pltpu.VMEM((HALF, 3 * C, ATOM), f32),
    pltpu.VMEM((HALF, 3 * C, ATOM), f32),
    pltpu.VMEM((HALF, 24, ATOM), f32),
    pltpu.VMEM((HALF, C, ATOM), f32),
    pltpu.SemaphoreType.DMA((1,)),
]


def slopes_kernel(
    k0, rel, kept, along, codes, in_wide, out_wide, columns, pulls,
    basis, basis_slope, harm, radial, radial_slope, gathered, up, sems,
):
    fetch_up = pltpu.make_async_copy(kept.at[k0 : k0 + HALF], up, sems.at[0])
    fetch_up.start()
    first = slot(k0)
    inv, ux, uy, uz = geometry(
        *(rel[c, first : first + 8, :] for c in range(3)), harm, basis, basis_slope
    )
    before = layered(in_wide, basis[0])
    before_slope = layered(in_wide, basis_slope[...])
    gate = jax.nn.sigmoid(before)
    hidden = before * gate
    hidden_slope = gate * (1.0 + before * (1.0 - gate)) * before_slope
    for k in range(HALF):
        radial[k] = layered(out_wide, hidden[RH * k : RH * k + RH])
        radial_slope[k] = layered(out_wide, hidden_slope[RH * k : RH * k + RH])

    fetch_up.wait()
    for half in range(2):
        spots = slice(128 * half, 128 * half + 128)

        for k in range(HALF):
            total = [jnp.zeros((8, 128), f32) for _ in range(18)]
            shapes = [
                jnp.broadcast_to(harm[m, k : k + 1, spots], (8, 128)) for m in range(8)
            ]
            for block in range(16):
                c0 = 8 * block
                rows = [slice(c0 + C * i, c0 + C * i + 8) for i in range(3)]
                u = up[k, rows[0], spots]
                turn = [along[m, rows[0], spots] for m in range(8)]
                turn_1 = sum(turn[m] * shapes[m] for m in range(3))
                turn_2 = sum(turn[m] * shapes[m] for m in range(3, 8))
                stretch = u * (
                    radial_slope[k, rows[0], spots]
                    + radial_slope[k, rows[1], spots] * turn_1
                    + radial_slope[k, rows[2], spots] * turn_2
                )
                first = radial[k, rows[1], spots] * u
                second = radial[k, rows[2], spots] * u
                for w in range(2):
                    weight = columns[4 * w, rows[0], :]
                    total[9 * w] += weight * stretch
                    first_w = weight * first
                    second_w = weight * second
                    for m in range(8):
                        total[9 * w + 1 + m] += (first_w if m < 3 else second_w) * turn[m]
            sums = [jnp.sum(total[i], axis=0, keepdims=True) for i in range(18)]
            gathered[k, :, spots] = jnp.concatenate(sums + [jnp.zeros((6, 128), f32)], axis=0)

    r3, r5, r15 = math.sqrt(3.0), math.sqrt(5.0), math.sqrt(15.0)
    for w in range(2):
        g = [
            jnp.concatenate(
                [gathered[k, i : i + 1, :] for k in range(HALF)] + [jnp.zeros((2, ATOM), f32)],
                axis=0,
            )
            for i in range(9 * w, 9 * w + 9)
        ]
        vx = r3 * g[1] + r15 * (uy * g[4] + uz * g[7] + ux * g[8])
        vy = r3 * g[2] + r15 * (ux * g[4] + uz * g[5] - uy * g[8])
        vz = r3 * g[3] + r15 * (uy * g[5] + ux * g[7]) + (3.0 * r5) * uz * g[6]
        radial_part = g[0] - (vx * ux + vy * uy + vz * uz) * inv
        for c, (v, along_c) in enumerate(((vx, ux), (vy, uy), (vz, uz))):
            first = 8 * (3 * w + c)
            pulls[first : first + HALF, :] = (radial_part * along_c + v * inv)[0:HALF]
            spare = codes[k0 + 2 * c : k0 + 2 * c + 2, :].astype(f32)
            pulls[first + HALF : first + 8, :] = spare if w == 0 else jnp.zeros_like(spare)


def reach_kernel(pulls_0, pulls_1, places, z_table, out, lower, upper):
    weights, slopes = spline_rows(places[2:3, :], 0, NZ, True)
    both = jnp.concatenate([weights, slopes[:, 128:384]], axis=1)
    out[...] = dot(z_table[...], both, highest)
    for half, pulls in enumerate((pulls_0, pulls_1)):
        rows = slice(48 * half, 48 * half + 48)
        lower[rows, :] = pulls[:, 0:128]
        upper[rows, :] = pulls[:, 128:256]


def final_kernel(
    potential, places, charge, waves, left, lower, upper, right, low, high, forces, energy_out,
    pulls, target_ref,
):
    pulls[:, 0:128] = left[...]
    pulls[:, 128:256] = lower[...]
    pulls[:, 256:384] = upper[...]
    pulls[:, 384:512] = right[...]
    pulls[:, 512:576] = low[...]
    pulls[:, 576:640] = high[...]
    codes = [
        pulls[48 * half + 8 * c + HALF : 48 * half + 8 * c + 8, :]
        for half in range(2)
        for c in range(3)
    ]
    codes = jnp.concatenate(codes, axis=0)
    target_ref[...] = own_targets(codes.astype(jnp.int32))

    mine = slice(128, 384)
    weights_x, slopes_x = spline_rows(places[0:1, :], PLANE0, 8, False)
    weights_y, slopes_y = spline_rows(places[1:2, :], ROW0, ROW_PAD, False)
    lane = lax.broadcasted_iota(jnp.int32, (ROW_PAD, 128), 1)
    energy = jnp.zeros((1, 3), f32)
    for g in range(N_GY):
        energy = energy + potential[g, SUM_ROW : SUM_ROW + 1, SUM_LANE : SUM_LANE + 3]
    energy_out[...] = jnp.sum(energy, axis=1, keepdims=True) * (1.0 / ATOMS_ALL)
    planes = []
    for p in range(PLANES):
        plane = jnp.zeros((ROW_PAD, 128), f32)
        for g in range(N_GY):
            amount = (16 * (g - p)) % 128
            moved = pltpu.roll(potential[g], amount, 1) if amount else potential[g]
            plane = jnp.where((lane >> 4) == g, moved, plane)
        planes.append(plane)
    felt = dot(jnp.concatenate(planes, axis=0), waves[...], highest)
    phi = jnp.zeros((1, EXT), f32)
    slope = [jnp.zeros((1, ATOM), f32)] * 3
    for p in range(PLANES):
        here = felt[ROW_PAD * p : ROW_PAD * p + ROW_PAD, 0:EXT]
        by_y = jnp.sum(here * weights_y, axis=0, keepdims=True)
        phi = phi + by_y * weights_x[p : p + 1]
        slope[0] = slope[0] + by_y[:, mine] * slopes_x[p : p + 1, mine]
        by_y = jnp.sum(here[:, mine] * slopes_y[:, mine], axis=0, keepdims=True)
        slope[1] = slope[1] + by_y * weights_x[p : p + 1, mine]
        here = felt[ROW_PAD * p : ROW_PAD * p + ROW_PAD, EXT:]
        by_y = jnp.sum(here * weights_y[:, mine], axis=0, keepdims=True)
        slope[2] = slope[2] + by_y * weights_x[p : p + 1, mine]

    total = [
        [
            pulls[i + 8 * c : i + 8 * c + 8, :] + phi * pulls[i + 24 + 8 * c : i + 32 + 8 * c, :]
            for c in range(3)
        ]
        for i in (0, 48)
    ]
    table = jnp.zeros((16, ATOM), f32)
    for k in range(K):
        rows = jnp.concatenate(
            [total[k // HALF][c][k % HALF : k % HALF + 1, :] for c in range(3)]
            + [jnp.zeros((5, EXT), f32)],
            axis=0,
        )
        top, rest = halves(rows)
        both = jnp.concatenate([top, rest], axis=0).astype(bf16)
        table = table + dot_nt(both, one_hot(target_ref, k, ATOM))
    for c in range(3):
        forces[c : c + 1, :] = (
            jnp.sum(total[0][c][0:HALF, mine] + total[1][c][0:HALF, mine], axis=0, keepdims=True)
            - table[c : c + 1]
            - table[8 + c : 9 + c]
            - charge[...] * slope[c]
        )


def call(kernel, outs, scratch, flops, *args, far_in=(), far_out=(), mib=8):
    args = [
        pltpu.with_memory_space_constraint(x, pltpu.HBM) if i in far_in else x
        for i, x in enumerate(args)
    ]
    near, far = pl.BlockSpec(memory_space=pltpu.VMEM), pl.BlockSpec(memory_space=pltpu.HBM)
    out_specs = near
    if isinstance(outs, tuple):
        out_specs = tuple(far if i in far_out else near for i in range(len(outs)))
    return pl.pallas_call(
        kernel,
        out_shape=outs,
        in_specs=[far if i in far_in else near for i in range(len(args))],
        out_specs=out_specs,
        scratch_shapes=scratch,
        compiler_params=pltpu.CompilerParams(vmem_limit_bytes=mib * 1024 * 1024),
        cost_estimate=pl.CostEstimate(flops=flops, bytes_accessed=2000000, transcendentals=0),
    )(*args)


def passed_along(array, axis, by):
    devices = lax.axis_size(axis)
    return lax.ppermute(array, axis, [(i, (i + by) % devices) for i in range(devices)])


def ghosts(lower, upper):
    left = passed_along(upper, "gx", 1)
    right = passed_along(lower, "gx", -1)
    planes = (left, lower, upper, right)
    low = passed_along(jnp.concatenate([x[:, 112:] for x in planes], axis=1), "gy", 1)
    high = passed_along(jnp.concatenate([x[:, :16] for x in planes], axis=1), "gy", -1)
    return left, right, low, high


def struct(*shape, dtype=f32):
    return jax.ShapeDtypeStruct(shape, dtype)


def shards(
    positions, features, neighbours, up_weight, radial_in, radial_out, coupling, mix_weight,
    readout, charge_weight,
):
    table = {name: jnp.asarray(value) for name, value in TABLES.items()}
    own = jnp.concatenate([features, positions, jnp.zeros((5, ATOM), f32)], axis=0)
    left, right, low, high = ghosts(own[:, 0:128], own[:, 128:256])
    waves_z, columns, up_wide, in_wide, out_wide = call(
        prepare_kernel,
        (
            struct(NZ, 3 * ATOM, dtype=bf16),
            struct(10, C, 128),
            struct(C, 3 * C, dtype=bf16),
            struct(HALF * RH, 24 * NB, dtype=bf16),
            struct(3 * C, 3 * RH, dtype=bf16),
        ),
        [pltpu.VMEM((8, C), f32)],
        10**8,
        own,
        coupling,
        mix_weight,
        readout.reshape(1, C),
        charge_weight.reshape(1, C),
        up_weight,
        radial_in.T,
        radial_out.T,
        table["z"],
    )
    device = lax.axis_index("gx") * N_GY + lax.axis_index("gy")
    yz = lax.dynamic_slice(table["yz"], (device, 0, 0), (1, 4, 128))

    spread, charge, rel, places, along, kept = call(
        charges_kernel,
        (
            struct(N_GY, ROW_PAD, 128),
            struct(1, ATOM),
            struct(3, 16, ATOM),
            struct(8, EXT),
            struct(8, C, ATOM),
            pltpu.HBM((K, C, ATOM), f32),
        ),
        CHARGE_SCRATCH,
        10**9,
        left,
        own,
        right,
        low,
        high,
        neighbours,
        up_wide,
        in_wide,
        out_wide,
        columns,
        waves_z,
        far_out=(5,),
        mib=28,
    )
    spread, yz = lax.optimization_barrier((spread, yz))

    def pulls_of(k0, kept):
        return call(
            functools.partial(slopes_kernel, k0),
            struct(48, ATOM),
            SLOPE_SCRATCH,
            2 * 10**9,
            rel,
            kept,
            along,
            neighbours,
            in_wide,
            out_wide,
            columns,
            far_in=(1,),
            mib=28,
        )

    rows = lax.all_to_all(spread, "gy", split_axis=0, concat_axis=0, tiled=True)
    pulls_0 = pulls_of(0, kept)
    rows, pulls_0 = lax.optimization_barrier((rows, pulls_0))
    waves = call(y_in_kernel, struct(N_GX, 2, 128), [], 10**7, rows, table["y_in"])
    waves, kept = lax.optimization_barrier((waves, kept))
    planes = lax.all_to_all(waves, "gx", split_axis=0, concat_axis=0, tiled=True)
    pulls_1 = pulls_of(HALF, kept)
    planes, pulls_1 = lax.optimization_barrier((planes, pulls_1))
    waves = call(
        x_kernel,
        struct(N_GX, 2, 128),
        [],
        10**7,
        planes,
        table["x_in"],
        table["x_out"],
        table["x_gain"],
        table["x_square"],
        yz,
    )
    waves, pulls_0, pulls_1 = lax.optimization_barrier((waves, pulls_0, pulls_1))
    reach, lower, upper = call(
        reach_kernel,
        (struct(NZ, EXT + ATOM), struct(96, 128), struct(96, 128)),
        [],
        10**9,
        pulls_0,
        pulls_1,
        places,
        table["z"],
    )
    waves = lax.all_to_all(waves, "gx", split_axis=0, concat_axis=0, tiled=True)
    left, right, low, high = ghosts(lower, upper)
    rows = call(y_out_kernel, struct(N_GY, ROW_PAD, 128), [], 10**7, waves, table["y_out"])
    potential = lax.all_to_all(rows, "gy", split_axis=0, concat_axis=0, tiled=True)
    forces, energy = call(
        final_kernel,
        (struct(3, ATOM), struct(1, 1)),
        [pltpu.VMEM((96, EXT), f32), pltpu.VMEM((K, EXT), jnp.int32)],
        10**9,
        potential,
        places,
        charge,
        reach,
        left,
        lower,
        upper,
        right,
        low,
        high,
    )
    return (forces, energy.reshape(()))


def solution(mesh):
    placed = (P(None, ("gx", "gy")),) * 3 + (P(),) * 7
    return jax.shard_map(
        shards, mesh=mesh, in_specs=placed, out_specs=(P(None, ("gx", "gy")), P()), check_vma=False
    )
```

time: 134 us -> 115 us (0.86)
  the two profiles are of different devices: /device:TPU:6 before, /device:TPU:1 now
where the time goes in v2:
time: 115 us; the launch traced here: 114 us
  starting transfers between devices  62.7 us (55%)
  waiting for transfers between devices  27.3 us (24%)
  Pallas kernels  20.1 us (17%)
  other arithmetic  1.51 us (1%)
  local copies, waits for them, and re-layouts  1.34 us (1%)
    ppermute x8, starting transfers between devices, passed_along(): lax.ppermute(array, axis, [(i, (i + by) % devices) for i in range(devices)])  31.9 us
    pallas_call x9, Pallas kernels, call(): pl.pallas_call(kernel, out_shape=outs, in_specs=[far if i in far_in else...  20.1 us
    all_to_all x1, starting transfers between devices, shards(): lax.all_to_all(waves, 'gx', split_axis=0, concat_axis=0, tiled=True)  12.1 us
    all_to_all x1, waiting for transfers between devices, shards(): waves = lax.all_to_all(waves, 'gx', split_axis=0, concat_axis=0, tiled=True)  10.8 us
    all_to_all x1, waiting for transfers between devices, shards(): lax.all_to_all(waves, 'gx', split_axis=0, concat_axis=0, tiled=True)  10.7 us
    all_to_all x1, starting transfers between devices, shards(): lax.all_to_all(rows, 'gy', split_axis=0, concat_axis=0, tiled=True)  7.34 us
    all_to_all x1, starting transfers between devices, shards(): rows = lax.all_to_all(spread, 'gy', split_axis=0, concat_axis=0, tiled=True)  6.78 us
    all_to_all x1, starting transfers between devices, shards(): waves = lax.all_to_all(waves, 'gx', split_axis=0, concat_axis=0, tiled=True)  4.57 us
  transfers between devices with their start and end apart: 12, of which 7 were waited for; matrix products, arithmetic and copies ran while one was open for 1% of the time, Pallas kernels for 8%

profile of v2, /device:TPU:1, one launch (start us, length us, event | category | flops | bytes accessed | tf_op | source)
XLA Modules:
  0.0 114.0 jit_solution(17186529360652319064)
XLA Ops:
  0.6 0.0 copy-start.9
  0.6 0.0 copy-start.12
  0.7 0.0 copy-start.13
  0.7 0.0 copy-start.10
  0.7 0.0 copy-start.4
  0.7 0.0 copy-start.8
  0.7 0.0 copy-start.11
  0.7 0.0 copy-start.7
  0.7 0.0 copy-start.14
  0.7 0.1 pad.18.clone
  0.8 1.0 maximum_maximum_fusion.own
  1.9 3.9 %collective-permute-start = (f32[136,128]{1,0:T(8,128)S(1)}, f32[136,128]{1,0:T(8,128)S(1)}, u32[]{:S(2)}, u32[]{:S(2)}) collective-permute-start(f32[136,128]{1,0:T(8,128)S(1)} %get-tuple-element.61), channel_id=1, source_target_pairs={{0,8},{8,16},{16,24},{24,32},{32,40},{40,48},{48,56},{56,64},{64,7... | collective-permute-start | bytes 208904 | tf_op jit(solution)/shard_map/ppermute | solution.py:663
  5.8 12.1 %collective-permute-start.1 = (f32[136,128]{1,0:T(8,128)S(1)}, f32[136,128]{1,0:T(8,128)S(1)}, u32[]{:S(2)}, u32[]{:S(2)}) collective-permute-start(f32[136,128]{1,0:T(8,128)S(1)} %get-tuple-element.60), channel_id=1, source_target_pairs={{0,504},{8,0},{16,8},{24,16},{32,24},{40,32},{48,40},{56,48},{64,5... | collective-permute-start | bytes 208904 | tf_op jit(solution)/shard_map/ppermute | solution.py:663
  18.0 0.1 fusion
  18.1 0.0 collective-permute-done.left
  18.1 0.1 fusion.2
  18.2 1.1 %collective-permute-done.1.right = f32[136,128]{1,0:T(8,128)S(1)} collective-permute-done((f32[136,128]{1,0:T(8,128)S(1)}, f32[136,128]{1,0:T(8,128)S(1)}, u32[]{:S(2)}, u32[]{:S(2)}) %collective-permute-start.1) | collective-permute-done | bytes 69664 | tf_op jit(solution)/shard_map/ppermute | solution.py:663
  19.3 0.1 fusion.3
  19.4 0.1 pad_maximum_fusion.1
  19.5 1.5 %collective-permute-start.3 = (f32[136,64]{1,0:T(8,128)S(1)}, f32[136,64]{1,0:T(8,128)S(1)}, u32[]{:S(2)}, u32[]{:S(2)}) collective-permute-start(f32[136,64]{1,0:T(8,128)S(1)} %pad_maximum_fusion.1), channel_id=1, source_target_pairs={{0,7},{1,0},{2,1},{3,2},{4,3},{5,4},{6,5},{7,6},{8,15},{9,8},{10,9... | collective-permute-start | bytes 104456 | tf_op jit(solution)/shard_map/ppermute | solution.py:663
  21.1 0.1 pad_maximum_fusion
  21.2 1.2 %collective-permute-start.2 = (f32[136,64]{1,0:T(8,128)S(1)}, f32[136,64]{1,0:T(8,128)S(1)}, u32[]{:S(2)}, u32[]{:S(2)}) collective-permute-start(f32[136,64]{1,0:T(8,128)S(1)} %pad_maximum_fusion), channel_id=1, source_target_pairs={{0,1},{1,2},{2,3},{3,4},{4,5},{5,6},{6,7},{7,0},{8,9},{9,10},{10,1... | collective-permute-start | bytes 104456 | tf_op jit(solution)/shard_map/ppermute | solution.py:663
  22.4 0.7 constant_dynamic-slice_fusion.yz
  23.1 0.0 copy-done.9
  23.1 0.0 copy-done.12
  23.1 0.0 copy-done.13
  23.1 0.0 copy-done.10
  23.2 0.9 shard_map.185
  24.0 0.2 collective-permute-done.3.high
  24.2 0.0 collective-permute-done.2.low
  24.3 5.9 %shard_map.186 = (f32[8,24,128]{2,1,0:T(8,128)}, f32[1,256]{1,0:T(1,128)S(1)}, f32[3,16,256]{2,1,0:T(8,128)S(1)}, f32[8,640]{1,0:T(8,128)S(1)}, f32[8,128,256]{2,1,0:T(8,128)S(1)}, /*index=5*/f32[12,128,256]{2,1,0:T(8,128)}) custom-call(f32[136,128]{1,0:T(8,128)S(1)} %collective-permute-done.left, f32[136,256]{1,0:T(8,128)S(1)} %maximum_maximum_fusion.own, ...), custom_call_target="tpu_custom_call" | custom-call | flops 1000000000 | bytes 2000000 | tf_op jit(solution)/shard_map/pallas_call | solution.py:650
  30.2 6.8 %all-to-all-start = ((f32[8,24,128]{2,1,0:T(8,128)}), f32[8,24,128]{2,1,0:T(8,128)S(1)}, u32[]{:S(2)}, u32[]{:S(2)}) async-start(f32[8,24,128]{2,1,0:T(8,128)} %get-tuple-element.35), calls=%async_computation | async-start | bytes 196608 | tf_op jit(solution)/shard_map/all_to_all | solution.py:755
  37.0 3.9 %shard_map.187.pulls_0 = f32[48,256]{1,0:T(8,128)S(1)} custom-call(f32[3,16,256]{2,1,0:T(8,128)S(1)} %get-tuple-element.36.rel, f32[12,128,256]{2,1,0:T(8,128)} %get-tuple-element.41.kept, f32[8,128,256]{2,1,0:T(8,128)S(1)} %get-tuple-element.38.along, s32[12,256]{1,0:T(8,128)S(1)} %copy-done.14, bf16[384,192]{1,0:T(8,128)(2,1)S(1)} %get-tuple-element.30.in_wide, ...), custom_call_target="tpu_custom_call" | custom-call | flops 2000000000 | bytes 2000000 | tf_op jit(solution)/shard_map/pallas_call | solution.py:650
  40.8 1.1 all-to-all-done.rows
  42.0 0.8 shard_map.188
  42.8 12.1 %all-to-all-start.1 = ((f32[64,2,128]{2,1,0:T(2,128)}), f32[64,2,128]{2,1,0:T(2,128)S(1)}, u32[]{:S(2)}, u32[]{:S(2)}) async-start(f32[64,2,128]{2,1,0:T(2,128)} %shard_map.188), calls=%async_computation.1 | async-start | bytes 131072 | tf_op jit(solution)/shard_map/all_to_all | solution.py:760
  54.9 0.0 copy-start
  54.9 0.0 copy-start.1
  54.9 0.0 copy-start.5
  54.9 0.0 copy-start.6
  54.9 3.1 %shard_map.189.pulls_1 = f32[48,256]{1,0:T(8,128)S(1)} custom-call(f32[3,16,256]{2,1,0:T(8,128)S(1)} %get-tuple-element.36.rel, f32[12,128,256]{2,1,0:T(8,128)} %get-tuple-element.41.kept, f32[8,128,256]{2,1,0:T(8,128)S(1)} %get-tuple-element.38.along, s32[12,256]{1,0:T(8,128)S(1)} %copy-done.14, bf16[384,192]{1,0:T(8,128)(2,1)S(1)} %get-tuple-element.30.in_wide, ...), custom_call_target="tpu_custom_call" | custom-call | flops 2000000000 | bytes 2000000 | tf_op jit(solution)/shard_map/pallas_call | solution.py:650
  58.1 10.7 %all-to-all-done.1.planes = f32[64,2,128]{2,1,0:T(2,128)S(1)} async-done(((f32[64,2,128]{2,1,0:T(2,128)}), f32[64,2,128]{2,1,0:T(2,128)S(1)}, u32[]{:S(2)}, u32[]{:S(2)}) %all-to-all-start.1) | async-done | bytes 65568 | tf_op jit(solution)/shard_map/all_to_all | solution.py:760
  68.8 0.0 copy-done.1
  68.8 1.5 %shard_map.190 = f32[64,2,128]{2,1,0:T(2,128)} custom-call(f32[64,2,128]{2,1,0:T(2,128)S(1)} %all-to-all-done.1.planes, bf16[640,192]{1,0:T(8,128)(2,1)S(1)} %copy-done.1, bf16[448,384]{1,0:T(8,128)(2,1)S(1)} %copy-done, f32[128,128]{1,0:T(8,128)S(1)} %copy-done.5, f32[128,128]{1,0:T(8,128)S(1)} %copy-done.6, f32[1,4,128]{2,1,0:T(4,128)S(1)} %constant_dynamic-slice_fusion.yz), custom_call_target="tpu_custom_call" | custom-call | flops 10000000 | bytes 2000000 | tf_op jit(solution)/shard_map/pallas_call | solution.py:650
  70.3 0.6 shard_map.192
  70.9 2.1 %collective-permute-start.4 = (f32[96,128]{1,0:T(8,128)S(1)}, f32[96,128]{1,0:T(8,128)S(1)}, u32[]{:S(2)}, u32[]{:S(2)}) collective-permute-start(f32[96,128]{1,0:T(8,128)S(1)} %get-tuple-element.52.upper), channel_id=1, source_target_pairs={{0,8},{8,16},{16,24},{24,32},{32,40},{40,48},{48,56},{56,64},{64,7... | collective-permute-start | bytes 147464 | tf_op jit(solution)/shard_map/ppermute | solution.py:663
  73.0 0.1 fusion.5
  73.1 6.5 %collective-permute-start.5 = (f32[96,128]{1,0:T(8,128)S(1)}, f32[96,128]{1,0:T(8,128)S(1)}, u32[]{:S(2)}, u32[]{:S(2)}) collective-permute-start(f32[96,128]{1,0:T(8,128)S(1)} %get-tuple-element.53.lower), channel_id=1, source_target_pairs={{0,504},{8,0},{16,8},{24,16},{32,24},{40,32},{48,40},{56,48},{64,5... | collective-permute-start | bytes 147464 | tf_op jit(solution)/shard_map/ppermute | solution.py:663
  79.6 4.6 %all-to-all-start.2 = ((f32[64,2,128]{2,1,0:T(2,128)}), f32[64,2,128]{2,1,0:T(2,128)S(1)}, u32[]{:S(2)}, u32[]{:S(2)}) async-start(f32[64,2,128]{2,1,0:T(2,128)} %shard_map.190), calls=%async_computation.2 | async-start | bytes 131072 | tf_op jit(solution)/shard_map/all_to_all | solution.py:786
  84.2 0.0 collective-permute-done.4.left
  84.2 0.1 fusion.4
  84.3 0.0 collective-permute-done.5.right
  84.3 0.1 fusion.7
  84.4 0.1 pad_maximum_fusion.3
  84.5 2.9 %collective-permute-start.7 = (f32[96,64]{1,0:T(8,128)S(1)}, f32[96,64]{1,0:T(8,128)S(1)}, u32[]{:S(2)}, u32[]{:S(2)}) collective-permute-start(f32[96,64]{1,0:T(8,128)S(1)} %pad_maximum_fusion.3), channel_id=1, source_target_pairs={{0,7},{1,0},{2,1},{3,2},{4,3},{5,4},{6,5},{7,6},{8,15},{9,8},{10,9... | collective-permute-start | bytes 73736 | tf_op jit(solution)/shard_map/ppermute | solution.py:663
  87.4 10.8 %all-to-all-done.2.waves = f32[64,2,128]{2,1,0:T(2,128)S(1)} async-done(((f32[64,2,128]{2,1,0:T(2,128)}), f32[64,2,128]{2,1,0:T(2,128)S(1)}, u32[]{:S(2)}, u32[]{:S(2)}) %all-to-all-start.2) | async-done | bytes 65568 | tf_op jit(solution)/shard_map/all_to_all | solution.py:786
  98.2 0.8 shard_map.191
  99.0 7.3 %all-to-all-start.3 = ((f32[8,24,128]{2,1,0:T(8,128)}), f32[8,24,128]{2,1,0:T(8,128)S(1)}, u32[]{:S(2)}, u32[]{:S(2)}) async-start(f32[8,24,128]{2,1,0:T(8,128)} %shard_map.191), calls=%async_computation.3 | async-start | bytes 196608 | tf_op jit(solution)/shard_map/all_to_all | solution.py:789
  106.4 0.1 pad_maximum_fusion.2
  106.5 1.6 %collective-permute-start.6 = (f32[96,64]{1,0:T(8,128)S(1)}, f32[96,64]{1,0:T(8,128)S(1)}, u32[]{:S(2)}, u32[]{:S(2)}) collective-permute-start(f32[96,64]{1,0:T(8,128)S(1)} %pad_maximum_fusion.2), channel_id=1, source_target_pairs={{0,1},{1,2},{2,3},{3,4},{4,5},{5,6},{6,7},{7,0},{8,9},{9,10},{10,1... | collective-permute-start | bytes 73736 | tf_op jit(solution)/shard_map/ppermute | solution.py:663
  108.2 0.0 collective-permute-done.7.high
  108.2 1.2 %collective-permute-done.6.low = f32[96,64]{1,0:T(8,128)S(1)} collective-permute-done((f32[96,64]{1,0:T(8,128)S(1)}, f32[96,64]{1,0:T(8,128)S(1)}, u32[]{:S(2)}, u32[]{:S(2)}) %collective-permute-start.6) | collective-permute-done | bytes 24608 | tf_op jit(solution)/shard_map/ppermute | solution.py:663
  109.3 2.1 %all-to-all-done.3.potential = f32[8,24,128]{2,1,0:T(8,128)S(1)} async-done(((f32[8,24,128]{2,1,0:T(8,128)}), f32[8,24,128]{2,1,0:T(8,128)S(1)}, u32[]{:S(2)}, u32[]{:S(2)}) %all-to-all-start.3) | async-done | bytes 98336 | tf_op jit(solution)/shard_map/all_to_all | solution.py:789
  111.4 2.5 %shard_map.193 = (f32[3,256]{1,0:T(4,128)}, f32[1,1]{1,0:T(1,128)}) custom-call(f32[8,24,128]{2,1,0:T(8,128)S(1)} %all-to-all-done.3.potential, f32[8,640]{1,0:T(8,128)S(1)} %get-tuple-element.47.places, f32[1,256]{1,0:T(1,128)S(1)} %get-tuple-element.48.charge, f32[128,896]{1,0:T(8,128)S(1)} %get-tuple-element.51.waves, ...), custom_call_target="tpu_custom_call" | custom-call | flops 1000000000 | bytes 2000000 | tf_op jit(solution)/shard_map/pallas_call | solution.py:650
  (14 shorter events, 0.0 us)
Async XLA Ops:
  0.6 22.5 %copy-start.9 = (f32[128,128]{1,0:T(8,128)S(1)}, f32[128,128]{1,0:T(8,128)}, u32[]{:S(2)}) copy-start(f32[128,128]{1,0:T(8,128)} %constant.33.clone.z_table) | copy-start | bytes 196612
  0.6 22.5 %copy-start.12 = (f32[128]{0:T(128)S(1)}, f32[128]{0:T(128)}, u32[]{:S(2)}) copy-start(f32[128]{0:T(128)} %param.26) | copy-start | bytes 1540
  0.7 22.4 %copy-start.13 = (f32[128]{0:T(128)S(1)}, f32[128]{0:T(128)}, u32[]{:S(2)}) copy-start(f32[128]{0:T(128)} %param.27) | copy-start | bytes 1540
  0.7 22.4 %copy-start.10 = (f32[64,8]{0,1:T(8,128)S(1)}, f32[64,8]{0,1:T(8,128)}, u32[]{:S(2)}) copy-start(f32[64,8]{0,1:T(8,128)} %param.22) | copy-start | bytes 6148
  0.7 22.4 %copy-start.4 = (f32[384,64]{0,1:T(8,128)S(1)}, f32[384,64]{0,1:T(8,128)}, u32[]{:S(2)}) copy-start(f32[384,64]{0,1:T(8,128)} %param.23) | copy-start | bytes 294916
  0.7 22.4 %copy-start.8 = (f32[128,128]{1,0:T(8,128)S(1)}, f32[128,128]{1,0:T(8,128)}, u32[]{:S(2)}) copy-start(f32[128,128]{1,0:T(8,128)} %up_weight.1) | copy-start | bytes 196612
  0.7 22.4 %copy-start.11 = (f32[2,128]{1,0:T(2,128)S(1)}, f32[2,128]{1,0:T(2,128)}, u32[]{:S(2)}) copy-start(f32[2,128]{1,0:T(2,128)} %coupling.1) | copy-start | bytes 3076
  0.7 22.4 %copy-start.7 = (f32[128,128]{1,0:T(8,128)S(1)}, f32[128,128]{1,0:T(8,128)}, u32[]{:S(2)}) copy-start(f32[128,128]{1,0:T(8,128)} %mix_weight.1) | copy-start | bytes 196612
  0.7 23.5 %copy-start.14 = (s32[12,256]{1,0:T(8,128)S(1)}, s32[12,256]{1,0:T(8,128)}, u32[]{:S(2)}) copy-start(s32[12,256]{1,0:T(8,128)} %codes.5) | copy-start | bytes 36868
  1.9 16.2 %collective-permute-start = (f32[136,128]{1,0:T(8,128)S(1)}, f32[136,128]{1,0:T(8,128)S(1)}, u32[]{:S(2)}, u32[]{:S(2)}) collective-permute-start(f32[136,128]{1,0:T(8,128)S(1)} %get-tuple-element.61), channel_id=1, source_target_pairs={{0,8},{8,16},{16,24},{24,32},{32,40},{40,48},{48,56},{56,64},{64,7... | collective-permute-start | bytes 208904 | tf_op jit(solution)/shard_map/ppermute | solution.py:663
  5.8 13.5 %collective-permute-start.1 = (f32[136,128]{1,0:T(8,128)S(1)}, f32[136,128]{1,0:T(8,128)S(1)}, u32[]{:S(2)}, u32[]{:S(2)}) collective-permute-start(f32[136,128]{1,0:T(8,128)S(1)} %get-tuple-element.60), channel_id=1, source_target_pairs={{0,504},{8,0},{16,8},{24,16},{32,24},{40,32},{48,40},{56,48},{64,5... | collective-permute-start | bytes 208904 | tf_op jit(solution)/shard_map/ppermute | solution.py:663
  19.5 4.7 %collective-permute-start.3 = (f32[136,64]{1,0:T(8,128)S(1)}, f32[136,64]{1,0:T(8,128)S(1)}, u32[]{:S(2)}, u32[]{:S(2)}) collective-permute-start(f32[136,64]{1,0:T(8,128)S(1)} %pad_maximum_fusion.1), channel_id=1, source_target_pairs={{0,7},{1,0},{2,1},{3,2},{4,3},{5,4},{6,5},{7,6},{8,15},{9,8},{10,9... | collective-permute-start | bytes 104456 | tf_op jit(solution)/shard_map/ppermute | solution.py:663
  21.2 3.1 %collective-permute-start.2 = (f32[136,64]{1,0:T(8,128)S(1)}, f32[136,64]{1,0:T(8,128)S(1)}, u32[]{:S(2)}, u32[]{:S(2)}) collective-permute-start(f32[136,64]{1,0:T(8,128)S(1)} %pad_maximum_fusion), channel_id=1, source_target_pairs={{0,1},{1,2},{2,3},{3,4},{4,5},{5,6},{6,7},{7,0},{8,9},{9,10},{10,1... | collective-permute-start | bytes 104456 | tf_op jit(solution)/shard_map/ppermute | solution.py:663
  30.2 11.8 %all-to-all-start = ((f32[8,24,128]{2,1,0:T(8,128)}), f32[8,24,128]{2,1,0:T(8,128)S(1)}, u32[]{:S(2)}, u32[]{:S(2)}) async-start(f32[8,24,128]{2,1,0:T(8,128)} %get-tuple-element.35), calls=%async_computation | async-start | bytes 196608 | tf_op jit(solution)/shard_map/all_to_all | solution.py:755
  37.0 5.0 %copy-start.2 = (bf16[128,576]{1,0:T(8,128)(2,1)S(1)}, bf16[128,576]{1,0:T(8,128)(2,1)}, u32[]{:S(2)}) copy-start(bf16[128,576]{1,0:T(8,128)(2,1)} %constant.34.clone.table) | copy-start | bytes 442372
  42.8 26.0 %all-to-all-start.1 = ((f32[64,2,128]{2,1,0:T(2,128)}), f32[64,2,128]{2,1,0:T(2,128)S(1)}, u32[]{:S(2)}, u32[]{:S(2)}) async-start(f32[64,2,128]{2,1,0:T(2,128)} %shard_map.188), calls=%async_computation.1 | async-start | bytes 131072 | tf_op jit(solution)/shard_map/all_to_all | solution.py:760
  54.9 13.9 %copy-start = (bf16[448,384]{1,0:T(8,128)(2,1)S(1)}, bf16[448,384]{1,0:T(8,128)(2,1)}, u32[]{:S(2)}) copy-start(bf16[448,384]{1,0:T(8,128)(2,1)} %constant.37.clone.x_out) | copy-start | bytes 1032196
  54.9 13.9 %copy-start.1 = (bf16[640,192]{1,0:T(8,128)(2,1)S(1)}, bf16[640,192]{1,0:T(8,128)(2,1)}, u32[]{:S(2)}) copy-start(bf16[640,192]{1,0:T(8,128)(2,1)} %constant.36.clone.x_in) | copy-start | bytes 737284
  54.9 13.9 %copy-start.5 = (f32[128,128]{1,0:T(8,128)S(1)}, f32[128,128]{1,0:T(8,128)}, u32[]{:S(2)}) copy-start(f32[128,128]{1,0:T(8,128)} %constant.38.clone.x_gain) | copy-start | bytes 196612
  54.9 13.8 %copy-start.6 = (f32[128,128]{1,0:T(8,128)S(1)}, f32[128,128]{1,0:T(8,128)}, u32[]{:S(2)}) copy-start(f32[128,128]{1,0:T(8,128)} %constant.39.clone.x_square) | copy-start | bytes 196612
  70.3 27.9 %copy-start.3 = (bf16[192,384]{1,0:T(8,128)(2,1)S(1)}, bf16[192,384]{1,0:T(8,128)(2,1)}, u32[]{:S(2)}) copy-start(bf16[192,384]{1,0:T(8,128)(2,1)} %constant.35.clone.table) | copy-start | bytes 442372
  70.9 13.3 %collective-permute-start.4 = (f32[96,128]{1,0:T(8,128)S(1)}, f32[96,128]{1,0:T(8,128)S(1)}, u32[]{:S(2)}, u32[]{:S(2)}) collective-permute-start(f32[96,128]{1,0:T(8,128)S(1)} %get-tuple-element.52.upper), channel_id=1, source_target_pairs={{0,8},{8,16},{16,24},{24,32},{32,40},{40,48},{48,56},{56,64},{64,7... | collective-permute-start | bytes 147464 | tf_op jit(solution)/shard_map/ppermute | solution.py:663
  73.1 11.2 %collective-permute-start.5 = (f32[96,128]{1,0:T(8,128)S(1)}, f32[96,128]{1,0:T(8,128)S(1)}, u32[]{:S(2)}, u32[]{:S(2)}) collective-permute-start(f32[96,128]{1,0:T(8,128)S(1)} %get-tuple-element.53.lower), channel_id=1, source_target_pairs={{0,504},{8,0},{16,8},{24,16},{32,24},{40,32},{48,40},{56,48},{64,5... | collective-permute-start | bytes 147464 | tf_op jit(solution)/shard_map/ppermute | solution.py:663
  79.6 18.6 %all-to-all-start.2 = ((f32[64,2,128]{2,1,0:T(2,128)}), f32[64,2,128]{2,1,0:T(2,128)S(1)}, u32[]{:S(2)}, u32[]{:S(2)}) async-start(f32[64,2,128]{2,1,0:T(2,128)} %shard_map.190), calls=%async_computation.2 | async-start | bytes 131072 | tf_op jit(solution)/shard_map/all_to_all | solution.py:786
  84.5 23.7 %collective-permute-start.7 = (f32[96,64]{1,0:T(8,128)S(1)}, f32[96,64]{1,0:T(8,128)S(1)}, u32[]{:S(2)}, u32[]{:S(2)}) collective-permute-start(f32[96,64]{1,0:T(8,128)S(1)} %pad_maximum_fusion.3), channel_id=1, source_target_pairs={{0,7},{1,0},{2,1},{3,2},{4,3},{5,4},{6,5},{7,6},{8,15},{9,8},{10,9... | collective-permute-start | bytes 73736 | tf_op jit(solution)/shard_map/ppermute | solution.py:663
  99.0 12.4 %all-to-all-start.3 = ((f32[8,24,128]{2,1,0:T(8,128)}), f32[8,24,128]{2,1,0:T(8,128)S(1)}, u32[]{:S(2)}, u32[]{:S(2)}) async-start(f32[8,24,128]{2,1,0:T(8,128)} %shard_map.191), calls=%async_computation.3 | async-start | bytes 196608 | tf_op jit(solution)/shard_map/all_to_all | solution.py:789
  106.5 2.8 %collective-permute-start.6 = (f32[96,64]{1,0:T(8,128)S(1)}, f32[96,64]{1,0:T(8,128)S(1)}, u32[]{:S(2)}, u32[]{:S(2)}) collective-permute-start(f32[96,64]{1,0:T(8,128)S(1)} %pad_maximum_fusion.2), channel_id=1, source_target_pairs={{0,1},{1,2},{2,3},{3,4},{4,5},{5,6},{6,7},{7,0},{8,9},{9,10},{10,1... | collective-permute-start | bytes 73736 | tf_op jit(solution)/shard_map/ppermute | solution.py:663

commit v3 on v2

--- a/solution.py
+++ b/solution.py
@@ -483,9 +483,14 @@
 
 
 def slopes_kernel(
-    k0, rel, kept, along, codes, in_wide, out_wide, columns, pulls,
-    basis, basis_slope, harm, radial, radial_slope, gathered, up, sems,
+    k0, rel, kept, along, codes, in_wide, out_wide, columns, *refs
 ):
+    scratch = refs[-8:]
+    basis, basis_slope, harm, radial, radial_slope, gathered, up, sems = scratch
+    before_planes, planes = (refs[0:2], refs[2:4]) if k0 else ((), refs[0:2])
+    base = 8 * k0
+    for done, plane in zip(before_planes, planes):
+        plane[0:base, :] = done[...]
     fetch_up = pltpu.make_async_copy(kept.at[k0 : k0 + HALF], up, sems.at[0])
     fetch_up.start()
     first = slot(k0)
@@ -548,20 +553,18 @@
         vz = r3 * g[3] + r15 * (uy * g[5] + ux * g[7]) + (3.0 * r5) * uz * g[6]
         radial_part = g[0] - (vx * ux + vy * uy + vz * uz) * inv
         for c, (v, along_c) in enumerate(((vx, ux), (vy, uy), (vz, uz))):
-            first = 8 * (3 * w + c)
-            pulls[first : first + HALF, :] = (radial_part * along_c + v * inv)[0:HALF]
+            first = base + 8 * (3 * w + c)
+            pull = radial_part * along_c + v * inv
             spare = codes[k0 + 2 * c : k0 + 2 * c + 2, :].astype(f32)
-            pulls[first + HALF : first + 8, :] = spare if w == 0 else jnp.zeros_like(spare)
-
-
-def reach_kernel(pulls_0, pulls_1, places, z_table, out, lower, upper):
+            pull = jnp.concatenate([pull[0:HALF], spare if w == 0 else 0.0 * spare], axis=0)
+            planes[0][first : first + 8, :] = pull[:, 0:128]
+            planes[1][first : first + 8, :] = pull[:, 128:256]
+
+
+def reach_kernel(places, z_table, out):
     weights, slopes = spline_rows(places[2:3, :], 0, NZ, True)
     both = jnp.concatenate([weights, slopes[:, 128:384]], axis=1)
     out[...] = dot(z_table[...], both, highest)
-    for half, pulls in enumerate((pulls_0, pulls_1)):
-        rows = slice(48 * half, 48 * half + 48)
-        lower[rows, :] = pulls[:, 0:128]
-        upper[rows, :] = pulls[:, 128:256]
 
 
 def final_kernel(
@@ -663,13 +666,14 @@
     return lax.ppermute(array, axis, [(i, (i + by) % devices) for i in range(devices)])
 
 
-def ghosts(lower, upper):
-    left = passed_along(upper, "gx", 1)
-    right = passed_along(lower, "gx", -1)
-    planes = (left, lower, upper, right)
+def plane_ghosts(lower, upper):
+    return passed_along(upper, "gx", 1), passed_along(lower, "gx", -1)
+
+
+def row_ghosts(*planes):
     low = passed_along(jnp.concatenate([x[:, 112:] for x in planes], axis=1), "gy", 1)
     high = passed_along(jnp.concatenate([x[:, :16] for x in planes], axis=1), "gy", -1)
-    return left, right, low, high
+    return low, high
 
 
 def struct(*shape, dtype=f32):
@@ -682,7 +686,9 @@
 ):
     table = {name: jnp.asarray(value) for name, value in TABLES.items()}
     own = jnp.concatenate([features, positions, jnp.zeros((5, ATOM), f32)], axis=0)
-    left, right, low, high = ghosts(own[:, 0:128], own[:, 128:256])
+    lower, upper = own[:, 0:128], own[:, 128:256]
+    left, right = plane_ghosts(lower, upper)
+    low, high = row_ghosts(left, lower, upper, right)
     waves_z, columns, up_wide, in_wide, out_wide = call(
         prepare_kernel,
         (
@@ -735,10 +741,10 @@
     )
     spread, yz = lax.optimization_barrier((spread, yz))
 
-    def pulls_of(k0, kept):
+    def pulls_of(k0, kept, *before):
         return call(
             functools.partial(slopes_kernel, k0),
-            struct(48, ATOM),
+            (struct(8 * k0 + 48, 128),) * 2,
             SLOPE_SCRATCH,
             2 * 10**9,
             rel,
@@ -748,18 +754,19 @@
             in_wide,
             out_wide,
             columns,
+            *before,
             far_in=(1,),
             mib=28,
         )
 
     rows = lax.all_to_all(spread, "gy", split_axis=0, concat_axis=0, tiled=True)
-    pulls_0 = pulls_of(0, kept)
-    rows, pulls_0 = lax.optimization_barrier((rows, pulls_0))
+    pulls = pulls_of(0, kept)
+    rows, *pulls = lax.optimization_barrier((rows, *pulls))
     waves = call(y_in_kernel, struct(N_GX, 2, 128), [], 10**7, rows, table["y_in"])
     waves, kept = lax.optimization_barrier((waves, kept))
     planes = lax.all_to_all(waves, "gx", split_axis=0, concat_axis=0, tiled=True)
-    pulls_1 = pulls_of(HALF, kept)
-    planes, pulls_1 = lax.optimization_barrier((planes, pulls_1))
+    lower, upper = pulls_of(HALF, kept, *pulls)
+    planes, _ = lax.optimization_barrier((planes, lower))
     waves = call(
         x_kernel,
         struct(N_GX, 2, 128),
@@ -772,19 +779,11 @@
         table["x_square"],
         yz,
     )
-    waves, pulls_0, pulls_1 = lax.optimization_barrier((waves, pulls_0, pulls_1))
-    reach, lower, upper = call(
-        reach_kernel,
-        (struct(NZ, EXT + ATOM), struct(96, 128), struct(96, 128)),
-        [],
-        10**9,
-        pulls_0,
-        pulls_1,
-        places,
-        table["z"],
-    )
+    reach = call(reach_kernel, struct(NZ, EXT + ATOM), [], 10**8, places, table["z"])
     waves = lax.all_to_all(waves, "gx", split_axis=0, concat_axis=0, tiled=True)
-    left, right, low, high = ghosts(lower, upper)
+    left, right = plane_ghosts(lower, upper)
+    waves, left, right = lax.optimization_barrier((waves, left, right))
+    low, high = row_ghosts(left, lower, upper, right)
     rows = call(y_out_kernel, struct(N_GY, ROW_PAD, 128), [], 10**7, waves, table["y_out"])
     potential = lax.all_to_all(rows, "gy", split_axis=0, concat_axis=0, tiled=True)
     forces, energy = call(

time: 115 us -> 106 us (0.922)
  waiting for transfers between devices: 27.3 us -> 21.9 us
  starting transfers between devices: 62.7 us -> 59.3 us
    all_to_all x1, waiting for transfers between devices: 10.8 us -> 0.01 us  [shards(): waves = lax.all_to_all(waves, 'gx', split_axis=0, concat_axis=0, tiled=True)]
    ppermute x8, waiting for transfers between devices: 2.57 us -> 8.4 us  [passed_along(): lax.ppermute(array, axis, [(i, (i + by) % devices) for i in range(devices)])]
    all_to_all x1, starting transfers between devices: 7.34 us -> 3.31 us  [shards(): lax.all_to_all(rows, 'gy', split_axis=0, concat_axis=0, tiled=True)]
  transfers between devices with their start and end apart: 12 -> 12, of which waited for: 7 -> 7; matrix products, arithmetic and copies ran while one was open for 1% -> 1% of each run, Pallas kernels for 8% -> 9%
where the time goes in v3:
time: 106 us; the launch traced here: 105 us
  starting transfers between devices  59.3 us (56%)
  waiting for transfers between devices  21.9 us (21%)
  Pallas kernels  20.5 us (19%)
  other arithmetic  1.51 us (1%)
  local copies, waits for them, and re-layouts  1.27 us (1%)
    ppermute x8, starting transfers between devices, passed_along(): lax.ppermute(array, axis, [(i, (i + by) % devices) for i in range(devices)])  32.6 us
    pallas_call x9, Pallas kernels, call(): pl.pallas_call(kernel, out_shape=outs, in_specs=[far if i in far_in else...  20.5 us
    all_to_all x1, starting transfers between devices, shards(): lax.all_to_all(waves, 'gx', split_axis=0, concat_axis=0, tiled=True)  12.1 us
    all_to_all x1, waiting for transfers between devices, shards(): lax.all_to_all(waves, 'gx', split_axis=0, concat_axis=0, tiled=True)  10.5 us
    ppermute x8, waiting for transfers between devices, passed_along(): lax.ppermute(array, axis, [(i, (i + by) % devices) for i in range(devices)])  8.4 us
    all_to_all x1, starting transfers between devices, shards(): rows = lax.all_to_all(spread, 'gy', split_axis=0, concat_axis=0, tiled=True)  6.78 us
    all_to_all x1, starting transfers between devices, shards(): waves = lax.all_to_all(waves, 'gx', split_axis=0, concat_axis=0, tiled=True)  4.56 us
    all_to_all x1, starting transfers between devices, shards(): lax.all_to_all(rows, 'gy', split_axis=0, concat_axis=0, tiled=True)  3.31 us
  transfers between devices with their start and end apart: 12, of which 7 were waited for; matrix products, arithmetic and copies ran while one was open for 1% of the time, Pallas kernels for 9%

profile of v3, /device:TPU:1, one launch (start us, length us, event | category | flops | bytes accessed | tf_op | source)
XLA Modules:
  0.0 105.5 jit_solution(13939288147114939467)
XLA Ops:
  0.6 0.0 copy-start.2
  0.6 0.0 copy-start.12
  0.7 0.0 copy-start.13
  0.7 0.0 copy-start.10
  0.7 0.0 copy-start.5
  0.7 0.0 copy-start.9
  0.7 0.1 pad.18.clone
  0.8 1.0 maximum_maximum_fusion.own
  1.9 3.9 %collective-permute-start = (f32[136,128]{1,0:T(8,128)S(1)}, f32[136,128]{1,0:T(8,128)S(1)}, u32[]{:S(2)}, u32[]{:S(2)}) collective-permute-start(f32[136,128]{1,0:T(8,128)S(1)} %get-tuple-element.63), channel_id=1, source_target_pairs={{0,8},{8,16},{16,24},{24,32},{32,40},{40,48},{48,56},{56,64},{64,7... | collective-permute-start | bytes 208904 | tf_op jit(solution)/shard_map/ppermute | solution.py:666
  5.8 12.1 %collective-permute-start.1 = (f32[136,128]{1,0:T(8,128)S(1)}, f32[136,128]{1,0:T(8,128)S(1)}, u32[]{:S(2)}, u32[]{:S(2)}) collective-permute-start(f32[136,128]{1,0:T(8,128)S(1)} %get-tuple-element.62), channel_id=1, source_target_pairs={{0,504},{8,0},{16,8},{24,16},{32,24},{40,32},{48,40},{56,48},{64,5... | collective-permute-start | bytes 208904 | tf_op jit(solution)/shard_map/ppermute | solution.py:666
  18.0 0.1 fusion
  18.1 0.0 collective-permute-done.left
  18.1 0.1 fusion.2
  18.2 1.1 %collective-permute-done.1.right = f32[136,128]{1,0:T(8,128)S(1)} collective-permute-done((f32[136,128]{1,0:T(8,128)S(1)}, f32[136,128]{1,0:T(8,128)S(1)}, u32[]{:S(2)}, u32[]{:S(2)}) %collective-permute-start.1) | collective-permute-done | bytes 69664 | tf_op jit(solution)/shard_map/ppermute | solution.py:666
  19.3 0.1 fusion.3
  19.4 0.1 pad_maximum_fusion.1
  19.5 1.5 %collective-permute-start.3 = (f32[136,64]{1,0:T(8,128)S(1)}, f32[136,64]{1,0:T(8,128)S(1)}, u32[]{:S(2)}, u32[]{:S(2)}) collective-permute-start(f32[136,64]{1,0:T(8,128)S(1)} %pad_maximum_fusion.1), channel_id=1, source_target_pairs={{0,7},{1,0},{2,1},{3,2},{4,3},{5,4},{6,5},{7,6},{8,15},{9,8},{10,9... | collective-permute-start | bytes 104456 | tf_op jit(solution)/shard_map/ppermute | solution.py:666
  21.1 0.1 pad_maximum_fusion
  21.2 1.2 %collective-permute-start.2 = (f32[136,64]{1,0:T(8,128)S(1)}, f32[136,64]{1,0:T(8,128)S(1)}, u32[]{:S(2)}, u32[]{:S(2)}) collective-permute-start(f32[136,64]{1,0:T(8,128)S(1)} %pad_maximum_fusion), channel_id=1, source_target_pairs={{0,1},{1,2},{2,3},{3,4},{4,5},{5,6},{6,7},{7,0},{8,9},{9,10},{10,1... | collective-permute-start | bytes 104456 | tf_op jit(solution)/shard_map/ppermute | solution.py:666
  22.4 0.7 constant_dynamic-slice_fusion.yz
  23.1 0.0 copy-done.13
  23.1 0.0 copy-done.10
  23.1 0.0 copy-done.5
  23.1 0.0 copy-done.9
  23.1 0.0 copy-done.11
  23.1 0.0 copy-done.8
  23.2 0.9 shard_map.185
  24.0 0.2 collective-permute-done.3.high
  24.2 0.0 collective-permute-done.2.low
  24.3 5.9 %shard_map.186 = (f32[8,24,128]{2,1,0:T(8,128)}, f32[1,256]{1,0:T(1,128)S(1)}, f32[3,16,256]{2,1,0:T(8,128)S(1)}, f32[8,640]{1,0:T(8,128)S(1)}, f32[8,128,256]{2,1,0:T(8,128)S(1)}, /*index=5*/f32[12,128,256]{2,1,0:T(8,128)}) custom-call(f32[136,128]{1,0:T(8,128)S(1)} %collective-permute-done.left, f32[136,256]{1,0:T(8,128)S(1)} %maximum_maximum_fusion.own, ...), custom_call_target="tpu_custom_call" | custom-call | flops 1000000000 | bytes 2000000 | tf_op jit(solution)/shard_map/pallas_call | solution.py:653
  30.2 6.8 %all-to-all-start = ((f32[8,24,128]{2,1,0:T(8,128)}), f32[8,24,128]{2,1,0:T(8,128)S(1)}, u32[]{:S(2)}, u32[]{:S(2)}) async-start(f32[8,24,128]{2,1,0:T(8,128)} %get-tuple-element.36), calls=%async_computation | async-start | bytes 196608 | tf_op jit(solution)/shard_map/all_to_all | solution.py:762
  37.0 4.1 %shard_map.187 = (f32[48,128]{1,0:T(8,128)S(1)}, f32[48,128]{1,0:T(8,128)S(1)}) custom-call(f32[3,16,256]{2,1,0:T(8,128)S(1)} %get-tuple-element.37.rel, f32[12,128,256]{2,1,0:T(8,128)} %get-tuple-element.44.kept, f32[8,128,256]{2,1,0:T(8,128)S(1)} %get-tuple-element.39.along, s32[12,256]{1,0:T(8,128)S(1)} %copy-done.14, ...), custom_call_target="tpu_custom_call" | custom-call | flops 2000000000 | bytes 2000000 | tf_op jit(solution)/shard_map/pallas_call | solution.py:653
  41.0 0.9 all-to-all-done.rows
  42.0 0.8 shard_map.188
  42.8 12.1 %all-to-all-start.1 = ((f32[64,2,128]{2,1,0:T(2,128)}), f32[64,2,128]{2,1,0:T(2,128)S(1)}, u32[]{:S(2)}, u32[]{:S(2)}) async-start(f32[64,2,128]{2,1,0:T(2,128)} %shard_map.188), calls=%async_computation.1 | async-start | bytes 131072 | tf_op jit(solution)/shard_map/all_to_all | solution.py:767
  54.9 0.0 copy-start
  54.9 0.0 copy-start.1
  54.9 0.0 copy-start.6
  54.9 0.0 copy-start.7
  54.9 3.3 %shard_map.189 = (f32[96,128]{1,0:T(8,128)S(1)}, f32[96,128]{1,0:T(8,128)S(1)}) custom-call(f32[3,16,256]{2,1,0:T(8,128)S(1)} %get-tuple-element.37.rel, f32[12,128,256]{2,1,0:T(8,128)} %get-tuple-element.44.kept, f32[8,128,256]{2,1,0:T(8,128)S(1)} %get-tuple-element.39.along, s32[12,256]{1,0:T(8,128)S(1)} %copy-done.14, ...), custom_call_target="tpu_custom_call" | custom-call | flops 2000000000 | bytes 2000000 | tf_op jit(solution)/shard_map/pallas_call | solution.py:653
  58.2 0.0 copy-start.4
  58.3 10.5 %all-to-all-done.1.planes = f32[64,2,128]{2,1,0:T(2,128)S(1)} async-done(((f32[64,2,128]{2,1,0:T(2,128)}), f32[64,2,128]{2,1,0:T(2,128)S(1)}, u32[]{:S(2)}, u32[]{:S(2)}) %all-to-all-start.1) | async-done | bytes 65568 | tf_op jit(solution)/shard_map/all_to_all | solution.py:767
  68.8 0.0 copy-done
  68.8 1.5 %shard_map.190 = f32[64,2,128]{2,1,0:T(2,128)} custom-call(f32[64,2,128]{2,1,0:T(2,128)S(1)} %all-to-all-done.1.planes, bf16[640,192]{1,0:T(8,128)(2,1)S(1)} %copy-done.1, bf16[448,384]{1,0:T(8,128)(2,1)S(1)} %copy-done, f32[128,128]{1,0:T(8,128)S(1)} %copy-done.6, f32[128,128]{1,0:T(8,128)S(1)} %copy-done.7, f32[1,4,128]{2,1,0:T(4,128)S(1)} %constant_dynamic-slice_fusion.yz), custom_call_target="tpu_custom_call" | custom-call | flops 10000000 | bytes 2000000 | tf_op jit(solution)/shard_map/pallas_call | solution.py:653
  70.3 4.6 %all-to-all-start.2 = ((f32[64,2,128]{2,1,0:T(2,128)}), f32[64,2,128]{2,1,0:T(2,128)S(1)}, u32[]{:S(2)}, u32[]{:S(2)}) async-start(f32[64,2,128]{2,1,0:T(2,128)} %shard_map.190), calls=%async_computation.2 | async-start | bytes 131072 | tf_op jit(solution)/shard_map/all_to_all | solution.py:783
  74.8 6.6 %collective-permute-start.5 = (f32[96,128]{1,0:T(8,128)S(1)}, f32[96,128]{1,0:T(8,128)S(1)}, u32[]{:S(2)}, u32[]{:S(2)}) collective-permute-start(f32[96,128]{1,0:T(8,128)S(1)} %get-tuple-element.47.lower), channel_id=1, source_target_pairs={{0,504},{8,0},{16,8},{24,16},{32,24},{40,32},{48,40},{56,48},{64,5... | collective-permute-start | bytes 147464 | tf_op jit(solution)/shard_map/ppermute | solution.py:666
  81.4 1.9 %collective-permute-start.4 = (f32[96,128]{1,0:T(8,128)S(1)}, f32[96,128]{1,0:T(8,128)S(1)}, u32[]{:S(2)}, u32[]{:S(2)}) collective-permute-start(f32[96,128]{1,0:T(8,128)S(1)} %get-tuple-element.50.upper), channel_id=1, source_target_pairs={{0,8},{8,16},{16,24},{24,32},{32,40},{40,48},{48,56},{56,64},{64,7... | collective-permute-start | bytes 147464 | tf_op jit(solution)/shard_map/ppermute | solution.py:666
  83.3 0.1 fusion.5
  83.4 6.5 %collective-permute-done.4.left = f32[96,128]{1,0:T(8,128)S(1)} collective-permute-done((f32[96,128]{1,0:T(8,128)S(1)}, f32[96,128]{1,0:T(8,128)S(1)}, u32[]{:S(2)}, u32[]{:S(2)}) %collective-permute-start.4) | collective-permute-done | bytes 49184 | tf_op jit(solution)/shard_map/ppermute | solution.py:666
  89.9 0.0 collective-permute-done.5.right
  89.9 0.0 all-to-all-done.2.waves
  89.9 0.1 fusion.4
  90.0 0.1 pad_maximum_fusion.3
  90.1 3.7 %collective-permute-start.7 = (f32[96,64]{1,0:T(8,128)S(1)}, f32[96,64]{1,0:T(8,128)S(1)}, u32[]{:S(2)}, u32[]{:S(2)}) collective-permute-start(f32[96,64]{1,0:T(8,128)S(1)} %pad_maximum_fusion.3), channel_id=1, source_target_pairs={{0,7},{1,0},{2,1},{3,2},{4,3},{5,4},{6,5},{7,6},{8,15},{9,8},{10,9... | collective-permute-start | bytes 73736 | tf_op jit(solution)/shard_map/ppermute | solution.py:666
  93.8 0.0 copy-done.4
  93.8 0.8 shard_map.191
  94.6 3.3 %all-to-all-start.3 = ((f32[8,24,128]{2,1,0:T(8,128)}), f32[8,24,128]{2,1,0:T(8,128)S(1)}, u32[]{:S(2)}, u32[]{:S(2)}) async-start(f32[8,24,128]{2,1,0:T(8,128)} %shard_map.191), calls=%async_computation.3 | async-start | bytes 196608 | tf_op jit(solution)/shard_map/all_to_all | solution.py:788
  98.0 0.1 pad_maximum_fusion.2
  98.1 1.6 %collective-permute-start.6 = (f32[96,64]{1,0:T(8,128)S(1)}, f32[96,64]{1,0:T(8,128)S(1)}, u32[]{:S(2)}, u32[]{:S(2)}) collective-permute-start(f32[96,64]{1,0:T(8,128)S(1)} %pad_maximum_fusion.2), channel_id=1, source_target_pairs={{0,1},{1,2},{2,3},{3,4},{4,5},{5,6},{6,7},{7,0},{8,9},{9,10},{10,1... | collective-permute-start | bytes 73736 | tf_op jit(solution)/shard_map/ppermute | solution.py:666
  99.7 0.6 shard_map.192.waves
  100.3 0.0 collective-permute-done.7.high
  100.3 0.5 collective-permute-done.6.low
  100.9 2.1 %all-to-all-done.3.potential = f32[8,24,128]{2,1,0:T(8,128)S(1)} async-done(((f32[8,24,128]{2,1,0:T(8,128)}), f32[8,24,128]{2,1,0:T(8,128)S(1)}, u32[]{:S(2)}, u32[]{:S(2)}) %all-to-all-start.3) | async-done | bytes 98336 | tf_op jit(solution)/shard_map/all_to_all | solution.py:788
  102.9 2.5 %shard_map.193 = (f32[3,256]{1,0:T(4,128)}, f32[1,1]{1,0:T(1,128)}) custom-call(f32[8,24,128]{2,1,0:T(8,128)S(1)} %all-to-all-done.3.potential, f32[8,640]{1,0:T(8,128)S(1)} %get-tuple-element.52.places, f32[1,256]{1,0:T(1,128)S(1)} %get-tuple-element.53.charge, f32[128,896]{1,0:T(8,128)S(1)} %shard_map.192.waves, ...), custom_call_target="tpu_custom_call" | custom-call | flops 1000000000 | bytes 2000000 | tf_op jit(solution)/shard_map/pallas_call | solution.py:653
  (13 shorter events, 0.0 us)
Async XLA Ops:
  0.6 22.5 %copy-start.2 = (f32[128,128]{1,0:T(8,128)S(1)}, f32[128,128]{1,0:T(8,128)}, u32[]{:S(2)}) copy-start(f32[128,128]{1,0:T(8,128)} %constant.33.clone.z_table) | copy-start | bytes 196612
  0.6 22.5 %copy-start.12 = (f32[128]{0:T(128)S(1)}, f32[128]{0:T(128)}, u32[]{:S(2)}) copy-start(f32[128]{0:T(128)} %param.26) | copy-start | bytes 1540
  0.7 22.4 %copy-start.13 = (f32[128]{0:T(128)S(1)}, f32[128]{0:T(128)}, u32[]{:S(2)}) copy-start(f32[128]{0:T(128)} %param.27) | copy-start | bytes 1540
  0.7 22.4 %copy-start.10 = (f32[64,8]{0,1:T(8,128)S(1)}, f32[64,8]{0,1:T(8,128)}, u32[]{:S(2)}) copy-start(f32[64,8]{0,1:T(8,128)} %param.22) | copy-start | bytes 6148
  0.7 22.4 %copy-start.5 = (f32[384,64]{0,1:T(8,128)S(1)}, f32[384,64]{0,1:T(8,128)}, u32[]{:S(2)}) copy-start(f32[384,64]{0,1:T(8,128)} %param.23) | copy-start | bytes 294916
  0.7 22.4 %copy-start.9 = (f32[128,128]{1,0:T(8,128)S(1)}, f32[128,128]{1,0:T(8,128)}, u32[]{:S(2)}) copy-start(f32[128,128]{1,0:T(8,128)} %up_weight.1) | copy-start | bytes 196612
  0.7 22.4 %copy-start.11 = (f32[2,128]{1,0:T(2,128)S(1)}, f32[2,128]{1,0:T(2,128)}, u32[]{:S(2)}) copy-start(f32[2,128]{1,0:T(2,128)} %coupling.1) | copy-start | bytes 3076
  0.7 22.4 %copy-start.8 = (f32[128,128]{1,0:T(8,128)S(1)}, f32[128,128]{1,0:T(8,128)}, u32[]{:S(2)}) copy-start(f32[128,128]{1,0:T(8,128)} %mix_weight.1) | copy-start | bytes 196612
  0.7 23.5 %copy-start.14 = (s32[12,256]{1,0:T(8,128)S(1)}, s32[12,256]{1,0:T(8,128)}, u32[]{:S(2)}) copy-start(s32[12,256]{1,0:T(8,128)} %codes.5) | copy-start | bytes 36868
  1.9 16.2 %collective-permute-start = (f32[136,128]{1,0:T(8,128)S(1)}, f32[136,128]{1,0:T(8,128)S(1)}, u32[]{:S(2)}, u32[]{:S(2)}) collective-permute-start(f32[136,128]{1,0:T(8,128)S(1)} %get-tuple-element.63), channel_id=1, source_target_pairs={{0,8},{8,16},{16,24},{24,32},{32,40},{40,48},{48,56},{56,64},{64,7... | collective-permute-start | bytes 208904 | tf_op jit(solution)/shard_map/ppermute | solution.py:666
  5.8 13.5 %collective-permute-start.1 = (f32[136,128]{1,0:T(8,128)S(1)}, f32[136,128]{1,0:T(8,128)S(1)}, u32[]{:S(2)}, u32[]{:S(2)}) collective-permute-start(f32[136,128]{1,0:T(8,128)S(1)} %get-tuple-element.62), channel_id=1, source_target_pairs={{0,504},{8,0},{16,8},{24,16},{32,24},{40,32},{48,40},{56,48},{64,5... | collective-permute-start | bytes 208904 | tf_op jit(solution)/shard_map/ppermute | solution.py:666
  19.5 4.7 %collective-permute-start.3 = (f32[136,64]{1,0:T(8,128)S(1)}, f32[136,64]{1,0:T(8,128)S(1)}, u32[]{:S(2)}, u32[]{:S(2)}) collective-permute-start(f32[136,64]{1,0:T(8,128)S(1)} %pad_maximum_fusion.1), channel_id=1, source_target_pairs={{0,7},{1,0},{2,1},{3,2},{4,3},{5,4},{6,5},{7,6},{8,15},{9,8},{10,9... | collective-permute-start | bytes 104456 | tf_op jit(solution)/shard_map/ppermute | solution.py:666
  21.2 3.1 %collective-permute-start.2 = (f32[136,64]{1,0:T(8,128)S(1)}, f32[136,64]{1,0:T(8,128)S(1)}, u32[]{:S(2)}, u32[]{:S(2)}) collective-permute-start(f32[136,64]{1,0:T(8,128)S(1)} %pad_maximum_fusion), channel_id=1, source_target_pairs={{0,1},{1,2},{2,3},{3,4},{4,5},{5,6},{6,7},{7,0},{8,9},{9,10},{10,1... | collective-permute-start | bytes 104456 | tf_op jit(solution)/shard_map/ppermute | solution.py:666
  30.2 11.8 %all-to-all-start = ((f32[8,24,128]{2,1,0:T(8,128)}), f32[8,24,128]{2,1,0:T(8,128)S(1)}, u32[]{:S(2)}, u32[]{:S(2)}) async-start(f32[8,24,128]{2,1,0:T(8,128)} %get-tuple-element.36), calls=%async_computation | async-start | bytes 196608 | tf_op jit(solution)/shard_map/all_to_all | solution.py:762
  37.0 5.0 %copy-start.3 = (bf16[128,576]{1,0:T(8,128)(2,1)S(1)}, bf16[128,576]{1,0:T(8,128)(2,1)}, u32[]{:S(2)}) copy-start(bf16[128,576]{1,0:T(8,128)(2,1)} %constant.34.clone.table) | copy-start | bytes 442372
  42.8 26.0 %all-to-all-start.1 = ((f32[64,2,128]{2,1,0:T(2,128)}), f32[64,2,128]{2,1,0:T(2,128)S(1)}, u32[]{:S(2)}, u32[]{:S(2)}) async-start(f32[64,2,128]{2,1,0:T(2,128)} %shard_map.188), calls=%async_computation.1 | async-start | bytes 131072 | tf_op jit(solution)/shard_map/all_to_all | solution.py:767
  54.9 13.9 %copy-start = (bf16[448,384]{1,0:T(8,128)(2,1)S(1)}, bf16[448,384]{1,0:T(8,128)(2,1)}, u32[]{:S(2)}) copy-start(bf16[448,384]{1,0:T(8,128)(2,1)} %constant.37.clone.x_out) | copy-start | bytes 1032196
  54.9 13.9 %copy-start.1 = (bf16[640,192]{1,0:T(8,128)(2,1)S(1)}, bf16[640,192]{1,0:T(8,128)(2,1)}, u32[]{:S(2)}) copy-start(bf16[640,192]{1,0:T(8,128)(2,1)} %constant.36.clone.x_in) | copy-start | bytes 737284
  54.9 13.9 %copy-start.6 = (f32[128,128]{1,0:T(8,128)S(1)}, f32[128,128]{1,0:T(8,128)}, u32[]{:S(2)}) copy-start(f32[128,128]{1,0:T(8,128)} %constant.38.clone.x_gain) | copy-start | bytes 196612
  54.9 13.8 %copy-start.7 = (f32[128,128]{1,0:T(8,128)S(1)}, f32[128,128]{1,0:T(8,128)}, u32[]{:S(2)}) copy-start(f32[128,128]{1,0:T(8,128)} %constant.39.clone.x_square) | copy-start | bytes 196612
  58.2 35.5 %copy-start.4 = (bf16[192,384]{1,0:T(8,128)(2,1)S(1)}, bf16[192,384]{1,0:T(8,128)(2,1)}, u32[]{:S(2)}) copy-start(bf16[192,384]{1,0:T(8,128)(2,1)} %constant.35.clone.table) | copy-start | bytes 442372
  70.3 19.6 %all-to-all-start.2 = ((f32[64,2,128]{2,1,0:T(2,128)}), f32[64,2,128]{2,1,0:T(2,128)S(1)}, u32[]{:S(2)}, u32[]{:S(2)}) async-start(f32[64,2,128]{2,1,0:T(2,128)} %shard_map.190), calls=%async_computation.2 | async-start | bytes 131072 | tf_op jit(solution)/shard_map/all_to_all | solution.py:783
  74.8 15.1 %collective-permute-start.5 = (f32[96,128]{1,0:T(8,128)S(1)}, f32[96,128]{1,0:T(8,128)S(1)}, u32[]{:S(2)}, u32[]{:S(2)}) collective-permute-start(f32[96,128]{1,0:T(8,128)S(1)} %get-tuple-element.47.lower), channel_id=1, source_target_pairs={{0,504},{8,0},{16,8},{24,16},{32,24},{40,32},{48,40},{56,48},{64,5... | collective-permute-start | bytes 147464 | tf_op jit(solution)/shard_map/ppermute | solution.py:666
  81.4 8.5 %collective-permute-start.4 = (f32[96,128]{1,0:T(8,128)S(1)}, f32[96,128]{1,0:T(8,128)S(1)}, u32[]{:S(2)}, u32[]{:S(2)}) collective-permute-start(f32[96,128]{1,0:T(8,128)S(1)} %get-tuple-element.50.upper), channel_id=1, source_target_pairs={{0,8},{8,16},{16,24},{24,32},{32,40},{40,48},{48,56},{56,64},{64,7... | collective-permute-start | bytes 147464 | tf_op jit(solution)/shard_map/ppermute | solution.py:666
  90.1 10.2 %collective-permute-start.7 = (f32[96,64]{1,0:T(8,128)S(1)}, f32[96,64]{1,0:T(8,128)S(1)}, u32[]{:S(2)}, u32[]{:S(2)}) collective-permute-start(f32[96,64]{1,0:T(8,128)S(1)} %pad_maximum_fusion.3), channel_id=1, source_target_pairs={{0,7},{1,0},{2,1},{3,2},{4,3},{5,4},{6,5},{7,6},{8,15},{9,8},{10,9... | collective-permute-start | bytes 73736 | tf_op jit(solution)/shard_map/ppermute | solution.py:666
  94.6 8.3 %all-to-all-start.3 = ((f32[8,24,128]{2,1,0:T(8,128)}), f32[8,24,128]{2,1,0:T(8,128)S(1)}, u32[]{:S(2)}, u32[]{:S(2)}) async-start(f32[8,24,128]{2,1,0:T(8,128)} %shard_map.191), calls=%async_computation.3 | async-start | bytes 196608 | tf_op jit(solution)/shard_map/all_to_all | solution.py:788
  98.1 2.8 %collective-permute-start.6 = (f32[96,64]{1,0:T(8,128)S(1)}, f32[96,64]{1,0:T(8,128)S(1)}, u32[]{:S(2)}, u32[]{:S(2)}) collective-permute-start(f32[96,64]{1,0:T(8,128)S(1)} %pad_maximum_fusion.2), channel_id=1, source_target_pairs={{0,1},{1,2},{2,3},{3,4},{4,5},{5,6},{6,7},{7,0},{8,9},{9,10},{10,1... | collective-permute-start | bytes 73736 | tf_op jit(solution)/shard_map/ppermute | solution.py:666

commit v4 on v3

--- a/solution.py
+++ b/solution.py
@@ -302,7 +302,7 @@
     pltpu.VMEM((8, 16, ATOM), f32),
     pltpu.VMEM((K, 3 * C, ATOM), f32),
     pltpu.VMEM((K, C, ATOM), f32),
-    pltpu.SemaphoreType.DMA((1,)),
+    pltpu.SemaphoreType.DMA((4,)),
 ]
 
 
@@ -346,15 +346,17 @@
     )
     target, wrap = edge_targets(padded)
     target_ref[...] = target
+    keep = []
     for k in range(K):
         found = dot(split[...], one_hot(target_ref, slot(k), EXT))
         up[k] = found[0:C] + found[C : 2 * C]
         place = found[256:264] + found[264:272] + found[272:280]
         for c in range(3):
             rel[c, slot(k) : slot(k) + 1, :] = place[c : c + 1]
-
-    keep_up = pltpu.make_async_copy(up, kept, sems.at[0])
-    keep_up.start()
+        if k % 3 == 2:
+            some = slice(k - 2, k + 1)
+            keep.append(pltpu.make_async_copy(up.at[some], kept.at[some], sems.at[k // 3]))
+            keep[-1].start()
 
     rel_x = rel[0] - own_pos[0:1]
     rel_y = rel[1] - own_pos[1:2]
@@ -403,7 +405,7 @@
             )
 
         zero = jnp.zeros((8, 128), f32)
-        sites, charges = lax.fori_loop(0, 16, accumulate, (zero, zero))
+        sites, charges = lax.fori_loop(0, 16, accumulate, (zero, zero), unroll=16)
         site = site + sites
         charge.append(jnp.sum(charges, axis=0, keepdims=True))
     charge = jnp.concatenate(charge, axis=1)
@@ -424,7 +426,8 @@
             moved = pltpu.roll(moved, amount, 1) if amount else moved
             part = jnp.where((lane >> 4) == p, moved, part)
         spread[g] = part
-    keep_up.wait()
+    for copy in keep:
+        copy.wait()
 
 
 def y_in_kernel(rows, table, out):
@@ -478,7 +481,7 @@
     pltpu.VMEM((HALF, 3 * C, ATOM), f32),
     pltpu.VMEM((HALF, 24, ATOM), f32),
     pltpu.VMEM((HALF, C, ATOM), f32),
-    pltpu.SemaphoreType.DMA((1,)),
+    pltpu.SemaphoreType.DMA((3,)),
 ]
 
 
@@ -491,8 +494,12 @@
     base = 8 * k0
     for done, plane in zip(before_planes, planes):
         plane[0:base, :] = done[...]
-    fetch_up = pltpu.make_async_copy(kept.at[k0 : k0 + HALF], up, sems.at[0])
-    fetch_up.start()
+    fetch = [
+        pltpu.make_async_copy(kept.at[k0 + k : k0 + k + 2], up.at[k : k + 2], sems.at[k // 2])
+        for k in range(0, HALF, 2)
+    ]
+    for copy in fetch:
+        copy.start()
     first = slot(k0)
     inv, ux, uy, uz = geometry(
         *(rel[c, first : first + 8, :] for c in range(3)), harm, basis, basis_slope
@@ -506,7 +513,8 @@
         radial[k] = layered(out_wide, hidden[RH * k : RH * k + RH])
         radial_slope[k] = layered(out_wide, hidden_slope[RH * k : RH * k + RH])
 
-    fetch_up.wait()
+    for copy in fetch:
+        copy.wait()
     for half in range(2):
         spots = slice(128 * half, 128 * half + 128)
 
@@ -564,7 +572,8 @@
 def reach_kernel(places, z_table, out):
     weights, slopes = spline_rows(places[2:3, :], 0, NZ, True)
     both = jnp.concatenate([weights, slopes[:, 128:384]], axis=1)
-    out[...] = dot(z_table[...], both, highest)
+    high, low = halves(dot(z_table[...], both, highest))
+    out[...] = jnp.concatenate([high, low, high], axis=0).astype(bf16)
 
 
 def final_kernel(
@@ -601,7 +610,7 @@
             moved = pltpu.roll(potential[g], amount, 1) if amount else potential[g]
             plane = jnp.where((lane >> 4) == g, moved, plane)
         planes.append(plane)
-    felt = dot(jnp.concatenate(planes, axis=0), waves[...], highest)
+    felt = dot(beside(jnp.concatenate(planes, axis=0)), waves[...])
     phi = jnp.zeros((1, EXT), f32)
     slope = [jnp.zeros((1, ATOM), f32)] * 3
     for p in range(PLANES):
@@ -622,21 +631,34 @@
         ]
         for i in (0, 48)
     ]
-    table = jnp.zeros((16, ATOM), f32)
+    part = lax.broadcasted_iota(jnp.int32, (16, EXT), 0)
+    table = jnp.zeros((96, 16), f32)
     for k in range(K):
         rows = jnp.concatenate(
             [total[k // HALF][c][k % HALF : k % HALF + 1, :] for c in range(3)]
             + [jnp.zeros((5, EXT), f32)],
             axis=0,
         )
-        top, rest = halves(rows)
-        both = jnp.concatenate([top, rest], axis=0).astype(bf16)
-        table = table + dot_nt(both, one_hot(target_ref, k, ATOM))
+        target = target_ref[k : k + 1, :]
+        here = part == (target >> 4)
+        by_row = [
+            jnp.where(here, x[c : c + 1, :], 0.0) for x in halves(rows) for c in range(3)
+        ]
+        by_site = jnp.where(part == (target & 15), 1.0, 0.0).astype(bf16)
+        table = table + dot_nt(jnp.concatenate(by_row, axis=0).astype(bf16), by_site)
+    table = table[0:48] + table[48:96]
+    table = jnp.concatenate([table, jnp.zeros((48, 112), f32)], axis=1)
     for c in range(3):
+        ends = []
+        for plane in range(2):
+            lanes = table[16 * c + 8 * plane : 16 * c + 8 * plane + 1]
+            for a in range(1, 8):
+                row = 16 * c + 8 * plane + a
+                lanes = lanes + pltpu.roll(table[row : row + 1], 16 * a, 1)
+            ends.append(lanes)
         forces[c : c + 1, :] = (
             jnp.sum(total[0][c][0:HALF, mine] + total[1][c][0:HALF, mine], axis=0, keepdims=True)
-            - table[c : c + 1]
-            - table[8 + c : 9 + c]
+            - jnp.concatenate(ends, axis=1)
             - charge[...] * slope[c]
         )
 
@@ -779,7 +801,7 @@
         table["x_square"],
         yz,
     )
-    reach = call(reach_kernel, struct(NZ, EXT + ATOM), [], 10**8, places, table["z"])
+    reach = call(reach_kernel, struct(3 * NZ, EXT + ATOM, dtype=bf16), [], 10**8, places, table["z"])
     waves = lax.all_to_all(waves, "gx", split_axis=0, concat_axis=0, tiled=True)
     left, right = plane_ghosts(lower, upper)
     waves, left, right = lax.optimization_barrier((waves, left, right))

time: 106 us -> 105 us (level)
  Pallas kernels: 20.5 us -> 19.4 us
  transfers between devices with their start and end apart: 12 -> 12, of which waited for: 7 -> 7; matrix products, arithmetic and copies ran while one was open for 1% -> 1% of each run, Pallas kernels for 9% -> 10%
where the time goes in v4:
time: 105 us; the launch traced here: 104 us
  starting transfers between devices  59.3 us (56%)
  waiting for transfers between devices  21.4 us (20%)
  Pallas kernels  19.4 us (18%)
  other arithmetic  1.51 us (1%)
  local copies, waits for them, and re-layouts  1.27 us (1%)
    ppermute x8, starting transfers between devices, passed_along(): lax.ppermute(array, axis, [(i, (i + by) % devices) for i in range(devices)])  32.6 us
    pallas_call x9, Pallas kernels, call(): pl.pallas_call(kernel, out_shape=outs, in_specs=[far if i in far_in else...  19.4 us
    all_to_all x1, starting transfers between devices, shards(): lax.all_to_all(waves, 'gx', split_axis=0, concat_axis=0, tiled=True)  12.1 us
    all_to_all x1, waiting for transfers between devices, shards(): lax.all_to_all(waves, 'gx', split_axis=0, concat_axis=0, tiled=True)  9.83 us
    ppermute x8, waiting for transfers between devices, passed_along(): lax.ppermute(array, axis, [(i, (i + by) % devices) for i in range(devices)])  8.4 us
    all_to_all x1, starting transfers between devices, shards(): rows = lax.all_to_all(spread, 'gy', split_axis=0, concat_axis=0, tiled=True)  6.78 us
    all_to_all x1, starting transfers between devices, shards(): waves = lax.all_to_all(waves, 'gx', split_axis=0, concat_axis=0, tiled=True)  4.56 us
    all_to_all x1, starting transfers between devices, shards(): lax.all_to_all(rows, 'gy', split_axis=0, concat_axis=0, tiled=True)  3.31 us
  transfers between devices with their start and end apart: 12, of which 7 were waited for; matrix products, arithmetic and copies ran while one was open for 1% of the time, Pallas kernels for 10%

profile of v4, /device:TPU:1, one launch (start us, length us, event | category | flops | bytes accessed | tf_op | source)
XLA Modules:
  0.0 103.9 jit_solution(13174130719264284458)
XLA Ops:
  0.6 0.0 copy-start.2
  0.6 0.0 copy-start.12
  0.7 0.0 copy-start.13
  0.7 0.0 copy-start.10
  0.7 0.0 copy-start.5
  0.7 0.0 copy-start.9
  0.7 0.0 copy-start.11
  0.7 0.0 copy-start.8
  0.7 0.1 pad.18.clone
  0.8 1.0 %maximum_maximum_fusion.own = f32[136,256]{1,0:T(8,128)S(1)} fusion(f32[3,256]{1,0:T(4,128)} %param.18, f32[128,256]{1,0:T(8,128)} %param.19, f32[136]{0:T(256)S(1)} %pad.18.clone), kind=kLoop, calls=%fused_computation | loop fusion | flops 69632 | bytes 273952 | tf_op jit(solution)/shard_map/concatenate | solution.py:710
  1.9 3.9 %collective-permute-start = (f32[136,128]{1,0:T(8,128)S(1)}, f32[136,128]{1,0:T(8,128)S(1)}, u32[]{:S(2)}, u32[]{:S(2)}) collective-permute-start(f32[136,128]{1,0:T(8,128)S(1)} %get-tuple-element.63), channel_id=1, source_target_pairs={{0,8},{8,16},{16,24},{24,32},{32,40},{40,48},{48,56},{56,64},{64,7... | collective-permute-start | bytes 208904 | tf_op jit(solution)/shard_map/ppermute | solution.py:688
  5.8 12.1 %collective-permute-start.1 = (f32[136,128]{1,0:T(8,128)S(1)}, f32[136,128]{1,0:T(8,128)S(1)}, u32[]{:S(2)}, u32[]{:S(2)}) collective-permute-start(f32[136,128]{1,0:T(8,128)S(1)} %get-tuple-element.62), channel_id=1, source_target_pairs={{0,504},{8,0},{16,8},{24,16},{32,24},{40,32},{48,40},{56,48},{64,5... | collective-permute-start | bytes 208904 | tf_op jit(solution)/shard_map/ppermute | solution.py:688
  18.0 0.1 fusion
  18.1 0.0 collective-permute-done.left
  18.1 0.1 fusion.2
  18.2 1.1 %collective-permute-done.1.right = f32[136,128]{1,0:T(8,128)S(1)} collective-permute-done((f32[136,128]{1,0:T(8,128)S(1)}, f32[136,128]{1,0:T(8,128)S(1)}, u32[]{:S(2)}, u32[]{:S(2)}) %collective-permute-start.1) | collective-permute-done | bytes 69664 | tf_op jit(solution)/shard_map/ppermute | solution.py:688
  19.3 0.1 fusion.3
  19.4 0.1 pad_maximum_fusion.1
  19.5 1.5 %collective-permute-start.3 = (f32[136,64]{1,0:T(8,128)S(1)}, f32[136,64]{1,0:T(8,128)S(1)}, u32[]{:S(2)}, u32[]{:S(2)}) collective-permute-start(f32[136,64]{1,0:T(8,128)S(1)} %pad_maximum_fusion.1), channel_id=1, source_target_pairs={{0,7},{1,0},{2,1},{3,2},{4,3},{5,4},{6,5},{7,6},{8,15},{9,8},{10,9... | collective-permute-start | bytes 104456 | tf_op jit(solution)/shard_map/ppermute | solution.py:688
  21.1 0.1 pad_maximum_fusion
  21.2 1.2 %collective-permute-start.2 = (f32[136,64]{1,0:T(8,128)S(1)}, f32[136,64]{1,0:T(8,128)S(1)}, u32[]{:S(2)}, u32[]{:S(2)}) collective-permute-start(f32[136,64]{1,0:T(8,128)S(1)} %pad_maximum_fusion), channel_id=1, source_target_pairs={{0,1},{1,2},{2,3},{3,4},{4,5},{5,6},{6,7},{7,0},{8,9},{9,10},{10,1... | collective-permute-start | bytes 104456 | tf_op jit(solution)/shard_map/ppermute | solution.py:688
  22.4 0.7 constant_dynamic-slice_fusion.yz
  23.1 0.0 copy-done.10
  23.1 0.0 copy-done.5
  23.1 0.0 copy-done.9
  23.1 0.0 copy-done.11
  23.1 0.0 copy-done.8
  23.2 0.9 shard_map.185
  24.0 0.2 collective-permute-done.3.high
  24.2 0.0 collective-permute-done.2.low
  24.3 5.1 %shard_map.186 = (f32[8,24,128]{2,1,0:T(8,128)}, f32[1,256]{1,0:T(1,128)S(1)}, f32[3,16,256]{2,1,0:T(8,128)S(1)}, f32[8,640]{1,0:T(8,128)S(1)}, f32[8,128,256]{2,1,0:T(8,128)S(1)}, /*index=5*/f32[12,128,256]{2,1,0:T(8,128)}) custom-call(f32[136,128]{1,0:T(8,128)S(1)} %collective-permute-done.left, f32[136,256]{1,0:T(8,128)S(1)} %maximum_maximum_fusion.own, ...), custom_call_target="tpu_custom_call" | custom-call | flops 1000000000 | bytes 2000000 | tf_op jit(solution)/shard_map/pallas_call | solution.py:675
  29.3 6.8 %all-to-all-start = ((f32[8,24,128]{2,1,0:T(8,128)}), f32[8,24,128]{2,1,0:T(8,128)S(1)}, u32[]{:S(2)}, u32[]{:S(2)}) async-start(f32[8,24,128]{2,1,0:T(8,128)} %get-tuple-element.36), calls=%async_computation | async-start | bytes 196608 | tf_op jit(solution)/shard_map/all_to_all | solution.py:784
  36.1 3.9 %shard_map.187 = (f32[48,128]{1,0:T(8,128)S(1)}, f32[48,128]{1,0:T(8,128)S(1)}) custom-call(f32[3,16,256]{2,1,0:T(8,128)S(1)} %get-tuple-element.37.rel, f32[12,128,256]{2,1,0:T(8,128)} %get-tuple-element.44.kept, f32[8,128,256]{2,1,0:T(8,128)S(1)} %get-tuple-element.39.along, s32[12,256]{1,0:T(8,128)S(1)} %copy-done.14, ...), custom_call_target="tpu_custom_call" | custom-call | flops 2000000000 | bytes 2000000 | tf_op jit(solution)/shard_map/pallas_call | solution.py:675
  40.0 1.1 %all-to-all-done.rows = f32[8,24,128]{2,1,0:T(8,128)S(1)} async-done(((f32[8,24,128]{2,1,0:T(8,128)}), f32[8,24,128]{2,1,0:T(8,128)S(1)}, u32[]{:S(2)}, u32[]{:S(2)}) %all-to-all-start) | async-done | bytes 98336 | tf_op jit(solution)/shard_map/all_to_all | solution.py:784
  41.1 0.8 shard_map.188
  41.9 12.1 %all-to-all-start.1 = ((f32[64,2,128]{2,1,0:T(2,128)}), f32[64,2,128]{2,1,0:T(2,128)S(1)}, u32[]{:S(2)}, u32[]{:S(2)}) async-start(f32[64,2,128]{2,1,0:T(2,128)} %shard_map.188), calls=%async_computation.1 | async-start | bytes 131072 | tf_op jit(solution)/shard_map/all_to_all | solution.py:789
  54.0 0.0 copy-start
  54.0 0.0 copy-start.1
  54.1 0.0 copy-start.6
  54.1 0.0 copy-start.7
  54.1 4.0 %shard_map.189 = (f32[96,128]{1,0:T(8,128)S(1)}, f32[96,128]{1,0:T(8,128)S(1)}) custom-call(f32[3,16,256]{2,1,0:T(8,128)S(1)} %get-tuple-element.37.rel, f32[12,128,256]{2,1,0:T(8,128)} %get-tuple-element.44.kept, f32[8,128,256]{2,1,0:T(8,128)S(1)} %get-tuple-element.39.along, s32[12,256]{1,0:T(8,128)S(1)} %copy-done.14, ...), custom_call_target="tpu_custom_call" | custom-call | flops 2000000000 | bytes 2000000 | tf_op jit(solution)/shard_map/pallas_call | solution.py:675
  58.1 0.0 copy-start.4
  58.1 9.8 %all-to-all-done.1.planes = f32[64,2,128]{2,1,0:T(2,128)S(1)} async-done(((f32[64,2,128]{2,1,0:T(2,128)}), f32[64,2,128]{2,1,0:T(2,128)S(1)}, u32[]{:S(2)}, u32[]{:S(2)}) %all-to-all-start.1) | async-done | bytes 65568 | tf_op jit(solution)/shard_map/all_to_all | solution.py:789
  67.9 0.0 copy-done.1
  67.9 1.5 %shard_map.190 = f32[64,2,128]{2,1,0:T(2,128)} custom-call(f32[64,2,128]{2,1,0:T(2,128)S(1)} %all-to-all-done.1.planes, bf16[640,192]{1,0:T(8,128)(2,1)S(1)} %copy-done.1, bf16[448,384]{1,0:T(8,128)(2,1)S(1)} %copy-done, f32[128,128]{1,0:T(8,128)S(1)} %copy-done.6, f32[128,128]{1,0:T(8,128)S(1)} %copy-done.7, f32[1,4,128]{2,1,0:T(4,128)S(1)} %constant_dynamic-slice_fusion.yz), custom_call_target="tpu_custom_call" | custom-call | flops 10000000 | bytes 2000000 | tf_op jit(solution)/shard_map/pallas_call | solution.py:675
  69.4 4.6 %all-to-all-start.2 = ((f32[64,2,128]{2,1,0:T(2,128)}), f32[64,2,128]{2,1,0:T(2,128)S(1)}, u32[]{:S(2)}, u32[]{:S(2)}) async-start(f32[64,2,128]{2,1,0:T(2,128)} %shard_map.190), calls=%async_computation.2 | async-start | bytes 131072 | tf_op jit(solution)/shard_map/all_to_all | solution.py:805
  74.0 6.6 %collective-permute-start.5 = (f32[96,128]{1,0:T(8,128)S(1)}, f32[96,128]{1,0:T(8,128)S(1)}, u32[]{:S(2)}, u32[]{:S(2)}) collective-permute-start(f32[96,128]{1,0:T(8,128)S(1)} %get-tuple-element.47.lower), channel_id=1, source_target_pairs={{0,504},{8,0},{16,8},{24,16},{32,24},{40,32},{48,40},{56,48},{64,5... | collective-permute-start | bytes 147464 | tf_op jit(solution)/shard_map/ppermute | solution.py:688
  80.5 1.9 %collective-permute-start.4 = (f32[96,128]{1,0:T(8,128)S(1)}, f32[96,128]{1,0:T(8,128)S(1)}, u32[]{:S(2)}, u32[]{:S(2)}) collective-permute-start(f32[96,128]{1,0:T(8,128)S(1)} %get-tuple-element.50.upper), channel_id=1, source_target_pairs={{0,8},{8,16},{16,24},{24,32},{32,40},{40,48},{48,56},{56,64},{64,7... | collective-permute-start | bytes 147464 | tf_op jit(solution)/shard_map/ppermute | solution.py:688
  82.5 0.1 fusion.5
  82.6 6.5 %collective-permute-done.4.left = f32[96,128]{1,0:T(8,128)S(1)} collective-permute-done((f32[96,128]{1,0:T(8,128)S(1)}, f32[96,128]{1,0:T(8,128)S(1)}, u32[]{:S(2)}, u32[]{:S(2)}) %collective-permute-start.4) | collective-permute-done | bytes 49184 | tf_op jit(solution)/shard_map/ppermute | solution.py:688
  89.0 0.0 collective-permute-done.5.right
  89.0 0.0 all-to-all-done.2.waves
  89.0 0.1 fusion.4
  89.1 0.1 pad_maximum_fusion.3
  89.2 3.7 %collective-permute-start.7 = (f32[96,64]{1,0:T(8,128)S(1)}, f32[96,64]{1,0:T(8,128)S(1)}, u32[]{:S(2)}, u32[]{:S(2)}) collective-permute-start(f32[96,64]{1,0:T(8,128)S(1)} %pad_maximum_fusion.3), channel_id=1, source_target_pairs={{0,7},{1,0},{2,1},{3,2},{4,3},{5,4},{6,5},{7,6},{8,15},{9,8},{10,9... | collective-permute-start | bytes 73736 | tf_op jit(solution)/shard_map/ppermute | solution.py:688
  92.9 0.8 shard_map.191
  93.8 3.3 %all-to-all-start.3 = ((f32[8,24,128]{2,1,0:T(8,128)}), f32[8,24,128]{2,1,0:T(8,128)S(1)}, u32[]{:S(2)}, u32[]{:S(2)}) async-start(f32[8,24,128]{2,1,0:T(8,128)} %shard_map.191), calls=%async_computation.3 | async-start | bytes 196608 | tf_op jit(solution)/shard_map/all_to_all | solution.py:810
  97.1 0.1 pad_maximum_fusion.2
  97.2 1.6 %collective-permute-start.6 = (f32[96,64]{1,0:T(8,128)S(1)}, f32[96,64]{1,0:T(8,128)S(1)}, u32[]{:S(2)}, u32[]{:S(2)}) collective-permute-start(f32[96,64]{1,0:T(8,128)S(1)} %pad_maximum_fusion.2), channel_id=1, source_target_pairs={{0,1},{1,2},{2,3},{3,4},{4,5},{5,6},{6,7},{7,0},{8,9},{9,10},{10,1... | collective-permute-start | bytes 73736 | tf_op jit(solution)/shard_map/ppermute | solution.py:688
  98.8 0.6 shard_map.192.waves
  99.5 0.0 collective-permute-done.7.high
  99.5 0.5 collective-permute-done.6.low
  100.0 2.1 %all-to-all-done.3.potential = f32[8,24,128]{2,1,0:T(8,128)S(1)} async-done(((f32[8,24,128]{2,1,0:T(8,128)}), f32[8,24,128]{2,1,0:T(8,128)S(1)}, u32[]{:S(2)}, u32[]{:S(2)}) %all-to-all-start.3) | async-done | bytes 98336 | tf_op jit(solution)/shard_map/all_to_all | solution.py:810
  102.1 1.9 %shard_map.193 = (f32[3,256]{1,0:T(4,128)}, f32[1,1]{1,0:T(1,128)}) custom-call(f32[8,24,128]{2,1,0:T(8,128)S(1)} %all-to-all-done.3.potential, f32[8,640]{1,0:T(8,128)S(1)} %get-tuple-element.52.places, f32[1,256]{1,0:T(1,128)S(1)} %get-tuple-element.53.charge, bf16[384,896]{1,0:T(8,128)(2,1)S(1)} %shard_map.192.waves, ...), custom_call_target="tpu_custom_call" | custom-call | flops 1000000000 | bytes 2000000 | tf_op jit(solution)/shard_map/pallas_call | solution.py:675
  (13 shorter events, 0.0 us)
Async XLA Ops:
  0.6 22.5 %copy-start.2 = (f32[128,128]{1,0:T(8,128)S(1)}, f32[128,128]{1,0:T(8,128)}, u32[]{:S(2)}) copy-start(f32[128,128]{1,0:T(8,128)} %constant.33.clone.z_table) | copy-start | bytes 196612
  0.6 22.5 %copy-start.12 = (f32[128]{0:T(128)S(1)}, f32[128]{0:T(128)}, u32[]{:S(2)}) copy-start(f32[128]{0:T(128)} %param.26) | copy-start | bytes 1540
  0.7 22.4 %copy-start.13 = (f32[128]{0:T(128)S(1)}, f32[128]{0:T(128)}, u32[]{:S(2)}) copy-start(f32[128]{0:T(128)} %param.27) | copy-start | bytes 1540
  0.7 22.4 %copy-start.10 = (f32[64,8]{0,1:T(8,128)S(1)}, f32[64,8]{0,1:T(8,128)}, u32[]{:S(2)}) copy-start(f32[64,8]{0,1:T(8,128)} %param.22) | copy-start | bytes 6148
  0.7 22.4 %copy-start.5 = (f32[384,64]{0,1:T(8,128)S(1)}, f32[384,64]{0,1:T(8,128)}, u32[]{:S(2)}) copy-start(f32[384,64]{0,1:T(8,128)} %param.23) | copy-start | bytes 294916
  0.7 22.4 %copy-start.9 = (f32[128,128]{1,0:T(8,128)S(1)}, f32[128,128]{1,0:T(8,128)}, u32[]{:S(2)}) copy-start(f32[128,128]{1,0:T(8,128)} %up_weight.1) | copy-start | bytes 196612
  0.7 22.4 %copy-start.11 = (f32[2,128]{1,0:T(2,128)S(1)}, f32[2,128]{1,0:T(2,128)}, u32[]{:S(2)}) copy-start(f32[2,128]{1,0:T(2,128)} %coupling.1) | copy-start | bytes 3076
  0.7 22.4 %copy-start.8 = (f32[128,128]{1,0:T(8,128)S(1)}, f32[128,128]{1,0:T(8,128)}, u32[]{:S(2)}) copy-start(f32[128,128]{1,0:T(8,128)} %mix_weight.1) | copy-start | bytes 196612
  0.7 23.5 %copy-start.14 = (s32[12,256]{1,0:T(8,128)S(1)}, s32[12,256]{1,0:T(8,128)}, u32[]{:S(2)}) copy-start(s32[12,256]{1,0:T(8,128)} %codes.5) | copy-start | bytes 36868
  1.9 16.2 %collective-permute-start = (f32[136,128]{1,0:T(8,128)S(1)}, f32[136,128]{1,0:T(8,128)S(1)}, u32[]{:S(2)}, u32[]{:S(2)}) collective-permute-start(f32[136,128]{1,0:T(8,128)S(1)} %get-tuple-element.63), channel_id=1, source_target_pairs={{0,8},{8,16},{16,24},{24,32},{32,40},{40,48},{48,56},{56,64},{64,7... | collective-permute-start | bytes 208904 | tf_op jit(solution)/shard_map/ppermute | solution.py:688
  5.8 13.5 %collective-permute-start.1 = (f32[136,128]{1,0:T(8,128)S(1)}, f32[136,128]{1,0:T(8,128)S(1)}, u32[]{:S(2)}, u32[]{:S(2)}) collective-permute-start(f32[136,128]{1,0:T(8,128)S(1)} %get-tuple-element.62), channel_id=1, source_target_pairs={{0,504},{8,0},{16,8},{24,16},{32,24},{40,32},{48,40},{56,48},{64,5... | collective-permute-start | bytes 208904 | tf_op jit(solution)/shard_map/ppermute | solution.py:688
  19.5 4.7 %collective-permute-start.3 = (f32[136,64]{1,0:T(8,128)S(1)}, f32[136,64]{1,0:T(8,128)S(1)}, u32[]{:S(2)}, u32[]{:S(2)}) collective-permute-start(f32[136,64]{1,0:T(8,128)S(1)} %pad_maximum_fusion.1), channel_id=1, source_target_pairs={{0,7},{1,0},{2,1},{3,2},{4,3},{5,4},{6,5},{7,6},{8,15},{9,8},{10,9... | collective-permute-start | bytes 104456 | tf_op jit(solution)/shard_map/ppermute | solution.py:688
  21.2 3.1 %collective-permute-start.2 = (f32[136,64]{1,0:T(8,128)S(1)}, f32[136,64]{1,0:T(8,128)S(1)}, u32[]{:S(2)}, u32[]{:S(2)}) collective-permute-start(f32[136,64]{1,0:T(8,128)S(1)} %pad_maximum_fusion), channel_id=1, source_target_pairs={{0,1},{1,2},{2,3},{3,4},{4,5},{5,6},{6,7},{7,0},{8,9},{9,10},{10,1... | collective-permute-start | bytes 104456 | tf_op jit(solution)/shard_map/ppermute | solution.py:688
  29.3 11.8 %all-to-all-start = ((f32[8,24,128]{2,1,0:T(8,128)}), f32[8,24,128]{2,1,0:T(8,128)S(1)}, u32[]{:S(2)}, u32[]{:S(2)}) async-start(f32[8,24,128]{2,1,0:T(8,128)} %get-tuple-element.36), calls=%async_computation | async-start | bytes 196608 | tf_op jit(solution)/shard_map/all_to_all | solution.py:784
  36.1 5.0 %copy-start.3 = (bf16[128,576]{1,0:T(8,128)(2,1)S(1)}, bf16[128,576]{1,0:T(8,128)(2,1)}, u32[]{:S(2)}) copy-start(bf16[128,576]{1,0:T(8,128)(2,1)} %constant.34.clone.table) | copy-start | bytes 442372
  41.9 26.0 %all-to-all-start.1 = ((f32[64,2,128]{2,1,0:T(2,128)}), f32[64,2,128]{2,1,0:T(2,128)S(1)}, u32[]{:S(2)}, u32[]{:S(2)}) async-start(f32[64,2,128]{2,1,0:T(2,128)} %shard_map.188), calls=%async_computation.1 | async-start | bytes 131072 | tf_op jit(solution)/shard_map/all_to_all | solution.py:789
  54.0 13.9 %copy-start = (bf16[448,384]{1,0:T(8,128)(2,1)S(1)}, bf16[448,384]{1,0:T(8,128)(2,1)}, u32[]{:S(2)}) copy-start(bf16[448,384]{1,0:T(8,128)(2,1)} %constant.37.clone.x_out) | copy-start | bytes 1032196
  54.0 13.9 %copy-start.1 = (bf16[640,192]{1,0:T(8,128)(2,1)S(1)}, bf16[640,192]{1,0:T(8,128)(2,1)}, u32[]{:S(2)}) copy-start(bf16[640,192]{1,0:T(8,128)(2,1)} %constant.36.clone.x_in) | copy-start | bytes 737284
  54.1 13.9 %copy-start.6 = (f32[128,128]{1,0:T(8,128)S(1)}, f32[128,128]{1,0:T(8,128)}, u32[]{:S(2)}) copy-start(f32[128,128]{1,0:T(8,128)} %constant.38.clone.x_gain) | copy-start | bytes 196612
  54.1 13.8 %copy-start.7 = (f32[128,128]{1,0:T(8,128)S(1)}, f32[128,128]{1,0:T(8,128)}, u32[]{:S(2)}) copy-start(f32[128,128]{1,0:T(8,128)} %constant.39.clone.x_square) | copy-start | bytes 196612
  58.1 34.9 %copy-start.4 = (bf16[192,384]{1,0:T(8,128)(2,1)S(1)}, bf16[192,384]{1,0:T(8,128)(2,1)}, u32[]{:S(2)}) copy-start(bf16[192,384]{1,0:T(8,128)(2,1)} %constant.35.clone.table) | copy-start | bytes 442372
  69.4 19.6 %all-to-all-start.2 = ((f32[64,2,128]{2,1,0:T(2,128)}), f32[64,2,128]{2,1,0:T(2,128)S(1)}, u32[]{:S(2)}, u32[]{:S(2)}) async-start(f32[64,2,128]{2,1,0:T(2,128)} %shard_map.190), calls=%async_computation.2 | async-start | bytes 131072 | tf_op jit(solution)/shard_map/all_to_all | solution.py:805
  74.0 15.1 %collective-permute-start.5 = (f32[96,128]{1,0:T(8,128)S(1)}, f32[96,128]{1,0:T(8,128)S(1)}, u32[]{:S(2)}, u32[]{:S(2)}) collective-permute-start(f32[96,128]{1,0:T(8,128)S(1)} %get-tuple-element.47.lower), channel_id=1, source_target_pairs={{0,504},{8,0},{16,8},{24,16},{32,24},{40,32},{48,40},{56,48},{64,5... | collective-permute-start | bytes 147464 | tf_op jit(solution)/shard_map/ppermute | solution.py:688
  80.5 8.5 %collective-permute-start.4 = (f32[96,128]{1,0:T(8,128)S(1)}, f32[96,128]{1,0:T(8,128)S(1)}, u32[]{:S(2)}, u32[]{:S(2)}) collective-permute-start(f32[96,128]{1,0:T(8,128)S(1)} %get-tuple-element.50.upper), channel_id=1, source_target_pairs={{0,8},{8,16},{16,24},{24,32},{32,40},{40,48},{48,56},{56,64},{64,7... | collective-permute-start | bytes 147464 | tf_op jit(solution)/shard_map/ppermute | solution.py:688
  89.2 10.2 %collective-permute-start.7 = (f32[96,64]{1,0:T(8,128)S(1)}, f32[96,64]{1,0:T(8,128)S(1)}, u32[]{:S(2)}, u32[]{:S(2)}) collective-permute-start(f32[96,64]{1,0:T(8,128)S(1)} %pad_maximum_fusion.3), channel_id=1, source_target_pairs={{0,7},{1,0},{2,1},{3,2},{4,3},{5,4},{6,5},{7,6},{8,15},{9,8},{10,9... | collective-permute-start | bytes 73736 | tf_op jit(solution)/shard_map/ppermute | solution.py:688
  93.8 8.3 %all-to-all-start.3 = ((f32[8,24,128]{2,1,0:T(8,128)}), f32[8,24,128]{2,1,0:T(8,128)S(1)}, u32[]{:S(2)}, u32[]{:S(2)}) async-start(f32[8,24,128]{2,1,0:T(8,128)} %shard_map.191), calls=%async_computation.3 | async-start | bytes 196608 | tf_op jit(solution)/shard_map/all_to_all | solution.py:810
  97.2 2.8 %collective-permute-start.6 = (f32[96,64]{1,0:T(8,128)S(1)}, f32[96,64]{1,0:T(8,128)S(1)}, u32[]{:S(2)}, u32[]{:S(2)}) collective-permute-start(f32[96,64]{1,0:T(8,128)S(1)} %pad_maximum_fusion.2), channel_id=1, source_target_pairs={{0,1},{1,2},{2,3},{3,4},{4,5},{5,6},{6,7},{7,0},{8,9},{9,10},{10,1... | collective-permute-start | bytes 73736 | tf_op jit(solution)/shard_map/ppermute | solution.py:688

commit v5 on v4

--- a/solution.py
+++ b/solution.py
@@ -481,7 +481,7 @@
     pltpu.VMEM((HALF, 3 * C, ATOM), f32),
     pltpu.VMEM((HALF, 24, ATOM), f32),
     pltpu.VMEM((HALF, C, ATOM), f32),
-    pltpu.SemaphoreType.DMA((3,)),
+    pltpu.SemaphoreType.DMA((1,)),
 ]
 
 
@@ -494,12 +494,8 @@
     base = 8 * k0
     for done, plane in zip(before_planes, planes):
         plane[0:base, :] = done[...]
-    fetch = [
-        pltpu.make_async_copy(kept.at[k0 + k : k0 + k + 2], up.at[k : k + 2], sems.at[k // 2])
-        for k in range(0, HALF, 2)
-    ]
-    for copy in fetch:
-        copy.start()
+    fetch = pltpu.make_async_copy(kept.at[k0 : k0 + HALF], up, sems.at[0])
+    fetch.start()
     first = slot(k0)
     inv, ux, uy, uz = geometry(
         *(rel[c, first : first + 8, :] for c in range(3)), harm, basis, basis_slope
@@ -513,8 +509,7 @@
         radial[k] = layered(out_wide, hidden[RH * k : RH * k + RH])
         radial_slope[k] = layered(out_wide, hidden_slope[RH * k : RH * k + RH])
 
-    for copy in fetch:
-        copy.wait()
+    fetch.wait()
     for half in range(2):
         spots = slice(128 * half, 128 * half + 128)
 

time: 105 us -> 105 us (level)
  transfers between devices with their start and end apart: 12 -> 12, of which waited for: 7 -> 7; matrix products, arithmetic and copies ran while one was open for 1% -> 1% of each run, Pallas kernels for 10% -> 9%
where the time goes in v5:
time: 105 us; the launch traced here: 104 us
  starting transfers between devices  59.3 us (56%)
  waiting for transfers between devices  22.3 us (21%)
  Pallas kernels  18.6 us (18%)
  other arithmetic  1.51 us (1%)
  local copies, waits for them, and re-layouts  1.27 us (1%)
    ppermute x8, starting transfers between devices, passed_along(): lax.ppermute(array, axis, [(i, (i + by) % devices) for i in range(devices)])  32.6 us
    pallas_call x9, Pallas kernels, call(): pl.pallas_call(kernel, out_shape=outs, in_specs=[far if i in far_in else...  18.6 us
    all_to_all x1, starting transfers between devices, shards(): lax.all_to_all(waves, 'gx', split_axis=0, concat_axis=0, tiled=True)  12.1 us
    all_to_all x1, waiting for transfers between devices, shards(): lax.all_to_all(waves, 'gx', split_axis=0, concat_axis=0, tiled=True)  10.7 us
    ppermute x8, waiting for transfers between devices, passed_along(): lax.ppermute(array, axis, [(i, (i + by) % devices) for i in range(devices)])  8.4 us
    all_to_all x1, starting transfers between devices, shards(): rows = lax.all_to_all(spread, 'gy', split_axis=0, concat_axis=0, tiled=True)  6.78 us
    all_to_all x1, starting transfers between devices, shards(): waves = lax.all_to_all(waves, 'gx', split_axis=0, concat_axis=0, tiled=True)  4.56 us
    all_to_all x1, starting transfers between devices, shards(): lax.all_to_all(rows, 'gy', split_axis=0, concat_axis=0, tiled=True)  3.31 us
  transfers between devices with their start and end apart: 12, of which 7 were waited for; matrix products, arithmetic and copies ran while one was open for 1% of the time, Pallas kernels for 9%

profile of v5, /device:TPU:1, one launch (start us, length us, event | category | flops | bytes accessed | tf_op | source)
XLA Modules:
  0.0 103.9 jit_solution(13657771660294501338)
XLA Ops:
  0.6 0.0 copy-start.2
  0.6 0.0 copy-start.12
  0.7 0.0 copy-start.13
  0.7 0.0 copy-start.10
  0.7 0.0 copy-start.5
  0.7 0.0 copy-start.9
  0.7 0.0 copy-start.11
  0.7 0.0 copy-start.8
  0.7 0.1 pad.18.clone
  0.8 1.0 %maximum_maximum_fusion.own = f32[136,256]{1,0:T(8,128)S(1)} fusion(f32[3,256]{1,0:T(4,128)} %param.18, f32[128,256]{1,0:T(8,128)} %param.19, f32[136]{0:T(256)S(1)} %pad.18.clone), kind=kLoop, calls=%fused_computation | loop fusion | flops 69632 | bytes 273952 | tf_op jit(solution)/shard_map/concatenate | solution.py:705
  1.9 3.9 %collective-permute-start = (f32[136,128]{1,0:T(8,128)S(1)}, f32[136,128]{1,0:T(8,128)S(1)}, u32[]{:S(2)}, u32[]{:S(2)}) collective-permute-start(f32[136,128]{1,0:T(8,128)S(1)} %get-tuple-element.63), channel_id=1, source_target_pairs={{0,8},{8,16},{16,24},{24,32},{32,40},{40,48},{48,56},{56,64},{64,7... | collective-permute-start | bytes 208904 | tf_op jit(solution)/shard_map/ppermute | solution.py:683
  5.8 12.1 %collective-permute-start.1 = (f32[136,128]{1,0:T(8,128)S(1)}, f32[136,128]{1,0:T(8,128)S(1)}, u32[]{:S(2)}, u32[]{:S(2)}) collective-permute-start(f32[136,128]{1,0:T(8,128)S(1)} %get-tuple-element.62), channel_id=1, source_target_pairs={{0,504},{8,0},{16,8},{24,16},{32,24},{40,32},{48,40},{56,48},{64,5... | collective-permute-start | bytes 208904 | tf_op jit(solution)/shard_map/ppermute | solution.py:683
  18.0 0.1 fusion
  18.1 0.0 collective-permute-done.left
  18.1 0.1 fusion.2
  18.2 1.1 %collective-permute-done.1.right = f32[136,128]{1,0:T(8,128)S(1)} collective-permute-done((f32[136,128]{1,0:T(8,128)S(1)}, f32[136,128]{1,0:T(8,128)S(1)}, u32[]{:S(2)}, u32[]{:S(2)}) %collective-permute-start.1) | collective-permute-done | bytes 69664 | tf_op jit(solution)/shard_map/ppermute | solution.py:683
  19.3 0.1 fusion.3
  19.4 0.1 pad_maximum_fusion.1
  19.5 1.5 %collective-permute-start.3 = (f32[136,64]{1,0:T(8,128)S(1)}, f32[136,64]{1,0:T(8,128)S(1)}, u32[]{:S(2)}, u32[]{:S(2)}) collective-permute-start(f32[136,64]{1,0:T(8,128)S(1)} %pad_maximum_fusion.1), channel_id=1, source_target_pairs={{0,7},{1,0},{2,1},{3,2},{4,3},{5,4},{6,5},{7,6},{8,15},{9,8},{10,9... | collective-permute-start | bytes 104456 | tf_op jit(solution)/shard_map/ppermute | solution.py:683
  21.1 0.1 pad_maximum_fusion
  21.2 1.2 %collective-permute-start.2 = (f32[136,64]{1,0:T(8,128)S(1)}, f32[136,64]{1,0:T(8,128)S(1)}, u32[]{:S(2)}, u32[]{:S(2)}) collective-permute-start(f32[136,64]{1,0:T(8,128)S(1)} %pad_maximum_fusion), channel_id=1, source_target_pairs={{0,1},{1,2},{2,3},{3,4},{4,5},{5,6},{6,7},{7,0},{8,9},{9,10},{10,1... | collective-permute-start | bytes 104456 | tf_op jit(solution)/shard_map/ppermute | solution.py:683
  22.4 0.7 constant_dynamic-slice_fusion.yz
  23.1 0.0 copy-done.10
  23.1 0.0 copy-done.5
  23.1 0.0 copy-done.9
  23.1 0.0 copy-done.11
  23.1 0.0 copy-done.8
  23.2 0.9 shard_map.185
  24.0 0.2 collective-permute-done.3.high
  24.2 0.0 collective-permute-done.2.low
  24.3 5.1 %shard_map.186 = (f32[8,24,128]{2,1,0:T(8,128)}, f32[1,256]{1,0:T(1,128)S(1)}, f32[3,16,256]{2,1,0:T(8,128)S(1)}, f32[8,640]{1,0:T(8,128)S(1)}, f32[8,128,256]{2,1,0:T(8,128)S(1)}, /*index=5*/f32[12,128,256]{2,1,0:T(8,128)}) custom-call(f32[136,128]{1,0:T(8,128)S(1)} %collective-permute-done.left, f32[136,256]{1,0:T(8,128)S(1)} %maximum_maximum_fusion.own, ...), custom_call_target="tpu_custom_call" | custom-call | flops 1000000000 | bytes 2000000 | tf_op jit(solution)/shard_map/pallas_call | solution.py:670
  29.3 6.8 %all-to-all-start = ((f32[8,24,128]{2,1,0:T(8,128)}), f32[8,24,128]{2,1,0:T(8,128)S(1)}, u32[]{:S(2)}, u32[]{:S(2)}) async-start(f32[8,24,128]{2,1,0:T(8,128)} %get-tuple-element.36), calls=%async_computation | async-start | bytes 196608 | tf_op jit(solution)/shard_map/all_to_all | solution.py:779
  36.1 3.9 %shard_map.187 = (f32[48,128]{1,0:T(8,128)S(1)}, f32[48,128]{1,0:T(8,128)S(1)}) custom-call(f32[3,16,256]{2,1,0:T(8,128)S(1)} %get-tuple-element.37.rel, f32[12,128,256]{2,1,0:T(8,128)} %get-tuple-element.44.kept, f32[8,128,256]{2,1,0:T(8,128)S(1)} %get-tuple-element.39.along, s32[12,256]{1,0:T(8,128)S(1)} %copy-done.14, ...), custom_call_target="tpu_custom_call" | custom-call | flops 2000000000 | bytes 2000000 | tf_op jit(solution)/shard_map/pallas_call | solution.py:670
  40.0 1.1 %all-to-all-done.rows = f32[8,24,128]{2,1,0:T(8,128)S(1)} async-done(((f32[8,24,128]{2,1,0:T(8,128)}), f32[8,24,128]{2,1,0:T(8,128)S(1)}, u32[]{:S(2)}, u32[]{:S(2)}) %all-to-all-start) | async-done | bytes 98336 | tf_op jit(solution)/shard_map/all_to_all | solution.py:779
  41.1 0.8 shard_map.188
  41.9 12.1 %all-to-all-start.1 = ((f32[64,2,128]{2,1,0:T(2,128)}), f32[64,2,128]{2,1,0:T(2,128)S(1)}, u32[]{:S(2)}, u32[]{:S(2)}) async-start(f32[64,2,128]{2,1,0:T(2,128)} %shard_map.188), calls=%async_computation.1 | async-start | bytes 131072 | tf_op jit(solution)/shard_map/all_to_all | solution.py:784
  54.0 0.0 copy-start
  54.0 0.0 copy-start.1
  54.1 0.0 copy-start.6
  54.1 0.0 copy-start.7
  54.1 3.1 %shard_map.189 = (f32[96,128]{1,0:T(8,128)S(1)}, f32[96,128]{1,0:T(8,128)S(1)}) custom-call(f32[3,16,256]{2,1,0:T(8,128)S(1)} %get-tuple-element.37.rel, f32[12,128,256]{2,1,0:T(8,128)} %get-tuple-element.44.kept, f32[8,128,256]{2,1,0:T(8,128)S(1)} %get-tuple-element.39.along, s32[12,256]{1,0:T(8,128)S(1)} %copy-done.14, ...), custom_call_target="tpu_custom_call" | custom-call | flops 2000000000 | bytes 2000000 | tf_op jit(solution)/shard_map/pallas_call | solution.py:670
  57.2 0.0 copy-start.4
  57.2 10.7 %all-to-all-done.1.planes = f32[64,2,128]{2,1,0:T(2,128)S(1)} async-done(((f32[64,2,128]{2,1,0:T(2,128)}), f32[64,2,128]{2,1,0:T(2,128)S(1)}, u32[]{:S(2)}, u32[]{:S(2)}) %all-to-all-start.1) | async-done | bytes 65568 | tf_op jit(solution)/shard_map/all_to_all | solution.py:784
  67.9 0.0 copy-done.1
  67.9 1.5 %shard_map.190 = f32[64,2,128]{2,1,0:T(2,128)} custom-call(f32[64,2,128]{2,1,0:T(2,128)S(1)} %all-to-all-done.1.planes, bf16[640,192]{1,0:T(8,128)(2,1)S(1)} %copy-done.1, bf16[448,384]{1,0:T(8,128)(2,1)S(1)} %copy-done, f32[128,128]{1,0:T(8,128)S(1)} %copy-done.6, f32[128,128]{1,0:T(8,128)S(1)} %copy-done.7, f32[1,4,128]{2,1,0:T(4,128)S(1)} %constant_dynamic-slice_fusion.yz), custom_call_target="tpu_custom_call" | custom-call | flops 10000000 | bytes 2000000 | tf_op jit(solution)/shard_map/pallas_call | solution.py:670
  69.4 4.6 %all-to-all-start.2 = ((f32[64,2,128]{2,1,0:T(2,128)}), f32[64,2,128]{2,1,0:T(2,128)S(1)}, u32[]{:S(2)}, u32[]{:S(2)}) async-start(f32[64,2,128]{2,1,0:T(2,128)} %shard_map.190), calls=%async_computation.2 | async-start | bytes 131072 | tf_op jit(solution)/shard_map/all_to_all | solution.py:800
  74.0 6.6 %collective-permute-start.5 = (f32[96,128]{1,0:T(8,128)S(1)}, f32[96,128]{1,0:T(8,128)S(1)}, u32[]{:S(2)}, u32[]{:S(2)}) collective-permute-start(f32[96,128]{1,0:T(8,128)S(1)} %get-tuple-element.47.lower), channel_id=1, source_target_pairs={{0,504},{8,0},{16,8},{24,16},{32,24},{40,32},{48,40},{56,48},{64,5... | collective-permute-start | bytes 147464 | tf_op jit(solution)/shard_map/ppermute | solution.py:683
  80.5 1.9 %collective-permute-start.4 = (f32[96,128]{1,0:T(8,128)S(1)}, f32[96,128]{1,0:T(8,128)S(1)}, u32[]{:S(2)}, u32[]{:S(2)}) collective-permute-start(f32[96,128]{1,0:T(8,128)S(1)} %get-tuple-element.50.upper), channel_id=1, source_target_pairs={{0,8},{8,16},{16,24},{24,32},{32,40},{40,48},{48,56},{56,64},{64,7... | collective-permute-start | bytes 147464 | tf_op jit(solution)/shard_map/ppermute | solution.py:683
  82.5 0.1 fusion.5
  82.6 6.5 %collective-permute-done.4.left = f32[96,128]{1,0:T(8,128)S(1)} collective-permute-done((f32[96,128]{1,0:T(8,128)S(1)}, f32[96,128]{1,0:T(8,128)S(1)}, u32[]{:S(2)}, u32[]{:S(2)}) %collective-permute-start.4) | collective-permute-done | bytes 49184 | tf_op jit(solution)/shard_map/ppermute | solution.py:683
  89.0 0.0 collective-permute-done.5.right
  89.0 0.0 all-to-all-done.2.waves
  89.0 0.1 fusion.4
  89.1 0.1 pad_maximum_fusion.3
  89.2 3.7 %collective-permute-start.7 = (f32[96,64]{1,0:T(8,128)S(1)}, f32[96,64]{1,0:T(8,128)S(1)}, u32[]{:S(2)}, u32[]{:S(2)}) collective-permute-start(f32[96,64]{1,0:T(8,128)S(1)} %pad_maximum_fusion.3), channel_id=1, source_target_pairs={{0,7},{1,0},{2,1},{3,2},{4,3},{5,4},{6,5},{7,6},{8,15},{9,8},{10,9... | collective-permute-start | bytes 73736 | tf_op jit(solution)/shard_map/ppermute | solution.py:683
  92.9 0.8 shard_map.191
  93.8 3.3 %all-to-all-start.3 = ((f32[8,24,128]{2,1,0:T(8,128)}), f32[8,24,128]{2,1,0:T(8,128)S(1)}, u32[]{:S(2)}, u32[]{:S(2)}) async-start(f32[8,24,128]{2,1,0:T(8,128)} %shard_map.191), calls=%async_computation.3 | async-start | bytes 196608 | tf_op jit(solution)/shard_map/all_to_all | solution.py:805
  97.1 0.1 pad_maximum_fusion.2
  97.2 1.6 %collective-permute-start.6 = (f32[96,64]{1,0:T(8,128)S(1)}, f32[96,64]{1,0:T(8,128)S(1)}, u32[]{:S(2)}, u32[]{:S(2)}) collective-permute-start(f32[96,64]{1,0:T(8,128)S(1)} %pad_maximum_fusion.2), channel_id=1, source_target_pairs={{0,1},{1,2},{2,3},{3,4},{4,5},{5,6},{6,7},{7,0},{8,9},{9,10},{10,1... | collective-permute-start | bytes 73736 | tf_op jit(solution)/shard_map/ppermute | solution.py:683
  98.8 0.6 shard_map.192.waves
  99.5 0.0 collective-permute-done.7.high
  99.5 0.5 collective-permute-done.6.low
  100.0 2.1 %all-to-all-done.3.potential = f32[8,24,128]{2,1,0:T(8,128)S(1)} async-done(((f32[8,24,128]{2,1,0:T(8,128)}), f32[8,24,128]{2,1,0:T(8,128)S(1)}, u32[]{:S(2)}, u32[]{:S(2)}) %all-to-all-start.3) | async-done | bytes 98336 | tf_op jit(solution)/shard_map/all_to_all | solution.py:805
  102.1 1.9 %shard_map.193 = (f32[3,256]{1,0:T(4,128)}, f32[1,1]{1,0:T(1,128)}) custom-call(f32[8,24,128]{2,1,0:T(8,128)S(1)} %all-to-all-done.3.potential, f32[8,640]{1,0:T(8,128)S(1)} %get-tuple-element.52.places, f32[1,256]{1,0:T(1,128)S(1)} %get-tuple-element.53.charge, bf16[384,896]{1,0:T(8,128)(2,1)S(1)} %shard_map.192.waves, ...), custom_call_target="tpu_custom_call" | custom-call | flops 1000000000 | bytes 2000000 | tf_op jit(solution)/shard_map/pallas_call | solution.py:670
  (13 shorter events, 0.0 us)
Async XLA Ops:
  0.6 22.5 %copy-start.2 = (f32[128,128]{1,0:T(8,128)S(1)}, f32[128,128]{1,0:T(8,128)}, u32[]{:S(2)}) copy-start(f32[128,128]{1,0:T(8,128)} %constant.33.clone.z_table) | copy-start | bytes 196612
  0.6 22.5 %copy-start.12 = (f32[128]{0:T(128)S(1)}, f32[128]{0:T(128)}, u32[]{:S(2)}) copy-start(f32[128]{0:T(128)} %param.26) | copy-start | bytes 1540
  0.7 22.4 %copy-start.13 = (f32[128]{0:T(128)S(1)}, f32[128]{0:T(128)}, u32[]{:S(2)}) copy-start(f32[128]{0:T(128)} %param.27) | copy-start | bytes 1540
  0.7 22.4 %copy-start.10 = (f32[64,8]{0,1:T(8,128)S(1)}, f32[64,8]{0,1:T(8,128)}, u32[]{:S(2)}) copy-start(f32[64,8]{0,1:T(8,128)} %param.22) | copy-start | bytes 6148
  0.7 22.4 %copy-start.5 = (f32[384,64]{0,1:T(8,128)S(1)}, f32[384,64]{0,1:T(8,128)}, u32[]{:S(2)}) copy-start(f32[384,64]{0,1:T(8,128)} %param.23) | copy-start | bytes 294916
  0.7 22.4 %copy-start.9 = (f32[128,128]{1,0:T(8,128)S(1)}, f32[128,128]{1,0:T(8,128)}, u32[]{:S(2)}) copy-start(f32[128,128]{1,0:T(8,128)} %up_weight.1) | copy-start | bytes 196612
  0.7 22.4 %copy-start.11 = (f32[2,128]{1,0:T(2,128)S(1)}, f32[2,128]{1,0:T(2,128)}, u32[]{:S(2)}) copy-start(f32[2,128]{1,0:T(2,128)} %coupling.1) | copy-start | bytes 3076
  0.7 22.4 %copy-start.8 = (f32[128,128]{1,0:T(8,128)S(1)}, f32[128,128]{1,0:T(8,128)}, u32[]{:S(2)}) copy-start(f32[128,128]{1,0:T(8,128)} %mix_weight.1) | copy-start | bytes 196612
  0.7 23.5 %copy-start.14 = (s32[12,256]{1,0:T(8,128)S(1)}, s32[12,256]{1,0:T(8,128)}, u32[]{:S(2)}) copy-start(s32[12,256]{1,0:T(8,128)} %codes.5) | copy-start | bytes 36868
  1.9 16.2 %collective-permute-start = (f32[136,128]{1,0:T(8,128)S(1)}, f32[136,128]{1,0:T(8,128)S(1)}, u32[]{:S(2)}, u32[]{:S(2)}) collective-permute-start(f32[136,128]{1,0:T(8,128)S(1)} %get-tuple-element.63), channel_id=1, source_target_pairs={{0,8},{8,16},{16,24},{24,32},{32,40},{40,48},{48,56},{56,64},{64,7... | collective-permute-start | bytes 208904 | tf_op jit(solution)/shard_map/ppermute | solution.py:683
  5.8 13.5 %collective-permute-start.1 = (f32[136,128]{1,0:T(8,128)S(1)}, f32[136,128]{1,0:T(8,128)S(1)}, u32[]{:S(2)}, u32[]{:S(2)}) collective-permute-start(f32[136,128]{1,0:T(8,128)S(1)} %get-tuple-element.62), channel_id=1, source_target_pairs={{0,504},{8,0},{16,8},{24,16},{32,24},{40,32},{48,40},{56,48},{64,5... | collective-permute-start | bytes 208904 | tf_op jit(solution)/shard_map/ppermute | solution.py:683
  19.5 4.7 %collective-permute-start.3 = (f32[136,64]{1,0:T(8,128)S(1)}, f32[136,64]{1,0:T(8,128)S(1)}, u32[]{:S(2)}, u32[]{:S(2)}) collective-permute-start(f32[136,64]{1,0:T(8,128)S(1)} %pad_maximum_fusion.1), channel_id=1, source_target_pairs={{0,7},{1,0},{2,1},{3,2},{4,3},{5,4},{6,5},{7,6},{8,15},{9,8},{10,9... | collective-permute-start | bytes 104456 | tf_op jit(solution)/shard_map/ppermute | solution.py:683
  21.2 3.1 %collective-permute-start.2 = (f32[136,64]{1,0:T(8,128)S(1)}, f32[136,64]{1,0:T(8,128)S(1)}, u32[]{:S(2)}, u32[]{:S(2)}) collective-permute-start(f32[136,64]{1,0:T(8,128)S(1)} %pad_maximum_fusion), channel_id=1, source_target_pairs={{0,1},{1,2},{2,3},{3,4},{4,5},{5,6},{6,7},{7,0},{8,9},{9,10},{10,1... | collective-permute-start | bytes 104456 | tf_op jit(solution)/shard_map/ppermute | solution.py:683
  29.3 11.8 %all-to-all-start = ((f32[8,24,128]{2,1,0:T(8,128)}), f32[8,24,128]{2,1,0:T(8,128)S(1)}, u32[]{:S(2)}, u32[]{:S(2)}) async-start(f32[8,24,128]{2,1,0:T(8,128)} %get-tuple-element.36), calls=%async_computation | async-start | bytes 196608 | tf_op jit(solution)/shard_map/all_to_all | solution.py:779
  36.1 5.0 %copy-start.3 = (bf16[128,576]{1,0:T(8,128)(2,1)S(1)}, bf16[128,576]{1,0:T(8,128)(2,1)}, u32[]{:S(2)}) copy-start(bf16[128,576]{1,0:T(8,128)(2,1)} %constant.34.clone.table) | copy-start | bytes 442372
  41.9 26.0 %all-to-all-start.1 = ((f32[64,2,128]{2,1,0:T(2,128)}), f32[64,2,128]{2,1,0:T(2,128)S(1)}, u32[]{:S(2)}, u32[]{:S(2)}) async-start(f32[64,2,128]{2,1,0:T(2,128)} %shard_map.188), calls=%async_computation.1 | async-start | bytes 131072 | tf_op jit(solution)/shard_map/all_to_all | solution.py:784
  54.0 13.9 %copy-start = (bf16[448,384]{1,0:T(8,128)(2,1)S(1)}, bf16[448,384]{1,0:T(8,128)(2,1)}, u32[]{:S(2)}) copy-start(bf16[448,384]{1,0:T(8,128)(2,1)} %constant.37.clone.x_out) | copy-start | bytes 1032196
  54.0 13.9 %copy-start.1 = (bf16[640,192]{1,0:T(8,128)(2,1)S(1)}, bf16[640,192]{1,0:T(8,128)(2,1)}, u32[]{:S(2)}) copy-start(bf16[640,192]{1,0:T(8,128)(2,1)} %constant.36.clone.x_in) | copy-start | bytes 737284
  54.1 13.9 %copy-start.6 = (f32[128,128]{1,0:T(8,128)S(1)}, f32[128,128]{1,0:T(8,128)}, u32[]{:S(2)}) copy-start(f32[128,128]{1,0:T(8,128)} %constant.38.clone.x_gain) | copy-start | bytes 196612
  54.1 13.8 %copy-start.7 = (f32[128,128]{1,0:T(8,128)S(1)}, f32[128,128]{1,0:T(8,128)}, u32[]{:S(2)}) copy-start(f32[128,128]{1,0:T(8,128)} %constant.39.clone.x_square) | copy-start | bytes 196612
  57.2 35.7 %copy-start.4 = (bf16[192,384]{1,0:T(8,128)(2,1)S(1)}, bf16[192,384]{1,0:T(8,128)(2,1)}, u32[]{:S(2)}) copy-start(bf16[192,384]{1,0:T(8,128)(2,1)} %constant.35.clone.table) | copy-start | bytes 442372
  69.4 19.6 %all-to-all-start.2 = ((f32[64,2,128]{2,1,0:T(2,128)}), f32[64,2,128]{2,1,0:T(2,128)S(1)}, u32[]{:S(2)}, u32[]{:S(2)}) async-start(f32[64,2,128]{2,1,0:T(2,128)} %shard_map.190), calls=%async_computation.2 | async-start | bytes 131072 | tf_op jit(solution)/shard_map/all_to_all | solution.py:800
  74.0 15.1 %collective-permute-start.5 = (f32[96,128]{1,0:T(8,128)S(1)}, f32[96,128]{1,0:T(8,128)S(1)}, u32[]{:S(2)}, u32[]{:S(2)}) collective-permute-start(f32[96,128]{1,0:T(8,128)S(1)} %get-tuple-element.47.lower), channel_id=1, source_target_pairs={{0,504},{8,0},{16,8},{24,16},{32,24},{40,32},{48,40},{56,48},{64,5... | collective-permute-start | bytes 147464 | tf_op jit(solution)/shard_map/ppermute | solution.py:683
  80.5 8.5 %collective-permute-start.4 = (f32[96,128]{1,0:T(8,128)S(1)}, f32[96,128]{1,0:T(8,128)S(1)}, u32[]{:S(2)}, u32[]{:S(2)}) collective-permute-start(f32[96,128]{1,0:T(8,128)S(1)} %get-tuple-element.50.upper), channel_id=1, source_target_pairs={{0,8},{8,16},{16,24},{24,32},{32,40},{40,48},{48,56},{56,64},{64,7... | collective-permute-start | bytes 147464 | tf_op jit(solution)/shard_map/ppermute | solution.py:683
  89.2 10.2 %collective-permute-start.7 = (f32[96,64]{1,0:T(8,128)S(1)}, f32[96,64]{1,0:T(8,128)S(1)}, u32[]{:S(2)}, u32[]{:S(2)}) collective-permute-start(f32[96,64]{1,0:T(8,128)S(1)} %pad_maximum_fusion.3), channel_id=1, source_target_pairs={{0,7},{1,0},{2,1},{3,2},{4,3},{5,4},{6,5},{7,6},{8,15},{9,8},{10,9... | collective-permute-start | bytes 73736 | tf_op jit(solution)/shard_map/ppermute | solution.py:683
  93.8 8.3 %all-to-all-start.3 = ((f32[8,24,128]{2,1,0:T(8,128)}), f32[8,24,128]{2,1,0:T(8,128)S(1)}, u32[]{:S(2)}, u32[]{:S(2)}) async-start(f32[8,24,128]{2,1,0:T(8,128)} %shard_map.191), calls=%async_computation.3 | async-start | bytes 196608 | tf_op jit(solution)/shard_map/all_to_all | solution.py:805
  97.2 2.8 %collective-permute-start.6 = (f32[96,64]{1,0:T(8,128)S(1)}, f32[96,64]{1,0:T(8,128)S(1)}, u32[]{:S(2)}, u32[]{:S(2)}) collective-permute-start(f32[96,64]{1,0:T(8,128)S(1)} %pad_maximum_fusion.2), channel_id=1, source_target_pairs={{0,1},{1,2},{2,3},{3,4},{4,5},{5,6},{6,7},{7,0},{8,9},{9,10},{10,1... | collective-permute-start | bytes 73736 | tf_op jit(solution)/shard_map/ppermute | solution.py:683
